TPU v7x, 32 devices: a whole 2x2x4 slice. The times are simulated.
32 devices in a mesh: grp: 2 (over y), own: 4 (over z), hlp: 4 (over x, core).
Axes of the slice: x: 2, y: 2, z: 4, core: 2. Of those that a mesh axis runs over, the one named last changes fastest.
Arguments:
- points: bfloat16 [8192, 1024], P(('grp', 'own', 'hlp')), parts along dimension 0, may hold values from -24 to 24
- cluster_of: int32 [8192], P(('grp', 'own', 'hlp')), parts along dimension 0, may hold values from 0 to 3, as said below
- subcentroids: bfloat16 [8, 256, 1024], P(('grp', 'own'), 'hlp'), parts along dimension 0, may hold values from -3 to 3
Outputs:
- refined: float32 [8, 256, 1024], P(('grp', 'own'), 'hlp'), parts along dimension 0
- log_resp: float32 [8192, 256], P(('grp', 'own', 'hlp')), parts along dimension 0
There are 2 independent parts, one for each index of `grp`. A program takes and returns all parts, laid end to end along the dimension named above; each array names one. Nothing has to cross between parts.
Inputs may be any that keep to these rules, and one draw needn't show every extreme that they name: `cluster_of`: the points of one device name each cluster at most 128 times; in every draw one cluster is named exactly 128 times by the points of every device.
All inputs are finite; a program needn't handle non-finite values.
Results may differ from a plain program's by a relative error of at most 0.0097.
Values may be sent and summed in bfloat16 or wider, within the bound.
No kernel may reach another device: no remote copies, remote signals or barrier semaphores. Data moves between devices by JAX's collectives and lax.ppermute only.
A program may use at most 64 MiB of HBM per device.

v0:
```python
import jax
import jax.numpy as jnp
from jax import lax
from jax.sharding import PartitionSpec as P

ITERS = 2


smoothing_factor = 16.0
prior_count = 1.0


def closeness_matrix(vector_samples, group_prototypes):
    return lax.dot_general(
        vector_samples,
        group_prototypes,
        (((1,), (1,)), ((), ())),
        preferred_element_type=jnp.float32,
    )


def weight_logarithms(vector_samples, group_prototypes, elementwise_power):
    membership_energies = (
        2.0 * closeness_matrix(vector_samples, group_prototypes) - elementwise_power[None, :]
    ) / smoothing_factor
    top = jnp.max(membership_energies, axis=1, keepdims=True)
    total = jnp.log(jnp.sum(jnp.exp(membership_energies - top), axis=1, keepdims=True))
    return membership_energies - (top + total)


def square_norms(group_prototypes):
    return jnp.sum(jnp.square(group_prototypes.astype(jnp.float32)), axis=1)


def accumulate(buffer, count, group_prototypes, elementwise_power):
    width = min(512, buffer.shape[0])
    rounds = (count + width - 1) // width

    def accumulate_advance(step, carry):
        sums, mass = carry
        start = step * width
        vector_samples = lax.dynamic_slice_in_dim(buffer, start, width, 0)
        living = start + jnp.arange(width, dtype=jnp.int32) < count
        share = jnp.exp(weight_logarithms(vector_samples, group_prototypes, elementwise_power))
        share = jnp.where(living[:, None], share, 0.0).astype(jnp.bfloat16)
        sums = sums + lax.dot_general(
            share, vector_samples, (((0,), (0,)), ((), ())), preferred_element_type=jnp.float32
        )
        mass = mass + jnp.sum(share.astype(jnp.float32), axis=0)
        return (sums, mass)

    initial_sums = jnp.zeros((group_prototypes.shape[0], buffer.shape[1]), jnp.float32)
    start_mass = jnp.zeros((group_prototypes.shape[0],), jnp.float32)
    return lax.fori_loop(0, rounds, accumulate_advance, (initial_sums, start_mass))


def log_pass(buffer, count, group_prototypes, elementwise_power):
    width = min(512, buffer.shape[0])
    rounds = (count + width - 1) // width

    def log_advance(step, logs):
        start = step * width
        vector_samples = lax.dynamic_slice_in_dim(buffer, start, width, 0)
        return lax.dynamic_update_slice_in_dim(
            logs, weight_logarithms(vector_samples, group_prototypes, elementwise_power), start, 0
        )

    return lax.fori_loop(
        0, rounds, log_advance, jnp.zeros((buffer.shape[0], group_prototypes.shape[0]), jnp.float32)
    )


def per_device(points, cluster_of, subcentroids):
    vector_samples = points.shape[0]
    width = points.shape[1]
    owners = lax.axis_size("own")
    depth = min(vector_samples // 2, 4 * vector_samples // owners)
    slots = owners * depth
    labels = jnp.arange(owners, dtype=jnp.int32)
    member = (cluster_of[:, None] == labels[None, :]).astype(jnp.int32)
    before = jnp.cumsum(member, axis=0) - member
    ranking = jnp.sum(before * member, axis=1)
    target = cluster_of * depth + ranking
    outbox = jnp.zeros((slots, width), jnp.bfloat16).at[target].set(points)
    sent_counts = jnp.sum(member, axis=0).reshape(owners, 1)
    inbox, got_counts = (
        lax.all_to_all(
            outbox.reshape(owners, depth, width), "own", split_axis=0, concat_axis=0, tiled=True
        ),
        lax.all_to_all(sent_counts, "own", split_axis=0, concat_axis=0, tiled=True),
    )
    member_tallies = got_counts[:, 0]
    offsets = jnp.cumsum(member_tallies) - member_tallies
    feature_index = jnp.arange(depth, dtype=jnp.int32)
    live_slot = (feature_index[None, :] < member_tallies[:, None]).reshape(-1)
    placing = jnp.where(live_slot, (offsets[:, None] + feature_index[None, :]).reshape(-1), slots)
    packed = (
        jnp.zeros((slots, width), jnp.bfloat16)
        .at[placing]
        .set(inbox.reshape(slots, width), mode="drop")
    )
    held = jnp.sum(member_tallies)
    helper = lax.axis_index("hlp")
    share_rows = subcentroids.shape[1]
    group_prototypes = lax.all_gather(subcentroids[0], "hlp", axis=0, tiled=True)
    refined = jnp.zeros((share_rows, width), jnp.float32)
    for turn in range(ITERS):
        elementwise_power = square_norms(group_prototypes)
        sums, mass = accumulate(packed, held, group_prototypes, elementwise_power)
        all_sums, all_mass = lax.psum((sums, mass), "hlp")
        whole = (all_sums + prior_count * group_prototypes.astype(jnp.float32)) / (
            all_mass[:, None] + prior_count
        )
        refined = lax.dynamic_slice_in_dim(whole, helper * share_rows, share_rows, 0)
        group_prototypes = whole.astype(jnp.bfloat16)
    logs = log_pass(packed, held, group_prototypes, square_norms(group_prototypes))
    slot_logs = jnp.take(logs, jnp.minimum(placing, slots - 1), axis=0)
    slot_logs = jnp.where(live_slot[:, None], slot_logs, 0.0)
    returned = lax.all_to_all(
        slot_logs.reshape(owners, depth, logs.shape[1]),
        "own",
        split_axis=0,
        concat_axis=0,
        tiled=True,
    )
    log_resp = jnp.take(returned.reshape(slots, logs.shape[1]), target, axis=0)
    return (refined[None], log_resp)


def solution(mesh):
    in_specs = (
        P(("grp", "own", "hlp"), None),
        P(("grp", "own", "hlp")),
        P(("grp", "own"), "hlp", None),
    )
    out_specs = (P(("grp", "own"), "hlp", None), P(("grp", "own", "hlp"), None))
    return jax.shard_map(
        per_device, mesh=mesh, in_specs=in_specs, out_specs=out_specs, check_vma=False
    )
```

profile of v0, /device:TPU:0, one launch (start us, length us, event | category | flops | bytes accessed | tf_op | source)
XLA Modules:
  0.0 170.1 jit_solution(11591906839309448224)
XLA Ops:
  7.2 0.7 copy-done.5
  7.8 1.2 reduce-window.19
  9.1 0.1 slice.12
  9.1 0.1 copy.22
  9.3 0.1 copy.23
  9.4 0.1 add_bitcast_fusion
  9.4 0.1 fusion.15
  9.6 0.7 copy.21
  10.2 6.3 %all-to-all-start = ((s32[4,1,1]{2,1,0:T(1,128)}), s32[4,1,1]{2,1,0:T(1,128)S(1)}, u32[]{:S(2)}, u32[]{:S(2)}) async-start(s32[4,1,1]{2,1,0:T(1,128)} %copy.21), calls=%async_computation | async-start | bytes 4096 | tf_op jit(solution)/shard_map/all_to_all | solution.py:90
  16.6 3.2 %scatter_custom_fusion = bf16[512,1024]{1,0:T(8,128)(2,1)} fusion(s32[256]{0:T(256)S(1)} %get-tuple-element.642, bf16[256,1024]{1,0:T(8,128)(2,1)} %param.9, bf16[]{:T(256)} %constant.194.clone.1), kind=kCustom, calls=%fused_computation.38 | custom fusion | bytes 1049088 | tf_op jit(solution)/shard_map/scatter | solution.py:84
  19.7 2.3 %all-to-all-done = s32[4,1,1]{2,1,0:T(1,128)S(1)} async-done(((s32[4,1,1]{2,1,0:T(1,128)}), s32[4,1,1]{2,1,0:T(1,128)S(1)}, u32[]{:S(2)}, u32[]{:S(2)}) %all-to-all-start) | async-done | bytes 48 | tf_op jit(solution)/shard_map/all_to_all | solution.py:90
  22.0 3.6 %all-to-all-start.1 = ((bf16[4,128,1024]{2,1,0:T(8,128)(2,1)}), bf16[4,128,1024]{2,1,0:T(8,128)(2,1)S(1)}, u32[]{:S(2)}, u32[]{:S(2)}) async-start(bf16[4,128,1024]{2,1,0:T(8,128)(2,1)} %bitcast.7), calls=%async_computation.1 | async-start | bytes 2097152 | tf_op jit(solution)/shard_map/all_to_all | solution.py:87
  25.7 0.0 all-reduce.3.cloned.1.call-start
  25.7 7.2 %all-gather = bf16[1,256,1024]{2,1,0:T(8,128)(2,1)S(1)} all-gather(bf16[1,64,1024]{2,1,0:T(8,128)(2,1)S(1)} %copy-done.4), channel_id=2, replica_groups=mesh['grp'=2,'own'=4,'hlp'=4] {'hlp'}, dimensions={1}, use_global_device_ids=true | all-gather | bytes 655360 | tf_op jit(solution)/shard_map/all_gather | solution.py:105
  32.9 0.2 fusion
  33.1 0.7 fusion.16
  34.5 0.2 reduce-window.18
  34.7 0.1 add_select_fusion
  34.7 15.5 %all-to-all-done.1 = bf16[4,128,1024]{2,1,0:T(8,128)(2,1)S(1)} async-done(((bf16[4,128,1024]{2,1,0:T(8,128)(2,1)}), bf16[4,128,1024]{2,1,0:T(8,128)(2,1)S(1)}, u32[]{:S(2)}, u32[]{:S(2)}) %all-to-all-start.1) | async-done | bytes 1048608 | tf_op jit(solution)/shard_map/all_to_all | solution.py:87
  50.2 2.8 %scatter_custom_fusion.1 = bf16[512,1024]{1,0:T(8,128)(2,1)S(1)} fusion(s32[512]{0:T(512)S(1)} %bitcast.57, bf16[512,1024]{1,0:T(8,128)(2,1)S(1)} %bitcast.51, bf16[]{:T(256)} %constant.194.clone.1), kind=kCustom, calls=%fused_computation.36 | custom fusion | bytes 1048578 | tf_op jit(solution)/shard_map/scatter | solution.py:100
  53.0 0.5 multiply_reduce_fusion.2
  53.5 0.2 copy.24
  53.7 0.1 broadcast.208.clone
  53.9 1.7 while.47
  53.9 0.2 exponential_reduce_fusion.5
  54.1 0.7 add_compare_fusion.4
  54.8 0.2 convert_reduce_fusion.5
  55.0 0.5 convolution_add_fusion.4
  55.5 1.0 copy-done
  56.6 0.0 all-reduce.3.cloned.1.call-update
  56.6 0.0 all-reduce.5.cloned.1.call-start
  56.6 5.8 %psum.29 = f32[256]{0:T(256)S(1)} all-reduce(f32[256]{0:T(256)S(1)} %get-tuple-element.442), channel_id=1, replica_groups=mesh['grp'=2,'own'=4,'hlp'=4] {'hlp'}, use_global_device_ids=true, to_apply=%region_15.16 | all-reduce | flops 256 | bytes 2048 | tf_op jit(solution)/shard_map/psum | solution.py:110
  62.4 29.5 %all-reduce.3.cloned.1.call-done = f32[256,1024]{1,0:T(8,128)} async-done(((f32[256,1024]{1,0:T(8,128)}), f32[256,1024]{1,0:T(8,128)}) %all-reduce.3.cloned.1.call-update) | async-done | bytes 1048592 | tf_op jit(solution)/shard_map/psum | solution.py:110
  91.9 1.5 fusion.3
  93.5 0.5 multiply_reduce_fusion.1
  94.0 0.3 copy-done.2
  94.3 0.2 copy.25
  94.5 0.1 broadcast.208
  94.6 1.7 while.48
  94.6 0.2 exponential_reduce_fusion.6
  94.9 0.7 add_compare_fusion.5
  95.5 0.2 convert_reduce_fusion.6
  95.8 0.5 convolution_add_fusion.5
  96.3 1.0 copy-done.1
  97.3 0.0 all-reduce.5.cloned.1.call-update
  97.3 0.1 iota_compare_fusion.1
  97.4 5.9 %psum.31 = f32[256]{0:T(256)S(1)} all-reduce(f32[256]{0:T(256)S(1)} %get-tuple-element.444), channel_id=1, replica_groups=mesh['grp'=2,'own'=4,'hlp'=4] {'hlp'}, use_global_device_ids=true, to_apply=%region_23.24 | all-reduce | flops 256 | bytes 2048 | tf_op jit(solution)/shard_map/psum | solution.py:110
  103.3 30.7 %all-reduce.5.cloned.1.call-done = f32[256,1024]{1,0:T(8,128)} async-done(((f32[256,1024]{1,0:T(8,128)}), f32[256,1024]{1,0:T(8,128)}) %all-reduce.5.cloned.1.call-update) | async-done | bytes 1048592 | tf_op jit(solution)/shard_map/psum | solution.py:110
  134.0 1.5 multiply_reduce_fusion
  135.5 0.5 fusion.11
  136.0 0.2 exponential_reduce_fusion.2
  136.2 0.6 log_add_fusion.2
  136.8 0.6 log.35
  137.3 0.2 copy.26
  137.5 0.8 broadcast_in_dim.107
  138.4 0.9 while.49
  138.4 0.9 multiply_subtract_fusion.2
  139.3 2.6 %gather_fusion = f32[512,256]{1,0:T(8,128)S(1)} fusion(f32[512,256]{1,0:T(8,128)} %get-tuple-element.445, s32[1024]{0:T(1024)S(1)} %pad_clamp_fusion.1), kind=kCustom, calls=%fused_computation | custom fusion | bytes 1050624 | tf_op jit(solution)/shard_map/jit(_take)/gather | solution.py:117
  141.9 1.0 select_select_fusion
  142.9 4.6 %all-to-all-start.2 = ((f32[4,128,256]{2,1,0:T(8,128)}), f32[4,128,256]{2,1,0:T(8,128)S(1)}, u32[]{:S(2)}, u32[]{:S(2)}) async-start(f32[4,128,256]{2,1,0:T(8,128)} %select_select_fusion), calls=%async_computation.2 | async-start | bytes 1048576 | tf_op jit(solution)/shard_map/all_to_all | solution.py:119
  147.5 0.7 dynamic-slice_bitcast_fusion
  148.2 13.3 %all-to-all-done.2 = f32[4,128,256]{2,1,0:T(8,128)S(1)} async-done(((f32[4,128,256]{2,1,0:T(8,128)}), f32[4,128,256]{2,1,0:T(8,128)S(1)}, u32[]{:S(2)}, u32[]{:S(2)}) %all-to-all-start.2) | async-done | bytes 524320 | tf_op jit(solution)/shard_map/all_to_all | solution.py:119
  161.5 1.0 gather_fusion.1
  162.5 0.8 broadcast_select_fusion
  (24 shorter events, 0.2 us)
Async XLA Ops:
  7.2 0.7 copy-start.5
  10.2 11.8 %all-to-all-start = ((s32[4,1,1]{2,1,0:T(1,128)}), s32[4,1,1]{2,1,0:T(1,128)S(1)}, u32[]{:S(2)}, u32[]{:S(2)}) async-start(s32[4,1,1]{2,1,0:T(1,128)} %copy.21), calls=%async_computation | async-start | bytes 4096 | tf_op jit(solution)/shard_map/all_to_all | solution.py:90
  22.0 3.7 %copy-start.4 = (bf16[1,64,1024]{2,1,0:T(8,128)(2,1)S(1)}, bf16[1,64,1024]{2,1,0:T(8,128)(2,1)}, u32[]{:S(2)}) copy-start(bf16[1,64,1024]{2,1,0:T(8,128)(2,1)} %param.11) | copy-start | bytes 393220
  22.0 28.2 %all-to-all-start.1 = ((bf16[4,128,1024]{2,1,0:T(8,128)(2,1)}), bf16[4,128,1024]{2,1,0:T(8,128)(2,1)S(1)}, u32[]{:S(2)}, u32[]{:S(2)}) async-start(bf16[4,128,1024]{2,1,0:T(8,128)(2,1)} %bitcast.7), calls=%async_computation.1 | async-start | bytes 2097152 | tf_op jit(solution)/shard_map/all_to_all | solution.py:87
  25.7 66.3 %all-reduce.3.cloned.1.call-start = ((), (), s32[]{:S(2)}) async-start(), calls=%async_computation.3 | async-start | bytes 2097152 | tf_op jit(solution)/shard_map/psum | solution.py:110
  55.5 1.0 copy-start
  56.6 77.4 %all-reduce.5.cloned.1.call-start = ((), (), s32[]{:S(2)}) async-start(), calls=%async_computation.4 | async-start | bytes 2097152 | tf_op jit(solution)/shard_map/psum | solution.py:110
  93.5 0.8 copy-start.2
  96.3 1.0 copy-start.1
  96.3 37.7 %copy-start.3 = (bf16[256,1024]{1,0:T(8,128)(2,1)S(1)}, bf16[256,1024]{1,0:T(8,128)(2,1)}, u32[]{:S(2)}) copy-start(bf16[256,1024]{1,0:T(8,128)(2,1)} %copy-done.2) | copy-start | bytes 1572868
  142.9 18.6 %all-to-all-start.2 = ((f32[4,128,256]{2,1,0:T(8,128)}), f32[4,128,256]{2,1,0:T(8,128)S(1)}, u32[]{:S(2)}, u32[]{:S(2)}) async-start(f32[4,128,256]{2,1,0:T(8,128)} %select_select_fusion), calls=%async_computation.2 | async-start | bytes 1048576 | tf_op jit(solution)/shard_map/all_to_all | solution.py:119
Sparse Core Ops, SparseCore 0:
  56.7 35.1 all-reduce.2
  97.4 36.4 all-reduce.4
where the time goes:
time: 171 us; the launch traced here: 170 us
  waiting for transfers between devices  91.3 us (53%)
  blocking collectives  18.9 us (11%)
  local copies, waits for them, and re-layouts  16.4 us (10%)
  between operations  14.9 us (9%)
  starting transfers between devices  14.6 us (9%)
  other arithmetic  11.5 us (7%)
  matrix products  2.42 us (1%)
    psum x2, waiting for transfers between devices, per_device(): all_sums, all_mass = lax.psum((sums, mass), 'hlp')  60.2 us
    all_to_all x1, waiting for transfers between devices, per_device(): lax.all_to_all(outbox.reshape(owners, depth, width), 'own', split_axis=0,...  15.5 us
    all_to_all x1, waiting for transfers between devices, per_device(): lax.all_to_all(slot_logs.reshape(owners, depth, logs.shape[1]), 'own', sp...  13.3 us
    psum x2, blocking collectives, per_device(): all_sums, all_mass = lax.psum((sums, mass), 'hlp')  11.7 us
    all_gather x1, blocking collectives, per_device(): lax.all_gather(subcentroids[0], 'hlp', axis=0, tiled=True)  7.17 us
    all_to_all x1, starting transfers between devices, per_device(): lax.all_to_all(sent_counts, 'own', split_axis=0, concat_axis=0, tiled=True)  6.32 us
    all_to_all x1, starting transfers between devices, per_device(): lax.all_to_all(slot_logs.reshape(owners, depth, logs.shape[1]), 'own', sp...  4.59 us
    all_to_all x1, starting transfers between devices, per_device(): lax.all_to_all(outbox.reshape(owners, depth, width), 'own', split_axis=0,...  3.65 us
  transfers between devices with their start and end apart: 5, of which 5 were waited for; matrix products, arithmetic and copies ran while one was open for 3% of the time, Pallas kernels for 0%

commit v1 on v0

v1 whole, which is shorter than its diff:
```python
import functools

import jax
import jax.numpy as jnp
from jax import lax
from jax.experimental import pallas as pl
from jax.experimental.pallas import tpu as pltpu
from jax.sharding import PartitionSpec as P

ITERS = 2
GROUPS = 4
TILE = 256

smoothing_factor = 16.0
prior_count = 1.0

EMPTY = 64.0
LIMIT = 32.0

BF = jnp.bfloat16
F32 = jnp.float32
NT = (((1,), (1,)), ((), ()))
NN = (((1,), (0,)), ((), ()))


def matmul(a, b, dims):
    return lax.dot_general(a, b, dims, preferred_element_type=F32)


def slots_of(me, cluster, depth, owners):
    count = cluster.shape[1]
    height = max(16, owners)
    offset = jnp.bitwise_xor(cluster, me)
    member = lax.broadcasted_iota(jnp.int32, (height, count), 0) == offset
    earlier = lax.broadcasted_iota(jnp.int32, (count, count), 0) < lax.broadcasted_iota(
        jnp.int32, (count, count), 1
    )
    member = jnp.where(member, 1.0, 0.0)
    before = matmul(member.astype(BF), jnp.where(earlier, 1.0, 0.0).astype(BF), NN)
    rank = jnp.sum(before * member, axis=0, keepdims=True).astype(jnp.int32)
    return offset * depth + rank, jnp.sum(member, axis=1, keepdims=True)


def pack_kernel(depth, owners, me_ref, cluster_ref, points_ref, *outs):
    slot, tally = slots_of(me_ref[0], cluster_ref[...], depth, owners)
    points = points_ref[...]
    height = outs[0].shape[0]
    per = height // depth
    for g, out in enumerate(outs):
        rows = lax.broadcasted_iota(jnp.int32, (height, points.shape[0]), 0) + g * height
        pick = jnp.where(rows == slot, 1.0, 0.0).astype(BF)
        block = matmul(pick, points, NN)
        for j in range(per):
            held = tally[g * per + j : g * per + j + 1, :].astype(jnp.int32)
            local = lax.broadcasted_iota(jnp.int32, (depth, 1), 0)
            part = block[j * depth : (j + 1) * depth]
            out[j * depth : (j + 1) * depth, :] = jnp.where(local < held, part, EMPTY).astype(BF)


def unpack_kernel(depth, owners, me_ref, cluster_ref, *refs):
    *logs, out = refs
    slot, _ = slots_of(me_ref[0], cluster_ref[...], depth, owners)
    count = slot.shape[1]
    column = jnp.broadcast_to(slot.astype(F32), (128, count)).T[:, 0:1].astype(jnp.int32)
    width = logs[0].shape[1]
    total = None
    for g, block in enumerate(logs):
        lanes = lax.broadcasted_iota(jnp.int32, (count, width), 1) + g * width
        pick = jnp.where(lanes == column, 1.0, 0.0).astype(BF)
        term = matmul(pick, block[...], NT)
        total = term if total is None else total + term
    out[...] = total


def square_norms(centres):
    wide = centres.astype(F32)
    return jnp.sum(wide * wide, axis=1, keepdims=True)


def tiles_of(refs):
    tiles, held, size = [], [], 0
    for ref in refs:
        rows = ref.shape[0]
        if rows >= TILE:
            for start in range(0, rows, TILE):
                tiles.append([ref[start : start + TILE, :]])
            continue
        held.append(ref[...])
        size += rows
        if size == TILE:
            tiles.append(held)
            held, size = [], 0
    if held:
        tiles.append(held)
    return [parts[0] if len(parts) == 1 else jnp.concatenate(parts, axis=0) for parts in tiles]


def energies(centres, norms, rows):
    return matmul(centres, rows, NT) * (2.0 / smoothing_factor) - norms * (1.0 / smoothing_factor)


def live_columns(rows):
    first = lax.broadcasted_iota(jnp.int32, (16, 128), 1) == 0
    value = matmul(jnp.where(first, 1.0, 0.0).astype(BF), rows[:, :128], NT)[0:1]
    return jnp.where(value < LIMIT, 1.0, 0.0)


def accumulate(centres, norms, rows, sums_ref, mass_ref, fresh):
    logits = energies(centres, norms, rows)
    top = jnp.max(logits, axis=0, keepdims=True)
    weight = jnp.exp(logits - top)
    scale = live_columns(rows) / jnp.sum(weight, axis=0, keepdims=True)
    share = (weight * scale).astype(BF)
    wide = share.astype(F32)
    mass = wide[:, 0:128]
    for start in range(128, wide.shape[1], 128):
        mass = mass + wide[:, start : start + 128]
    part = matmul(share, rows, NN)
    if fresh:
        mass_ref[...] = mass
        sums_ref[...] = part
    else:
        mass_ref[...] += mass
        sums_ref[...] += part


def first_kernel(centres_ref, *refs):
    *rows, sums_ref, mass_ref = refs
    centres = centres_ref[...]
    norms = square_norms(centres)
    for i, tile in enumerate(tiles_of(rows)):
        accumulate(centres, norms, tile, sums_ref, mass_ref, i == 0)


def next_kernel(centres_ref, old_sums, old_mass, *refs):
    *rows, sums_ref, mass_ref = refs
    centres = centres_ref[...]
    norms = square_norms(centres)
    sums_ref[...] = old_sums[...]
    mass_ref[...] = old_mass[...]
    for tile in tiles_of(rows):
        accumulate(centres, norms, tile, sums_ref, mass_ref, False)


def refine(centres, sums_ref, mass_ref):
    mass = jnp.sum(mass_ref[...], axis=1, keepdims=True)
    return (sums_ref[...] + prior_count * centres.astype(F32)) / (mass + prior_count)


def last_kernel(counts, share_rows, helper_ref, centres_ref, old_sums, old_mass, *refs):
    earlier, late, own = counts
    rows = refs[: earlier + late]
    refined_ref, *logs = refs[earlier + late : earlier + late + 1 + own]
    sums_ref, mass_ref = refs[earlier + late + 1 + own :]
    helper = helper_ref[0]
    centres = centres_ref[...]
    norms = square_norms(centres)
    sums_ref[...] = old_sums[...]
    mass_ref[...] = old_mass[...]
    for tile in tiles_of(rows[earlier:]):
        accumulate(centres, norms, tile, sums_ref, mass_ref, False)
    for turn in range(1, ITERS):
        centres = refine(centres, sums_ref, mass_ref).astype(BF)
        norms = square_norms(centres)
        for i, tile in enumerate(tiles_of(rows)):
            accumulate(centres, norms, tile, sums_ref, mass_ref, i == 0)
    refined = refine(centres, sums_ref, mass_ref)
    refined_ref[...] = refined[0:share_rows]
    centres = refined.astype(BF)
    norms = square_norms(centres)
    parts = (earlier + late) // own
    for g, out in enumerate(logs):
        logits = energies(centres, norms, rows[g * parts][...])
        top = jnp.max(logits, axis=0, keepdims=True)
        total = jnp.log(jnp.sum(jnp.exp(logits - top), axis=0, keepdims=True))
        result = (logits - (top + total)).astype(BF)
        for j in range(centres.shape[0] // share_rows):
            place = pl.multiple_of(jnp.bitwise_xor(helper, j) * share_rows, share_rows)
            out[pl.ds(place, share_rows), :] = result[j * share_rows : (j + 1) * share_rows]


def vmem(n):
    return [pl.BlockSpec(memory_space=pltpu.VMEM)] * n


SMEM = pl.BlockSpec(memory_space=pltpu.SMEM)
PARAMS = pltpu.CompilerParams(vmem_limit_bytes=56 * 1024 * 1024)


def hop(axis, size, step):
    pairs = [(i, i ^ step) for i in range(size)]
    return lambda x: lax.ppermute(x, axis, pairs)


def per_device(points, cluster_of, subcentroids):
    count, width = points.shape
    owners = lax.axis_size("own")
    helpers = lax.axis_size("hlp")
    depth = min(count // 2, 4 * count // owners)
    share_rows = subcentroids.shape[1]
    subs = share_rows * helpers
    groups = min(GROUPS, owners)
    per = owners // groups
    height = per * depth

    me = lax.axis_index("own").astype(jnp.int32).reshape(1)
    helper = lax.axis_index("hlp").astype(jnp.int32).reshape(1)
    cluster = cluster_of.reshape(1, count)

    packed = pl.pallas_call(
        functools.partial(pack_kernel, depth, owners),
        out_shape=[jax.ShapeDtypeStruct((height, width), BF)] * groups,
        in_specs=[SMEM] + vmem(2),
        out_specs=vmem(groups),
        compiler_params=PARAMS,
        name="pack",
    )(me, cluster, points)

    def across(blocks, g, axis):
        done = []
        for j in range(per):
            step = g * per + j
            piece = blocks if per == 1 else lax.slice_in_dim(blocks, j * depth, (j + 1) * depth, axis=axis)
            done.append(piece if step == 0 else hop("own", owners, step)(piece))
        return done[0] if per == 1 else jnp.concatenate(done, axis=axis)

    def spread(block):
        held = {0: block}
        for step in range(2, helpers, 2):
            held[step] = hop("hlp", helpers, step)(block)
        for step in range(0, helpers, 2):
            held[step + 1] = hop("hlp", helpers, 1)(held[step])
        return [held[j] for j in range(helpers)]

    start = jnp.concatenate(spread(subcentroids[0]), axis=0)
    rows = [spread(across(packed[g], g, 0)) for g in range(groups)]

    state = [jax.ShapeDtypeStruct((subs, width), F32), jax.ShapeDtypeStruct((subs, 128), F32)]
    sums, mass = pl.pallas_call(
        first_kernel,
        out_shape=state,
        in_specs=vmem(1 + helpers),
        out_specs=vmem(2),
        compiler_params=PARAMS,
        name="first_rows",
    )(start, *rows[0])
    for g in range(1, groups - 1):
        sums, mass = pl.pallas_call(
            next_kernel,
            out_shape=state,
            in_specs=vmem(3 + helpers),
            out_specs=vmem(2),
            compiler_params=PARAMS,
            name="more_rows",
        )(start, sums, mass, *rows[g])
    earlier = [r for part in rows[: groups - 1] for r in part]
    late = rows[groups - 1]
    refined, *logs = pl.pallas_call(
        functools.partial(last_kernel, (len(earlier), len(late), groups), share_rows),
        out_shape=[jax.ShapeDtypeStruct((share_rows, width), F32)]
        + [jax.ShapeDtypeStruct((subs, height), BF)] * groups,
        in_specs=[SMEM] + vmem(3 + len(earlier) + len(late)),
        out_specs=vmem(1 + groups),
        scratch_shapes=[pltpu.VMEM((subs, width), F32), pltpu.VMEM((subs, 128), F32)],
        compiler_params=PARAMS,
        name="rounds",
    )(helper, start, sums, mass, *earlier, *late)

    back = [across(logs[g], g, 1) for g in range(groups)]
    log_resp = pl.pallas_call(
        functools.partial(unpack_kernel, depth, owners),
        out_shape=jax.ShapeDtypeStruct((count, subs), F32),
        in_specs=[SMEM] + vmem(1 + groups),
        out_specs=pl.BlockSpec(memory_space=pltpu.VMEM),
        compiler_params=PARAMS,
        name="unpack",
    )(me, cluster, *back)
    return (refined[None], log_resp)


def solution(mesh):
    in_specs = (
        P(("grp", "own", "hlp"), None),
        P(("grp", "own", "hlp")),
        P(("grp", "own"), "hlp", None),
    )
    out_specs = (P(("grp", "own"), "hlp", None), P(("grp", "own", "hlp"), None))
    return jax.shard_map(
        per_device, mesh=mesh, in_specs=in_specs, out_specs=out_specs, check_vma=False
    )
```

time: 171 us -> 84.2 us (0.49)
  waiting for transfers between devices: 91.3 us -> 33.3 us
  Pallas kernels: 0 us -> 26.1 us
  blocking collectives: 18.9 us -> 0 us
  between operations: 14.9 us -> 0.8 us
  local copies, waits for them, and re-layouts: 16.4 us -> 2.78 us
  other arithmetic: 11.5 us -> 1.97 us
  starting transfers between devices: 14.6 us -> 18.9 us
  matrix products: 2.42 us -> 0 us
    psum x2 -> x0, waiting for transfers between devices: 60.2 us -> none  [per_device(): all_sums, all_mass = lax.psum((sums, mass), 'hlp')]
    ppermute x0 -> x21, waiting for transfers between devices: none -> 33.3 us  [hop(): return lambda x: lax.ppermute(x, axis, pairs)]
    all_to_all x3 -> x0, waiting for transfers between devices: 31.1 us -> none  [the longest x1 15.5 us: per_device(): lax.all_to_all(outbox.reshape(owners, depth, width), 'own', split_axis=0,...]
    pallas_call x0 -> x6, Pallas kernels: none -> 26.1 us  [the longest x1 10 us: per_device(): pl.pallas_call(functools.partial(last_kernel, (len(earlier), len(late), g...]
    ppermute x0 -> x21, starting transfers between devices: none -> 18.9 us  [hop(): return lambda x: lax.ppermute(x, axis, pairs)]
    all_to_all x3 -> x0, starting transfers between devices: 14.6 us -> none  [the longest x1 6.32 us: per_device(): lax.all_to_all(sent_counts, 'own', split_axis=0, concat_axis=0, tiled=True)]
    psum x2 -> x0, blocking collectives: 11.7 us -> none  [per_device(): all_sums, all_mass = lax.psum((sums, mass), 'hlp')]
    all_gather x1 -> x0, blocking collectives: 7.17 us -> none  [per_device(): lax.all_gather(subcentroids[0], 'hlp', axis=0, tiled=True)]
  transfers between devices with their start and end apart: 5 -> 21, of which waited for: 5 -> 8; matrix products, arithmetic and copies ran while one was open for 3% -> 2% of each run, Pallas kernels for 0% -> 16%
where the time goes in v1:
time: 84.2 us; the launch traced here: 83.9 us
  waiting for transfers between devices  33.3 us (40%)
  Pallas kernels  26.1 us (31%)
  starting transfers between devices  18.9 us (22%)
  local copies, waits for them, and re-layouts  2.78 us (3%)
  other arithmetic  1.97 us (2%)
    ppermute x21, waiting for transfers between devices, hop(): return lambda x: lax.ppermute(x, axis, pairs)  33.3 us
    ppermute x21, starting transfers between devices, hop(): return lambda x: lax.ppermute(x, axis, pairs)  18.9 us
    pallas_call x1, Pallas kernels, per_device(): pl.pallas_call(functools.partial(last_kernel, (len(earlier), len(late), g...  10 us
    pallas_call x2, Pallas kernels, per_device(): pl.pallas_call(next_kernel, out_shape=state, in_specs=vmem(3 + helpers),...  7.79 us
    pallas_call x1, Pallas kernels, per_device(): pl.pallas_call(first_kernel, out_shape=state, in_specs=vmem(1 + helpers),...  3.55 us
    unnamed x40, local copies, waits for them, and re-layouts  2.78 us
    pallas_call x1, Pallas kernels, per_device(): pl.pallas_call(functools.partial(pack_kernel, depth, owners), out_shape=[...  2.45 us
    pallas_call x1, Pallas kernels, per_device(): pl.pallas_call(functools.partial(unpack_kernel, depth, owners), out_shape...  2.32 us
  transfers between devices with their start and end apart: 21, of which 8 were waited for; matrix products, arithmetic and copies ran while one was open for 2% of the time, Pallas kernels for 16%

profile of v1, /device:TPU:0, one launch (start us, length us, event | category | flops | bytes accessed | tf_op | source)
XLA Modules:
  0.0 83.9 jit_solution(10393259722064909979)
XLA Ops:
  0.6 3.0 %collective-permute-start.1 = (bf16[64,1024]{1,0:T(8,128)(2,1)}, bf16[64,1024]{1,0:T(8,128)(2,1)S(1)}, u32[]{:S(2)}, u32[]{:S(2)}) collective-permute-start(bf16[64,1024]{1,0:T(8,128)(2,1)} %bitcast.5), channel_id=1, source_target_pairs={{0,2},{1,3},{2,0},{3,1},{4,6},{5,7},{6,4},{7,5},{8,10},{9,11},{10,... | collective-permute-start | bytes 393224 | tf_op jit(solution)/shard_map/ppermute | solution.py:192
  3.6 0.0 collective-permute-start
  3.6 3.7 %collective-permute-done.1 = bf16[64,1024]{1,0:T(8,128)(2,1)S(1)} collective-permute-done((bf16[64,1024]{1,0:T(8,128)(2,1)}, bf16[64,1024]{1,0:T(8,128)(2,1)S(1)}, u32[]{:S(2)}, u32[]{:S(2)}) %collective-permute-start.1) | collective-permute-done | bytes 131104 | tf_op jit(solution)/shard_map/ppermute | solution.py:192
  7.3 0.0 collective-permute-start.2
  7.3 2.5 %pack.1 = (bf16[128,1024]{1,0:T(8,128)(2,1)}, bf16[128,1024]{1,0:T(8,128)(2,1)}, bf16[128,1024]{1,0:T(8,128)(2,1)}, bf16[128,1024]{1,0:T(8,128)(2,1)}) custom-call(s32[1]{0:T(128)} %bitcast.2.me_ref, s32[1,256]{1,0:T(1,128)} %bitcast.8, bf16[256,1024]{1,0:T(8,128)(2,1)} %points_ref.1), custom_call_target="tpu_custom_call" | custom-call | tf_op jit(solution)/shard_map/pack/pallas_call | solution.py:210
  9.8 0.0 copy-done.14
  9.8 1.8 %collective-permute-start.6 = (bf16[128,1024]{1,0:T(8,128)(2,1)}, bf16[128,1024]{1,0:T(8,128)(2,1)S(1)}, u32[]{:S(2)}, u32[]{:S(2)}) collective-permute-start(bf16[128,1024]{1,0:T(8,128)(2,1)} %get-tuple-element.20), channel_id=1, source_target_pairs={{0,4},{4,0},{8,12},{12,8},{1,5},{5,1},{9,13},{13,9},{2,6},{6,2},{1... | collective-permute-start | bytes 786440 | tf_op jit(solution)/shard_map/ppermute | solution.py:192
  11.6 1.5 %collective-permute-start.4 = (bf16[128,1024]{1,0:T(8,128)(2,1)}, bf16[128,1024]{1,0:T(8,128)(2,1)S(1)}, u32[]{:S(2)}, u32[]{:S(2)}) collective-permute-start(bf16[128,1024]{1,0:T(8,128)(2,1)} %get-tuple-element.17.refs_0_), channel_id=1, source_target_pairs={{0,2},{1,3},{2,0},{3,1},{4,6},{5,7},{6,4},{7,5},{8,10},{9,11},{10,... | collective-permute-start | bytes 786440 | tf_op jit(solution)/shard_map/ppermute | solution.py:192
  13.1 2.6 %collective-permute-start.10 = (bf16[128,1024]{1,0:T(8,128)(2,1)}, bf16[128,1024]{1,0:T(8,128)(2,1)S(1)}, u32[]{:S(2)}, u32[]{:S(2)}) collective-permute-start(bf16[128,1024]{1,0:T(8,128)(2,1)} %get-tuple-element.23), channel_id=1, source_target_pairs={{0,8},{4,12},{8,0},{12,4},{1,9},{5,13},{9,1},{13,5},{2,10},{6,14},... | collective-permute-start | bytes 786440 | tf_op jit(solution)/shard_map/ppermute | solution.py:192
  15.7 0.0 collective-permute-done
  15.7 0.0 collective-permute-start.3
  15.7 0.0 collective-permute-done.2
  15.7 0.6 copy-done.15
  16.4 0.2 collective-permute-start.14
  16.6 6.5 %collective-permute-done.6.refs_0_.refs_4_ = bf16[128,1024]{1,0:T(8,128)(2,1)S(1)} collective-permute-done((bf16[128,1024]{1,0:T(8,128)(2,1)}, bf16[128,1024]{1,0:T(8,128)(2,1)S(1)}, u32[]{:S(2)}, u32[]{:S(2)}) %collective-permute-start.6) | collective-permute-done | bytes 262176 | tf_op jit(solution)/shard_map/ppermute | solution.py:192
  23.1 2.3 %collective-permute-start.8 = (bf16[128,1024]{1,0:T(8,128)(2,1)S(1)}, bf16[128,1024]{1,0:T(8,128)(2,1)S(1)}, u32[]{:S(2)}, u32[]{:S(2)}) collective-permute-start(bf16[128,1024]{1,0:T(8,128)(2,1)S(1)} %collective-permute-done.6.refs_0_.refs_4_), channel_id=1, source_target_pairs={{0,2},{1,3},{2,0},{3,1},{4,6},{5,7},{6,4},{7,5},{8,10},{9,11},{10,... | collective-permute-start | bytes 786440 | tf_op jit(solution)/shard_map/ppermute | solution.py:192
  25.4 0.0 collective-permute-done.4.refs_2_
  25.4 0.0 collective-permute-start.5
  25.4 9.3 %collective-permute-done.10.refs_0_.refs_8_ = bf16[128,1024]{1,0:T(8,128)(2,1)S(1)} collective-permute-done((bf16[128,1024]{1,0:T(8,128)(2,1)}, bf16[128,1024]{1,0:T(8,128)(2,1)S(1)}, u32[]{:S(2)}, u32[]{:S(2)}) %collective-permute-start.10) | collective-permute-done | bytes 262176 | tf_op jit(solution)/shard_map/ppermute | solution.py:192
  34.7 0.5 collective-permute-start.12
  35.2 0.0 collective-permute-done.3.refs_1_
  35.2 0.0 collective-permute-start.7
  35.2 0.0 copy-done.16
  35.2 0.0 collective-permute-done.14.refs_12_
  35.2 0.0 copy-start.11
  35.2 1.6 %collective-permute-start.16 = (bf16[128,1024]{1,0:T(8,128)(2,1)S(1)}, bf16[128,1024]{1,0:T(8,128)(2,1)S(1)}, u32[]{:S(2)}, u32[]{:S(2)}) collective-permute-start(bf16[128,1024]{1,0:T(8,128)(2,1)S(1)} %collective-permute-done.14.refs_12_), channel_id=1, source_target_pairs={{0,2},{1,3},{2,0},{3,1},{4,6},{5,7},{6,4},{7,5},{8,10},{9,11},{10,... | collective-permute-start | bytes 786440 | tf_op jit(solution)/shard_map/ppermute | solution.py:192
  36.8 0.0 collective-permute-done.8.refs_2_.refs_6_
  36.8 0.2 collective-permute-start.9
  37.0 0.0 collective-permute-done.5.refs_3_
  37.0 0.3 collective-permute-start.11
  37.3 6.4 %collective-permute-done.12.refs_2_.refs_10_ = bf16[128,1024]{1,0:T(8,128)(2,1)S(1)} collective-permute-done((bf16[128,1024]{1,0:T(8,128)(2,1)S(1)}, bf16[128,1024]{1,0:T(8,128)(2,1)S(1)}, u32[]{:S(2)}, u32[]{:S(2)}) %collective-permute-start.12) | collective-permute-done | bytes 262176 | tf_op jit(solution)/shard_map/ppermute | solution.py:192
  43.7 0.0 collective-permute-start.13
  43.7 0.0 collective-permute-done.7.refs_1_.refs_5_
  43.7 0.0 copy-start.7
  43.7 0.5 collective-permute-start.15
  44.2 2.4 %collective-permute-done.16.refs_14_ = bf16[128,1024]{1,0:T(8,128)(2,1)S(1)} collective-permute-done((bf16[128,1024]{1,0:T(8,128)(2,1)S(1)}, bf16[128,1024]{1,0:T(8,128)(2,1)S(1)}, u32[]{:S(2)}, u32[]{:S(2)}) %collective-permute-start.16) | collective-permute-done | bytes 262176 | tf_op jit(solution)/shard_map/ppermute | solution.py:192
  46.7 0.0 collective-permute-start.17
  46.7 0.0 copy-done.13
  46.7 2.0 %pad_maximum_fusion.centres_ref = bf16[256,1024]{1,0:T(8,128)(2,1)} fusion(bf16[64,1024]{1,0:T(8,128)(2,1)} %copy-done.16, bf16[64,1024]{1,0:T(8,128)(2,1)} %copy-done.14, bf16[64,1024]{1,0:T(8,128)(2,1)} %copy-done.15, bf16[64,1024]{1,0:T(8,128)(2,1)S(1)} %bitcast.7), kind=kLoop, calls=%fused_computation | loop fusion | flops 2097152 | bytes 1048576 | tf_op jit(solution)/shard_map/concatenate | solution.py:235
  48.6 3.6 %first_rows.1 = (f32[256,1024]{1,0:T(8,128)}, f32[256,128]{1,0:T(8,128)}) custom-call(bf16[256,1024]{1,0:T(8,128)(2,1)} %pad_maximum_fusion.centres_ref, bf16[128,1024]{1,0:T(8,128)(2,1)} %get-tuple-element.17.refs_0_, bf16[128,1024]{1,0:T(8,128)(2,1)} %copy-done.1, bf16[128,1024]{1,0:T(8,128)(2,1)} %copy-done, bf16[128,1024]{1,0:T(8,128)(2,1)} %copy-done.2), custom_call_target="tpu_custom_call" | custom-call | tf_op jit(solution)/shard_map/first_rows/pallas_call | solution.py:239
  52.2 0.0 copy-done.5
  52.2 0.0 copy-done.6
  52.2 0.0 copy-done.7
  52.2 0.0 copy-done.12
  52.2 0.0 collective-permute-done.9.refs_3_.refs_7_
  52.3 0.7 copy-done.8
  53.0 3.9 %more_rows.2 = (f32[256,1024]{1,0:T(8,128)}, f32[256,128]{1,0:T(8,128)}) custom-call(bf16[256,1024]{1,0:T(8,128)(2,1)} %pad_maximum_fusion.centres_ref, f32[256,1024]{1,0:T(8,128)} %get-tuple-element.18.old_sums, f32[256,128]{1,0:T(8,128)} %get-tuple-element.19.old_mass, bf16[128,1024]{1,0:T(8,128)(2,1)} %copy-done.3, bf16[128,1024]{1,0:T(8,128)(2,1)} %copy-done.7, ...), custom_call_target="tpu_custom_call" | custom-call | tf_op jit(solution)/shard_map/more_rows/pallas_call | solution.py:248
  56.8 0.0 collective-permute-done.11.refs_1_.refs_9_
  56.8 0.0 collective-permute-done.13.refs_3_.refs_11_
  56.9 0.7 copy-done.9
  57.6 0.1 copy-done.10
  57.7 3.9 %more_rows.3 = (f32[256,1024]{1,0:T(8,128)}, f32[256,128]{1,0:T(8,128)}) custom-call(bf16[256,1024]{1,0:T(8,128)(2,1)} %pad_maximum_fusion.centres_ref, f32[256,1024]{1,0:T(8,128)} %get-tuple-element.21.old_sums, f32[256,128]{1,0:T(8,128)} %get-tuple-element.22.old_mass, bf16[128,1024]{1,0:T(8,128)(2,1)} %copy-done.4, bf16[128,1024]{1,0:T(8,128)(2,1)} %copy-done.9, ...), custom_call_target="tpu_custom_call" | custom-call | tf_op jit(solution)/shard_map/more_rows/pallas_call | solution.py:248
  61.6 0.0 collective-permute-done.15.refs_13_
  61.6 0.0 collective-permute-done.17.refs_15_
  61.6 10.0 %rounds.1 = (f32[64,1024]{1,0:T(8,128)}, bf16[256,128]{1,0:T(8,128)(2,1)}, bf16[256,128]{1,0:T(8,128)(2,1)}, bf16[256,128]{1,0:T(8,128)(2,1)}, bf16[256,128]{1,0:T(8,128)(2,1)}) custom-call(s32[1]{0:T(128)} %bitcast.helper_ref, bf16[256,1024]{1,0:T(8,128)(2,1)} %pad_maximum_fusion.centres_ref, f32[256,1024]{1,0:T(8,128)} %get-tuple-element.24.old_sums, ...), custom_call_target="tpu_custom_call" | custom-call | tf_op jit(solution)/shard_map/rounds/pallas_call | solution.py:258
  71.6 0.5 collective-permute-start.18
  72.1 2.5 %collective-permute-start.19 = (bf16[256,128]{1,0:T(8,128)(2,1)}, bf16[256,128]{1,0:T(8,128)(2,1)S(1)}, u32[]{:S(2)}, u32[]{:S(2)}) collective-permute-start(bf16[256,128]{1,0:T(8,128)(2,1)} %get-tuple-element.30), channel_id=1, source_target_pairs={{0,8},{4,12},{8,0},{12,4},{1,9},{5,13},{9,1},{13,5},{2,10},{6,14},... | collective-permute-start | bytes 196616 | tf_op jit(solution)/shard_map/ppermute | solution.py:192
  74.6 1.4 %collective-permute-start.20 = (bf16[256,128]{1,0:T(8,128)(2,1)}, bf16[256,128]{1,0:T(8,128)(2,1)S(1)}, u32[]{:S(2)}, u32[]{:S(2)}) collective-permute-start(bf16[256,128]{1,0:T(8,128)(2,1)} %get-tuple-element.31), channel_id=1, source_target_pairs={{0,12},{4,8},{8,4},{12,0},{1,13},{5,9},{9,5},{13,1},{2,14},{6,10},... | collective-permute-start | bytes 196616 | tf_op jit(solution)/shard_map/ppermute | solution.py:192
  76.0 1.2 %collective-permute-done.18.refs_1_ = bf16[256,128]{1,0:T(8,128)(2,1)S(1)} collective-permute-done((bf16[256,128]{1,0:T(8,128)(2,1)}, bf16[256,128]{1,0:T(8,128)(2,1)S(1)}, u32[]{:S(2)}, u32[]{:S(2)}) %collective-permute-start.18) | collective-permute-done | bytes 65568 | tf_op jit(solution)/shard_map/ppermute | solution.py:192
  77.2 2.8 %collective-permute-done.19.refs_2_ = bf16[256,128]{1,0:T(8,128)(2,1)S(1)} collective-permute-done((bf16[256,128]{1,0:T(8,128)(2,1)}, bf16[256,128]{1,0:T(8,128)(2,1)S(1)}, u32[]{:S(2)}, u32[]{:S(2)}) %collective-permute-start.19) | collective-permute-done | bytes 65568 | tf_op jit(solution)/shard_map/ppermute | solution.py:192
  80.0 1.0 %collective-permute-done.20.refs_3_ = bf16[256,128]{1,0:T(8,128)(2,1)S(1)} collective-permute-done((bf16[256,128]{1,0:T(8,128)(2,1)}, bf16[256,128]{1,0:T(8,128)(2,1)S(1)}, u32[]{:S(2)}, u32[]{:S(2)}) %collective-permute-start.20) | collective-permute-done | bytes 65568 | tf_op jit(solution)/shard_map/ppermute | solution.py:192
  81.0 0.0 copy-done.18
  81.0 0.6 copy-done.19
  81.6 2.3 %unpack.1 = f32[256,256]{1,0:T(8,128)} custom-call(s32[1]{0:T(128)} %bitcast.2.me_ref, s32[1,256]{1,0:T(1,128)} %bitcast.9, bf16[256,128]{1,0:T(8,128)(2,1)} %get-tuple-element.28.refs_0_, bf16[256,128]{1,0:T(8,128)(2,1)} %copy-done.17, bf16[256,128]{1,0:T(8,128)(2,1)} %copy-done.18, bf16[256,128]{1,0:T(8,128)(2,1)} %copy-done.19), custom_call_target="tpu_custom_call" | custom-call | tf_op jit(solution)/shard_map/unpack/pallas_call | solution.py:270
  (25 shorter events, 0.0 us)
Async XLA Ops:
  0.6 6.7 %collective-permute-start.1 = (bf16[64,1024]{1,0:T(8,128)(2,1)}, bf16[64,1024]{1,0:T(8,128)(2,1)S(1)}, u32[]{:S(2)}, u32[]{:S(2)}) collective-permute-start(bf16[64,1024]{1,0:T(8,128)(2,1)} %bitcast.5), channel_id=1, source_target_pairs={{0,2},{1,3},{2,0},{3,1},{4,6},{5,7},{6,4},{7,5},{8,10},{9,11},{10,... | collective-permute-start | bytes 393224 | tf_op jit(solution)/shard_map/ppermute | solution.py:192
  3.6 12.1 %collective-permute-start = (bf16[64,1024]{1,0:T(8,128)(2,1)}, bf16[64,1024]{1,0:T(8,128)(2,1)S(1)}, u32[]{:S(2)}, u32[]{:S(2)}) collective-permute-start(bf16[64,1024]{1,0:T(8,128)(2,1)} %bitcast.6), channel_id=1, source_target_pairs={{0,1},{1,0},{2,3},{3,2},{4,5},{5,4},{6,7},{7,6},{8,9},{9,8},{10,11... | collective-permute-start | bytes 393224 | tf_op jit(solution)/shard_map/ppermute | solution.py:192
  7.3 2.5 %copy-start.14 = (bf16[64,1024]{1,0:T(8,128)(2,1)}, bf16[64,1024]{1,0:T(8,128)(2,1)S(1)}, u32[]{:S(2)}) copy-start(bf16[64,1024]{1,0:T(8,128)(2,1)S(1)} %collective-permute-done.1) | copy-start | bytes 393220
  7.3 8.4 %collective-permute-start.2 = (bf16[64,1024]{1,0:T(8,128)(2,1)S(1)}, bf16[64,1024]{1,0:T(8,128)(2,1)S(1)}, u32[]{:S(2)}, u32[]{:S(2)}) collective-permute-start(bf16[64,1024]{1,0:T(8,128)(2,1)S(1)} %collective-permute-done.1), channel_id=1, source_target_pairs={{0,1},{1,0},{2,3},{3,2},{4,5},{5,4},{6,7},{7,6},{8,9},{9,8},{10,11... | collective-permute-start | bytes 393224 | tf_op jit(solution)/shard_map/ppermute | solution.py:192
  7.3 39.3 %copy-start.13 = (bf16[1,64,1024]{2,1,0:T(8,128)(2,1)S(1)}, bf16[1,64,1024]{2,1,0:T(8,128)(2,1)}, u32[]{:S(2)}) copy-start(bf16[1,64,1024]{2,1,0:T(8,128)(2,1)} %param.5) | copy-start | bytes 393220
  9.8 13.3 %collective-permute-start.6 = (bf16[128,1024]{1,0:T(8,128)(2,1)}, bf16[128,1024]{1,0:T(8,128)(2,1)S(1)}, u32[]{:S(2)}, u32[]{:S(2)}) collective-permute-start(bf16[128,1024]{1,0:T(8,128)(2,1)} %get-tuple-element.20), channel_id=1, source_target_pairs={{0,4},{4,0},{8,12},{12,8},{1,5},{5,1},{9,13},{13,9},{2,6},{6,2},{1... | collective-permute-start | bytes 786440 | tf_op jit(solution)/shard_map/ppermute | solution.py:192
  11.6 13.8 %collective-permute-start.4 = (bf16[128,1024]{1,0:T(8,128)(2,1)}, bf16[128,1024]{1,0:T(8,128)(2,1)S(1)}, u32[]{:S(2)}, u32[]{:S(2)}) collective-permute-start(bf16[128,1024]{1,0:T(8,128)(2,1)} %get-tuple-element.17.refs_0_), channel_id=1, source_target_pairs={{0,2},{1,3},{2,0},{3,1},{4,6},{5,7},{6,4},{7,5},{8,10},{9,11},{10,... | collective-permute-start | bytes 786440 | tf_op jit(solution)/shard_map/ppermute | solution.py:192
  13.1 21.5 %collective-permute-start.10 = (bf16[128,1024]{1,0:T(8,128)(2,1)}, bf16[128,1024]{1,0:T(8,128)(2,1)S(1)}, u32[]{:S(2)}, u32[]{:S(2)}) collective-permute-start(bf16[128,1024]{1,0:T(8,128)(2,1)} %get-tuple-element.23), channel_id=1, source_target_pairs={{0,8},{4,12},{8,0},{12,4},{1,9},{5,13},{9,1},{13,5},{2,10},{6,14},... | collective-permute-start | bytes 786440 | tf_op jit(solution)/shard_map/ppermute | solution.py:192
  15.7 0.6 copy-start.15
  15.7 19.5 %collective-permute-start.3 = (bf16[128,1024]{1,0:T(8,128)(2,1)}, bf16[128,1024]{1,0:T(8,128)(2,1)S(1)}, u32[]{:S(2)}, u32[]{:S(2)}) collective-permute-start(bf16[128,1024]{1,0:T(8,128)(2,1)} %get-tuple-element.17.refs_0_), channel_id=1, source_target_pairs={{0,1},{1,0},{2,3},{3,2},{4,5},{5,4},{6,7},{7,6},{8,9},{9,8},{10,11... | collective-permute-start | bytes 786440 | tf_op jit(solution)/shard_map/ppermute | solution.py:192
  16.4 18.8 %copy-start.16 = (bf16[64,1024]{1,0:T(8,128)(2,1)}, bf16[64,1024]{1,0:T(8,128)(2,1)S(1)}, u32[]{:S(2)}) copy-start(bf16[64,1024]{1,0:T(8,128)(2,1)S(1)} %collective-permute-done.2) | copy-start | bytes 393220
  16.4 18.9 %collective-permute-start.14 = (bf16[128,1024]{1,0:T(8,128)(2,1)}, bf16[128,1024]{1,0:T(8,128)(2,1)S(1)}, u32[]{:S(2)}, u32[]{:S(2)}) collective-permute-start(bf16[128,1024]{1,0:T(8,128)(2,1)} %get-tuple-element.26), channel_id=1, source_target_pairs={{0,12},{4,8},{8,4},{12,0},{1,13},{5,9},{9,5},{13,1},{2,14},{6,10},... | collective-permute-start | bytes 786440 | tf_op jit(solution)/shard_map/ppermute | solution.py:192
  23.1 25.5 %copy-start.3 = (bf16[128,1024]{1,0:T(8,128)(2,1)}, bf16[128,1024]{1,0:T(8,128)(2,1)S(1)}, u32[]{:S(2)}) copy-start(bf16[128,1024]{1,0:T(8,128)(2,1)S(1)} %collective-permute-done.6.refs_0_.refs_4_) | copy-start | bytes 786436
  23.1 13.7 %collective-permute-start.8 = (bf16[128,1024]{1,0:T(8,128)(2,1)S(1)}, bf16[128,1024]{1,0:T(8,128)(2,1)S(1)}, u32[]{:S(2)}, u32[]{:S(2)}) collective-permute-start(bf16[128,1024]{1,0:T(8,128)(2,1)S(1)} %collective-permute-done.6.refs_0_.refs_4_), channel_id=1, source_target_pairs={{0,2},{1,3},{2,0},{3,1},{4,6},{5,7},{6,4},{7,5},{8,10},{9,11},{10,... | collective-permute-start | bytes 786440 | tf_op jit(solution)/shard_map/ppermute | solution.py:192
  25.4 23.2 %copy-start = (bf16[128,1024]{1,0:T(8,128)(2,1)}, bf16[128,1024]{1,0:T(8,128)(2,1)S(1)}, u32[]{:S(2)}) copy-start(bf16[128,1024]{1,0:T(8,128)(2,1)S(1)} %collective-permute-done.4.refs_2_) | copy-start | bytes 786436
  25.4 11.6 %collective-permute-start.5 = (bf16[128,1024]{1,0:T(8,128)(2,1)S(1)}, bf16[128,1024]{1,0:T(8,128)(2,1)S(1)}, u32[]{:S(2)}, u32[]{:S(2)}) collective-permute-start(bf16[128,1024]{1,0:T(8,128)(2,1)S(1)} %collective-permute-done.4.refs_2_), channel_id=1, source_target_pairs={{0,1},{1,0},{2,3},{3,2},{4,5},{5,4},{6,7},{7,6},{8,9},{9,8},{10,11... | collective-permute-start | bytes 786440 | tf_op jit(solution)/shard_map/ppermute | solution.py:192
  34.7 17.5 %copy-start.4 = (bf16[128,1024]{1,0:T(8,128)(2,1)}, bf16[128,1024]{1,0:T(8,128)(2,1)S(1)}, u32[]{:S(2)}) copy-start(bf16[128,1024]{1,0:T(8,128)(2,1)S(1)} %collective-permute-done.10.refs_0_.refs_8_) | copy-start | bytes 786436
  34.7 9.0 %collective-permute-start.12 = (bf16[128,1024]{1,0:T(8,128)(2,1)S(1)}, bf16[128,1024]{1,0:T(8,128)(2,1)S(1)}, u32[]{:S(2)}, u32[]{:S(2)}) collective-permute-start(bf16[128,1024]{1,0:T(8,128)(2,1)S(1)} %collective-permute-done.10.refs_0_.refs_8_), channel_id=1, source_target_pairs={{0,2},{1,3},{2,0},{3,1},{4,6},{5,7},{6,4},{7,5},{8,10},{9,11},{10,... | collective-permute-start | bytes 786440 | tf_op jit(solution)/shard_map/ppermute | solution.py:192
  35.2 13.4 %copy-start.1 = (bf16[128,1024]{1,0:T(8,128)(2,1)}, bf16[128,1024]{1,0:T(8,128)(2,1)S(1)}, u32[]{:S(2)}) copy-start(bf16[128,1024]{1,0:T(8,128)(2,1)S(1)} %collective-permute-done.3.refs_1_) | copy-start | bytes 786436
  35.2 8.5 %collective-permute-start.7 = (bf16[128,1024]{1,0:T(8,128)(2,1)S(1)}, bf16[128,1024]{1,0:T(8,128)(2,1)S(1)}, u32[]{:S(2)}, u32[]{:S(2)}) collective-permute-start(bf16[128,1024]{1,0:T(8,128)(2,1)S(1)} %collective-permute-done.6.refs_0_.refs_4_), channel_id=1, source_target_pairs={{0,1},{1,0},{2,3},{3,2},{4,5},{5,4},{6,7},{7,6},{8,9},{9,8},{10,11... | collective-permute-start | bytes 786440 | tf_op jit(solution)/shard_map/ppermute | solution.py:192
  35.2 17.0 %copy-start.11 = (bf16[128,1024]{1,0:T(8,128)(2,1)}, bf16[128,1024]{1,0:T(8,128)(2,1)S(1)}, u32[]{:S(2)}) copy-start(bf16[128,1024]{1,0:T(8,128)(2,1)S(1)} %collective-permute-done.14.refs_12_) | copy-start | bytes 786436
  35.2 11.4 %collective-permute-start.16 = (bf16[128,1024]{1,0:T(8,128)(2,1)S(1)}, bf16[128,1024]{1,0:T(8,128)(2,1)S(1)}, u32[]{:S(2)}, u32[]{:S(2)}) collective-permute-start(bf16[128,1024]{1,0:T(8,128)(2,1)S(1)} %collective-permute-done.14.refs_12_), channel_id=1, source_target_pairs={{0,2},{1,3},{2,0},{3,1},{4,6},{5,7},{6,4},{7,5},{8,10},{9,11},{10,... | collective-permute-start | bytes 786440 | tf_op jit(solution)/shard_map/ppermute | solution.py:192
  36.8 15.4 %copy-start.5 = (bf16[128,1024]{1,0:T(8,128)(2,1)}, bf16[128,1024]{1,0:T(8,128)(2,1)S(1)}, u32[]{:S(2)}) copy-start(bf16[128,1024]{1,0:T(8,128)(2,1)S(1)} %collective-permute-done.8.refs_2_.refs_6_) | copy-start | bytes 786436
  36.8 15.5 %collective-permute-start.9 = (bf16[128,1024]{1,0:T(8,128)(2,1)S(1)}, bf16[128,1024]{1,0:T(8,128)(2,1)S(1)}, u32[]{:S(2)}, u32[]{:S(2)}) collective-permute-start(bf16[128,1024]{1,0:T(8,128)(2,1)S(1)} %collective-permute-done.8.refs_2_.refs_6_), channel_id=1, source_target_pairs={{0,1},{1,0},{2,3},{3,2},{4,5},{5,4},{6,7},{7,6},{8,9},{9,8},{10,11... | collective-permute-start | bytes 786440 | tf_op jit(solution)/shard_map/ppermute | solution.py:192
  37.0 11.6 %copy-start.2 = (bf16[128,1024]{1,0:T(8,128)(2,1)}, bf16[128,1024]{1,0:T(8,128)(2,1)S(1)}, u32[]{:S(2)}) copy-start(bf16[128,1024]{1,0:T(8,128)(2,1)S(1)} %collective-permute-done.5.refs_3_) | copy-start | bytes 786436
  37.0 19.8 %collective-permute-start.11 = (bf16[128,1024]{1,0:T(8,128)(2,1)S(1)}, bf16[128,1024]{1,0:T(8,128)(2,1)S(1)}, u32[]{:S(2)}, u32[]{:S(2)}) collective-permute-start(bf16[128,1024]{1,0:T(8,128)(2,1)S(1)} %collective-permute-done.10.refs_0_.refs_8_), channel_id=1, source_target_pairs={{0,1},{1,0},{2,3},{3,2},{4,5},{5,4},{6,7},{7,6},{8,9},{9,8},{10,11... | collective-permute-start | bytes 786440 | tf_op jit(solution)/shard_map/ppermute | solution.py:192
  43.7 8.5 %copy-start.6 = (bf16[128,1024]{1,0:T(8,128)(2,1)}, bf16[128,1024]{1,0:T(8,128)(2,1)S(1)}, u32[]{:S(2)}) copy-start(bf16[128,1024]{1,0:T(8,128)(2,1)S(1)} %collective-permute-done.12.refs_2_.refs_10_) | copy-start | bytes 786436
  43.7 13.2 %collective-permute-start.13 = (bf16[128,1024]{1,0:T(8,128)(2,1)S(1)}, bf16[128,1024]{1,0:T(8,128)(2,1)S(1)}, u32[]{:S(2)}, u32[]{:S(2)}) collective-permute-start(bf16[128,1024]{1,0:T(8,128)(2,1)S(1)} %collective-permute-done.12.refs_2_.refs_10_), channel_id=1, source_target_pairs={{0,1},{1,0},{2,3},{3,2},{4,5},{5,4},{6,7},{7,6},{8,9},{9,8},{10,11... | collective-permute-start | bytes 786440 | tf_op jit(solution)/shard_map/ppermute | solution.py:192
  43.7 8.5 %copy-start.7 = (bf16[128,1024]{1,0:T(8,128)(2,1)}, bf16[128,1024]{1,0:T(8,128)(2,1)S(1)}, u32[]{:S(2)}) copy-start(bf16[128,1024]{1,0:T(8,128)(2,1)S(1)} %collective-permute-done.7.refs_1_.refs_5_) | copy-start | bytes 786436
  43.7 17.8 %collective-permute-start.15 = (bf16[128,1024]{1,0:T(8,128)(2,1)S(1)}, bf16[128,1024]{1,0:T(8,128)(2,1)}, u32[]{:S(2)}, u32[]{:S(2)}) collective-permute-start(bf16[128,1024]{1,0:T(8,128)(2,1)S(1)} %collective-permute-done.14.refs_12_), channel_id=1, source_target_pairs={{0,1},{1,0},{2,3},{3,2},{4,5},{5,4},{6,7},{7,6},{8,9},{9,8},{10,11... | collective-permute-start | bytes 786440 | tf_op jit(solution)/shard_map/ppermute | solution.py:192
  46.6 5.6 %copy-start.12 = (bf16[128,1024]{1,0:T(8,128)(2,1)}, bf16[128,1024]{1,0:T(8,128)(2,1)S(1)}, u32[]{:S(2)}) copy-start(bf16[128,1024]{1,0:T(8,128)(2,1)S(1)} %collective-permute-done.16.refs_14_) | copy-start | bytes 786436
  46.7 14.9 %collective-permute-start.17 = (bf16[128,1024]{1,0:T(8,128)(2,1)S(1)}, bf16[128,1024]{1,0:T(8,128)(2,1)}, u32[]{:S(2)}, u32[]{:S(2)}) collective-permute-start(bf16[128,1024]{1,0:T(8,128)(2,1)S(1)} %collective-permute-done.16.refs_14_), channel_id=1, source_target_pairs={{0,1},{1,0},{2,3},{3,2},{4,5},{5,4},{6,7},{7,6},{8,9},{9,8},{10,11... | collective-permute-start | bytes 786440 | tf_op jit(solution)/shard_map/ppermute | solution.py:192
  52.3 0.7 copy-start.8
  56.8 0.7 copy-start.9
  56.9 0.8 copy-start.10
  71.6 5.6 %collective-permute-start.18 = (bf16[256,128]{1,0:T(8,128)(2,1)}, bf16[256,128]{1,0:T(8,128)(2,1)S(1)}, u32[]{:S(2)}, u32[]{:S(2)}) collective-permute-start(bf16[256,128]{1,0:T(8,128)(2,1)} %get-tuple-element.29), channel_id=1, source_target_pairs={{0,4},{4,0},{8,12},{12,8},{1,5},{5,1},{9,13},{13,9},{2,6},{6,2},{1... | collective-permute-start | bytes 196616 | tf_op jit(solution)/shard_map/ppermute | solution.py:192
  72.1 7.9 %collective-permute-start.19 = (bf16[256,128]{1,0:T(8,128)(2,1)}, bf16[256,128]{1,0:T(8,128)(2,1)S(1)}, u32[]{:S(2)}, u32[]{:S(2)}) collective-permute-start(bf16[256,128]{1,0:T(8,128)(2,1)} %get-tuple-element.30), channel_id=1, source_target_pairs={{0,8},{4,12},{8,0},{12,4},{1,9},{5,13},{9,1},{13,5},{2,10},{6,14},... | collective-permute-start | bytes 196616 | tf_op jit(solution)/shard_map/ppermute | solution.py:192
  74.6 6.3 %collective-permute-start.20 = (bf16[256,128]{1,0:T(8,128)(2,1)}, bf16[256,128]{1,0:T(8,128)(2,1)S(1)}, u32[]{:S(2)}, u32[]{:S(2)}) collective-permute-start(bf16[256,128]{1,0:T(8,128)(2,1)} %get-tuple-element.31), channel_id=1, source_target_pairs={{0,12},{4,8},{8,4},{12,0},{1,13},{5,9},{9,5},{13,1},{2,14},{6,10},... | collective-permute-start | bytes 196616 | tf_op jit(solution)/shard_map/ppermute | solution.py:192
  77.2 3.8 %copy-start.17 = (bf16[256,128]{1,0:T(8,128)(2,1)}, bf16[256,128]{1,0:T(8,128)(2,1)S(1)}, u32[]{:S(2)}) copy-start(bf16[256,128]{1,0:T(8,128)(2,1)S(1)} %collective-permute-done.18.refs_1_) | copy-start | bytes 196612
  80.0 1.0 %copy-start.18 = (bf16[256,128]{1,0:T(8,128)(2,1)}, bf16[256,128]{1,0:T(8,128)(2,1)S(1)}, u32[]{:S(2)}) copy-start(bf16[256,128]{1,0:T(8,128)(2,1)S(1)} %collective-permute-done.19.refs_2_) | copy-start | bytes 196612
  81.0 0.6 copy-start.19

commit v2 on v1

v2 whole, which is shorter than its diff:
```python
import functools
import math

import jax
import jax.numpy as jnp
from jax import lax
from jax.experimental import pallas as pl
from jax.experimental.pallas import tpu as pltpu
from jax.sharding import PartitionSpec as P

ITERS = 2
GROUPS = 4
TILE = 256

smoothing_factor = 16.0
prior_count = 1.0

EMPTY = 64.0
LIMIT = 32.0

BF = jnp.bfloat16
F32 = jnp.float32
TN = (((0,), (0,)), ((), ()))
NN = (((1,), (0,)), ((), ()))


def matmul(a, b, dims):
    return lax.dot_general(a, b, dims, preferred_element_type=F32)


def slots_of(me, cluster, depth, owners):
    count = cluster.shape[1]
    height = max(16, owners)
    offset = jnp.bitwise_xor(cluster, me)
    member = lax.broadcasted_iota(jnp.int32, (height, count), 0) == offset
    earlier = lax.broadcasted_iota(jnp.int32, (count, count), 0) < lax.broadcasted_iota(
        jnp.int32, (count, count), 1
    )
    member = jnp.where(member, 1.0, 0.0)
    before = matmul(member.astype(BF), jnp.where(earlier, 1.0, 0.0).astype(BF), NN)
    rank = jnp.sum(before * member, axis=0, keepdims=True).astype(jnp.int32)
    return offset * depth + rank, jnp.sum(member, axis=1, keepdims=True)


def pack_kernel(depth, owners, me_ref, cluster_ref, points_ref, *outs):
    slot, tally = slots_of(me_ref[0], cluster_ref[...], depth, owners)
    points = points_ref[...]
    height = outs[0].shape[0]
    per = height // depth
    for g, out in enumerate(outs):
        rows = lax.broadcasted_iota(jnp.int32, (height, points.shape[0]), 0) + g * height
        pick = jnp.where(rows == slot, 1.0, 0.0).astype(BF)
        block = matmul(pick, points, NN)
        for j in range(per):
            held = tally[g * per + j : g * per + j + 1, :].astype(jnp.int32)
            local = lax.broadcasted_iota(jnp.int32, (depth, 1), 0)
            part = block[j * depth : (j + 1) * depth]
            out[j * depth : (j + 1) * depth, :] = jnp.where(local < held, part, EMPTY).astype(BF)


def unpack_kernel(depth, owners, me_ref, cluster_ref, *refs):
    *logs, out = refs
    slot, _ = slots_of(me_ref[0], cluster_ref[...], depth, owners)
    count = slot.shape[1]
    column = jnp.broadcast_to(slot.astype(F32), (128, count)).T[:, 0:1].astype(jnp.int32)
    height = logs[0].shape[0]
    total = None
    for g, block in enumerate(logs):
        lanes = lax.broadcasted_iota(jnp.int32, (count, height), 1) + g * height
        pick = jnp.where(lanes == column, 1.0, 0.0).astype(BF)
        term = matmul(pick, block[...], NN)
        total = term if total is None else total + term
    out[...] = total


def square_norms(centres):
    wide = centres.astype(F32)
    column = jnp.sum(wide * wide, axis=1, keepdims=True)
    return jnp.broadcast_to(column, (column.shape[0], 128)).T[0:1]


def tiles_of(refs):
    tiles, held, size = [], [], 0
    for ref in refs:
        rows = ref.shape[0]
        if rows >= TILE:
            for start in range(0, rows, TILE):
                tiles.append([ref[start : start + TILE, :]])
            continue
        held.append(ref[...])
        size += rows
        if size == TILE:
            tiles.append(held)
            held, size = [], 0
    if held:
        tiles.append(held)
    return [joined(parts) for parts in tiles]


def joined(parts):
    return parts[0] if len(parts) == 1 else jnp.concatenate(parts, axis=0)


def energies(turned, norms, rows):
    return matmul(rows, turned, NN) * (2.0 / smoothing_factor) - norms * (1.0 / smoothing_factor)


def accumulate(turned, norms, tiles, share_ref, sums_ref, mass_ref, fresh):
    start = 0
    for rows in tiles:
        logits = energies(turned, norms, rows)
        top = jnp.max(logits, axis=1, keepdims=True)
        weight = jnp.exp(logits - top)
        live = jnp.where(rows[:, 0:1].astype(F32) < LIMIT, 1.0, 0.0)
        scale = live / jnp.sum(weight, axis=1, keepdims=True)
        share_ref[start : start + rows.shape[0], :] = (weight * scale).astype(BF)
        start += rows.shape[0]
    start = 0
    for i, rows in enumerate(tiles):
        share = share_ref[start : start + rows.shape[0], :]
        mass = matmul(share, jnp.ones((rows.shape[0], 128), BF), TN)
        part = matmul(share, rows, TN)
        if fresh and i == 0:
            mass_ref[...] = mass
            sums_ref[...] = part
        else:
            mass_ref[...] += mass
            sums_ref[...] += part
        start += rows.shape[0]


def first_kernel(helpers, *refs):
    centres = joined([ref[...] for ref in refs[:helpers]])
    *rows, sums_ref, mass_ref, share_ref = refs[helpers:]
    accumulate(centres.T, square_norms(centres), tiles_of(rows), share_ref, sums_ref, mass_ref, True)


def refine(centres, sums_ref, mass_ref):
    mass = mass_ref[:, 0:1]
    return (sums_ref[...] + prior_count * centres.astype(F32)) / (mass + prior_count)


def last_kernel(helpers, counts, share_rows, helper_ref, *refs):
    earlier, late, own = counts
    centres = joined([ref[...] for ref in refs[:helpers]])
    old_sums, old_mass, *refs = refs[helpers:]
    given = refs[: earlier + late]
    refined_ref, *logs = refs[earlier + late : earlier + late + 1 + own]
    sums_ref, mass_ref, ordered, share_ref, rows, arrived = refs[earlier + late + 1 + own :]
    height = given[0].shape[0]
    copies = [
        pltpu.make_async_copy(ref, rows.at[i * height : (i + 1) * height], arrived.at[i])
        for i, ref in enumerate(given)
    ]
    for copy in copies[earlier:] + copies[:earlier]:
        copy.start()
    helper = helper_ref[0]
    norms = square_norms(centres)
    turned = centres.T
    sums_ref[...] = old_sums[...]
    mass_ref[...] = old_mass[...]
    for copy in copies[earlier:]:
        copy.wait()

    def tiles(first, last):
        return [rows[r : r + TILE, :] for r in range(first * height, last * height, TILE)]

    accumulate(turned, norms, tiles(earlier, earlier + late), share_ref, sums_ref, mass_ref, False)
    for copy in copies[:earlier]:
        copy.wait()
    for turn in range(1, ITERS):
        centres = refine(centres, sums_ref, mass_ref).astype(BF)
        norms = square_norms(centres)
        turned = centres.T
        accumulate(turned, norms, tiles(0, earlier + late), share_ref, sums_ref, mass_ref, True)
    refined = refine(centres, sums_ref, mass_ref)
    refined_ref[...] = refined[0:share_rows]
    centres = refined.astype(BF)
    for j in range(helpers):
        place = pl.multiple_of(jnp.bitwise_xor(helper, j) * share_rows, share_rows)
        ordered[pl.ds(place, share_rows), :] = centres[j * share_rows : (j + 1) * share_rows]
    centres = ordered[...]
    norms = square_norms(centres)
    turned = centres.T
    for g, out in enumerate(logs):
        first = g * helpers * height
        logits = energies(turned, norms, rows[first : first + height, :])
        top = jnp.max(logits, axis=1, keepdims=True)
        total = jnp.log(jnp.sum(jnp.exp(logits - top), axis=1, keepdims=True))
        out[...] = (logits - (top + total)).astype(BF)


def vmem(n):
    return [pl.BlockSpec(memory_space=pltpu.VMEM)] * n


SMEM = pl.BlockSpec(memory_space=pltpu.SMEM)
COST = pl.CostEstimate(flops=1, bytes_accessed=1, transcendentals=0)


def params(*arrays):
    held = sum(math.prod(a.shape) * a.dtype.itemsize for a in arrays)
    return pltpu.CompilerParams(vmem_limit_bytes=held + 8 * 1024 * 1024)


def after(value, *others):
    return lax.optimization_barrier((value,) + others)[0]


def hop(axis, size, step):
    pairs = [(i, i ^ step) for i in range(size)]
    return lambda x: lax.ppermute(x, axis, pairs)


def per_device(points, cluster_of, subcentroids):
    count, width = points.shape
    owners = lax.axis_size("own")
    helpers = lax.axis_size("hlp")
    depth = min(count // 2, 4 * count // owners)
    share_rows = subcentroids.shape[1]
    subs = share_rows * helpers
    groups = min(GROUPS, owners)
    per = owners // groups
    height = per * depth

    me = lax.axis_index("own").astype(jnp.int32).reshape(1)
    helper = lax.axis_index("hlp").astype(jnp.int32).reshape(1)
    cluster = cluster_of.reshape(1, count)

    blocks = [jax.ShapeDtypeStruct((height, width), BF)] * groups
    packed = pl.pallas_call(
        functools.partial(pack_kernel, depth, owners),
        out_shape=blocks,
        in_specs=[SMEM] + vmem(2),
        out_specs=vmem(groups),
        compiler_params=params(points, *blocks),
        cost_estimate=COST,
        name="pack",
    )(me, cluster, points)

    def across(block, g):
        done = []
        for j in range(per):
            step = g * per + j
            piece = block if per == 1 else block[j * depth : (j + 1) * depth]
            done.append(piece if step == 0 else hop("own", owners, step)(piece))
        return joined(done)

    def over_chips(block):
        return [block] + [hop("hlp", helpers, step)(block) for step in range(2, helpers, 2)]

    def over_cores(held):
        return [x for block in held for x in (block, hop("hlp", helpers, 1)(block))]

    state = [jax.ShapeDtypeStruct((subs, width), F32), jax.ShapeDtypeStruct((subs, 128), F32)]
    moved = [across(packed[g], g) for g in range(groups)]
    held = [over_chips(block) for block in moved]
    start = over_cores(over_chips(after(subcentroids[0], *held[0])))
    soon = groups // 2
    earlier = [r for part in held[:soon] for r in over_cores(part)]
    shares = jax.ShapeDtypeStruct((len(earlier) * height, subs), BF)
    sums, mass = pl.pallas_call(
        functools.partial(first_kernel, helpers),
        out_shape=state,
        in_specs=vmem(len(start) + len(earlier)),
        out_specs=vmem(2),
        scratch_shapes=[pltpu.VMEM(shares.shape, BF)],
        compiler_params=params(*start, *earlier, *state, shares),
        cost_estimate=COST,
        name="first_rows",
    )(*start, *earlier)
    late = [r for part in held[soon:-1] for r in over_cores(part)]
    late += over_cores(held[-1][:-1] + [after(held[-1][-1], sums)])
    logs = [jax.ShapeDtypeStruct((height, subs), BF)] * groups
    refined = jax.ShapeDtypeStruct((share_rows, width), F32)
    total = (len(earlier) + len(late)) * height
    scratch = state + [
        jax.ShapeDtypeStruct((subs, width), BF),
        jax.ShapeDtypeStruct((total, subs), BF),
        jax.ShapeDtypeStruct((total, width), BF),
    ]
    refined, *logs = pl.pallas_call(
        functools.partial(last_kernel, helpers, (len(earlier), len(late), groups), share_rows),
        out_shape=[refined] + logs,
        in_specs=[SMEM]
        + vmem(2 + helpers)
        + [pl.BlockSpec(memory_space=pl.ANY)] * (len(earlier) + len(late)),
        out_specs=vmem(1 + groups),
        scratch_shapes=[pltpu.VMEM(s.shape, s.dtype) for s in scratch]
        + [pltpu.SemaphoreType.DMA((len(earlier) + len(late),))],
        compiler_params=params(*start, *state, *scratch, refined, *logs),
        cost_estimate=COST,
        name="rounds",
    )(helper, *start, sums, mass, *earlier, *late)

    back = [across(logs[g], g) for g in range(groups)]
    out = jax.ShapeDtypeStruct((count, subs), F32)
    log_resp = pl.pallas_call(
        functools.partial(unpack_kernel, depth, owners),
        out_shape=out,
        in_specs=[SMEM] + vmem(1 + groups),
        out_specs=pl.BlockSpec(memory_space=pltpu.VMEM),
        compiler_params=params(*back, out),
        cost_estimate=COST,
        name="unpack",
    )(me, cluster, *back)
    return (refined[None], log_resp)


def solution(mesh):
    in_specs = (
        P(("grp", "own", "hlp"), None),
        P(("grp", "own", "hlp")),
        P(("grp", "own"), "hlp", None),
    )
    out_specs = (P(("grp", "own"), "hlp", None), P(("grp", "own", "hlp"), None))
    return jax.shard_map(
        per_device, mesh=mesh, in_specs=in_specs, out_specs=out_specs, check_vma=False
    )
```

time: 84.2 us -> 69.1 us (0.82)
  Pallas kernels: 26.1 us -> 11.2 us
  other arithmetic: 1.97 us -> 0 us
  local copies, waits for them, and re-layouts: 2.78 us -> 4.18 us
  waiting for transfers between devices: 33.3 us -> 34.5 us
    pallas_call x5 -> x3, Pallas kernels: 23.8 us -> 9.86 us  [the longest x1 7.39 us: per_device(): pl.pallas_call(functools.partial(last_kernel, helpers, (len(earlier), len...]
    concatenate x1 -> x0, other arithmetic: 1.97 us -> none  [per_device(): start = jnp.concatenate(spread(subcentroids[0]), axis=0)]
    unnamed x40 -> x14, local copies, waits for them, and re-layouts: 2.78 us -> 4.18 us
    ppermute x21, waiting for transfers between devices: 33.3 us -> 34.5 us  [hop(): return lambda x: lax.ppermute(x, axis, pairs)]
    pallas_call x1, Pallas kernels: 2.32 us -> 1.31 us  [per_device(): pl.pallas_call(functools.partial(unpack_kernel, depth, owners), out_shape...]
  transfers between devices with their start and end apart: 21 -> 21, of which waited for: 8 -> 7; matrix products, arithmetic and copies ran while one was open for 2% -> 0% of each run, Pallas kernels for 16% -> 3%
where the time goes in v2:
time: 69.1 us; the launch traced here: 68.9 us
  waiting for transfers between devices  34.5 us (50%)
  starting transfers between devices  18.3 us (26%)
  Pallas kernels  11.2 us (16%)
  local copies, waits for them, and re-layouts  4.18 us (6%)
  between operations  0.72 us (1%)
    ppermute x21, waiting for transfers between devices, hop(): return lambda x: lax.ppermute(x, axis, pairs)  34.5 us
    ppermute x21, starting transfers between devices, hop(): return lambda x: lax.ppermute(x, axis, pairs)  18.3 us
    pallas_call x1, Pallas kernels, per_device(): pl.pallas_call(functools.partial(last_kernel, helpers, (len(earlier), len...  7.39 us
    unnamed x14, local copies, waits for them, and re-layouts  4.18 us
    pallas_call x1, Pallas kernels, per_device(): pl.pallas_call(functools.partial(first_kernel, helpers), out_shape=state,...  1.88 us
  transfers between devices with their start and end apart: 21, of which 7 were waited for; matrix products, arithmetic and copies ran while one was open for 0% of the time, Pallas kernels for 3%

profile of v2, /device:TPU:0, one launch (start us, length us, event | category | flops | bytes accessed | tf_op | source)
XLA Modules:
  0.0 68.9 jit_solution(2977870691773605710)
XLA Ops:
  0.6 0.0 copy-start.6
  0.6 0.7 copy-done.6
  1.3 0.0 copy-start.3
  1.3 1.0 %copy-done.3 = bf16[256,1024]{1,0:T(8,128)(2,1)S(1)} copy-done((bf16[256,1024]{1,0:T(8,128)(2,1)S(1)}, bf16[256,1024]{1,0:T(8,128)(2,1)}, u32[]{:S(2)}) %copy-start.3) | copy-done | bytes 524312
  2.4 0.0 copy-start
  2.4 0.6 pack.1
  3.0 3.1 %collective-permute-start.6 = (bf16[128,1024]{1,0:T(8,128)(2,1)S(1)}, bf16[128,1024]{1,0:T(8,128)(2,1)S(1)}, u32[]{:S(2)}, u32[]{:S(2)}) collective-permute-start(bf16[128,1024]{1,0:T(8,128)(2,1)S(1)} %get-tuple-element.17), channel_id=1, source_target_pairs={{0,4},{4,0},{8,12},{12,8},{1,5},{5,1},{9,13},{13,9},{2,6},{6,2},{1... | collective-permute-start | bytes 786440 | tf_op jit(solution)/shard_map/ppermute | solution.py:212
  6.1 1.5 %collective-permute-start = (bf16[128,1024]{1,0:T(8,128)(2,1)S(1)}, bf16[128,1024]{1,0:T(8,128)(2,1)S(1)}, u32[]{:S(2)}, u32[]{:S(2)}) collective-permute-start(bf16[128,1024]{1,0:T(8,128)(2,1)S(1)} %get-tuple-element.15.refs_4_.refs_6_), channel_id=1, source_target_pairs={{0,2},{1,3},{2,0},{3,1},{4,6},{5,7},{6,4},{7,5},{8,10},{9,11},{10,... | collective-permute-start | bytes 786440 | tf_op jit(solution)/shard_map/ppermute | solution.py:212
  7.5 2.6 %collective-permute-start.10 = (bf16[128,1024]{1,0:T(8,128)(2,1)S(1)}, bf16[128,1024]{1,0:T(8,128)(2,1)}, u32[]{:S(2)}, u32[]{:S(2)}) collective-permute-start(bf16[128,1024]{1,0:T(8,128)(2,1)S(1)} %get-tuple-element.20), channel_id=1, source_target_pairs={{0,8},{4,12},{8,0},{12,4},{1,9},{5,13},{9,1},{13,5},{2,10},{6,14},... | collective-permute-start | bytes 786440 | tf_op jit(solution)/shard_map/ppermute | solution.py:212
  10.1 0.2 collective-permute-start.14
  10.4 0.0 collective-permute-start.4
  10.4 6.1 %collective-permute-done.6.refs_8_.refs_10_ = bf16[128,1024]{1,0:T(8,128)(2,1)S(1)} collective-permute-done((bf16[128,1024]{1,0:T(8,128)(2,1)S(1)}, bf16[128,1024]{1,0:T(8,128)(2,1)S(1)}, u32[]{:S(2)}, u32[]{:S(2)}) %collective-permute-start.6) | collective-permute-done | bytes 262176 | tf_op jit(solution)/shard_map/ppermute | solution.py:212
  16.4 2.1 %collective-permute-start.8 = (bf16[128,1024]{1,0:T(8,128)(2,1)S(1)}, bf16[128,1024]{1,0:T(8,128)(2,1)S(1)}, u32[]{:S(2)}, u32[]{:S(2)}) collective-permute-start(bf16[128,1024]{1,0:T(8,128)(2,1)S(1)} %collective-permute-done.6.refs_8_.refs_10_), channel_id=1, source_target_pairs={{0,2},{1,3},{2,0},{3,1},{4,6},{5,7},{6,4},{7,5},{8,10},{9,11},{10,... | collective-permute-start | bytes 786440 | tf_op jit(solution)/shard_map/ppermute | solution.py:212
  18.6 0.0 collective-permute-done.refs_6_.refs_8_
  18.6 0.0 collective-permute-start.7
  18.6 10.4 %collective-permute-done.10.refs_14_ = bf16[128,1024]{1,0:T(8,128)(2,1)} collective-permute-done((bf16[128,1024]{1,0:T(8,128)(2,1)S(1)}, bf16[128,1024]{1,0:T(8,128)(2,1)}, u32[]{:S(2)}, u32[]{:S(2)}) %collective-permute-start.10) | collective-permute-done | bytes 262176 | tf_op jit(solution)/shard_map/ppermute | solution.py:212
  29.0 0.0 copy-done
  29.0 0.5 collective-permute-start.2
  29.6 0.0 collective-permute-done.14.refs_18_
  29.6 0.0 collective-permute-start.1
  29.6 0.0 collective-permute-done.4.refs_5_.refs_7_
  29.6 1.6 %collective-permute-start.12 = (bf16[128,1024]{1,0:T(8,128)(2,1)}, bf16[128,1024]{1,0:T(8,128)(2,1)}, u32[]{:S(2)}, u32[]{:S(2)}) collective-permute-start(bf16[128,1024]{1,0:T(8,128)(2,1)} %collective-permute-done.10.refs_14_), channel_id=1, source_target_pairs={{0,2},{1,3},{2,0},{3,1},{4,6},{5,7},{6,4},{7,5},{8,10},{9,11},{10,... | collective-permute-start | bytes 786440 | tf_op jit(solution)/shard_map/ppermute | solution.py:212
  31.1 4.0 %collective-permute-done.2.refs_2_ = bf16[64,1024]{1,0:T(8,128)(2,1)S(1)} collective-permute-done((bf16[64,1024]{1,0:T(8,128)(2,1)S(1)}, bf16[64,1024]{1,0:T(8,128)(2,1)S(1)}, u32[]{:S(2)}, u32[]{:S(2)}) %collective-permute-start.2) | collective-permute-done | bytes 131104 | tf_op jit(solution)/shard_map/ppermute | solution.py:212
  35.1 0.0 collective-permute-start.5
  35.1 0.0 collective-permute-done.8.refs_10_.refs_12_
  35.1 0.5 collective-permute-start.9
  35.6 0.0 collective-permute-done.1.refs_1_
  35.6 0.0 collective-permute-start.16
  35.6 0.0 collective-permute-done.7.refs_9_.refs_11_
  35.6 0.2 collective-permute-start.3
  35.8 5.0 %collective-permute-done.12.refs_16_ = bf16[128,1024]{1,0:T(8,128)(2,1)} collective-permute-done((bf16[128,1024]{1,0:T(8,128)(2,1)}, bf16[128,1024]{1,0:T(8,128)(2,1)}, u32[]{:S(2)}, u32[]{:S(2)}) %collective-permute-start.12) | collective-permute-done | bytes 262176 | tf_op jit(solution)/shard_map/ppermute | solution.py:212
  40.8 0.0 collective-permute-start.11
  40.8 0.0 collective-permute-done.3.refs_3_
  40.8 0.0 copy-start.1
  40.8 0.5 collective-permute-start.15
  41.3 0.0 collective-permute-done.5.refs_7_.refs_9_
  41.3 0.1 collective-permute-start.13
  41.4 0.0 collective-permute-done.9.refs_11_.refs_13_
  41.4 1.9 %first_rows.1 = (f32[256,1024]{1,0:T(8,128)S(1)}, f32[256,128]{1,0:T(8,128)S(1)}) custom-call(bf16[64,1024]{1,0:T(8,128)(2,1)S(1)} %bitcast.7, bf16[64,1024]{1,0:T(8,128)(2,1)S(1)} %collective-permute-done.1.refs_1_, bf16[64,1024]{1,0:T(8,128)(2,1)S(1)} %collective-permute-done.2.refs_2_, bf16[64,1024]{1,0:T(8,128)(2,1)S(1)} %collective-permute-done.3.refs_3_, ...), custom_call_target="tpu_custom_call" | custom-call | flops 1 | bytes 1 | tf_op jit(solution)/shard_map/first_rows/pallas_call | solution.py:262
  43.3 0.0 copy-done.1
  43.3 0.0 copy-start.4
  43.3 0.6 copy-done.4
  44.0 1.4 %collective-permute-done.16.refs_20_ = bf16[128,1024]{1,0:T(8,128)(2,1)} collective-permute-done((bf16[128,1024]{1,0:T(8,128)(2,1)}, bf16[128,1024]{1,0:T(8,128)(2,1)}, u32[]{:S(2)}, u32[]{:S(2)}) %collective-permute-start.16) | collective-permute-done | bytes 262176 | tf_op jit(solution)/shard_map/ppermute | solution.py:212
  45.3 0.0 collective-permute-start.17
  45.3 0.0 collective-permute-done.11.refs_15_
  45.3 0.0 collective-permute-done.15.refs_19_
  45.3 0.0 collective-permute-done.13.refs_17_
  45.4 1.9 %collective-permute-done.17.refs_21_ = bf16[128,1024]{1,0:T(8,128)(2,1)} collective-permute-done((bf16[128,1024]{1,0:T(8,128)(2,1)}, bf16[128,1024]{1,0:T(8,128)(2,1)}, u32[]{:S(2)}, u32[]{:S(2)}) %collective-permute-start.17) | collective-permute-done | bytes 262176 | tf_op jit(solution)/shard_map/ppermute | solution.py:212
  47.2 0.0 copy-start.2
  47.2 0.9 %copy-done.2 = bf16[64,1024]{1,0:T(8,128)(2,1)S(1)} copy-done((bf16[64,1024]{1,0:T(8,128)(2,1)S(1)}, bf16[64,1024]{1,0:T(8,128)(2,1)}, u32[]{:S(2)}) %copy-start.2) | copy-done | bytes 131096
  48.1 0.0 copy-start.5
  48.1 0.9 %copy-done.5 = f32[256,128]{1,0:T(8,128)S(1)} copy-done((f32[256,128]{1,0:T(8,128)S(1)}, f32[256,128]{1,0:T(8,128)}, u32[]{:S(2)}) %copy-start.5) | copy-done | bytes 131096
  49.0 7.4 %rounds.1 = (f32[64,1024]{1,0:T(8,128)}, bf16[128,256]{1,0:T(8,128)(2,1)S(1)}, bf16[128,256]{1,0:T(8,128)(2,1)S(1)}, bf16[128,256]{1,0:T(8,128)(2,1)S(1)}, bf16[128,256]{1,0:T(8,128)(2,1)S(1)}) custom-call(s32[1]{0:T(128)} %bitcast.helper_ref, bf16[64,1024]{1,0:T(8,128)(2,1)S(1)} %bitcast.8, bf16[64,1024]{1,0:T(8,128)(2,1)S(1)} %collective-permute-done.1.refs_1_, ...), custom_call_target="tpu_custom_call" | custom-call | flops 1 | bytes 1 | tf_op jit(solution)/shard_map/rounds/pallas_call | solution.py:282
  56.4 2.9 %collective-permute-start.18 = (bf16[128,256]{1,0:T(8,128)(2,1)S(1)}, bf16[128,256]{1,0:T(8,128)(2,1)S(1)}, u32[]{:S(2)}, u32[]{:S(2)}) collective-permute-start(bf16[128,256]{1,0:T(8,128)(2,1)S(1)} %get-tuple-element.25), channel_id=1, source_target_pairs={{0,4},{4,0},{8,12},{12,8},{1,5},{5,1},{9,13},{13,9},{2,6},{6,2},{1... | collective-permute-start | bytes 196616 | tf_op jit(solution)/shard_map/ppermute | solution.py:212
  59.3 1.1 %collective-permute-start.19 = (bf16[128,256]{1,0:T(8,128)(2,1)S(1)}, bf16[128,256]{1,0:T(8,128)(2,1)S(1)}, u32[]{:S(2)}, u32[]{:S(2)}) collective-permute-start(bf16[128,256]{1,0:T(8,128)(2,1)S(1)} %get-tuple-element.26), channel_id=1, source_target_pairs={{0,8},{4,12},{8,0},{12,4},{1,9},{5,13},{9,1},{13,5},{2,10},{6,14},... | collective-permute-start | bytes 196616 | tf_op jit(solution)/shard_map/ppermute | solution.py:212
  60.4 1.4 %collective-permute-start.20 = (bf16[128,256]{1,0:T(8,128)(2,1)S(1)}, bf16[128,256]{1,0:T(8,128)(2,1)S(1)}, u32[]{:S(2)}, u32[]{:S(2)}) collective-permute-start(bf16[128,256]{1,0:T(8,128)(2,1)S(1)} %get-tuple-element.27), channel_id=1, source_target_pairs={{0,12},{4,8},{8,4},{12,0},{1,13},{5,9},{9,5},{13,1},{2,14},{6,10},... | collective-permute-start | bytes 196616 | tf_op jit(solution)/shard_map/ppermute | solution.py:212
  61.8 0.0 collective-permute-done.18.refs_1_
  61.8 5.7 %collective-permute-done.19.refs_2_ = bf16[128,256]{1,0:T(8,128)(2,1)S(1)} collective-permute-done((bf16[128,256]{1,0:T(8,128)(2,1)S(1)}, bf16[128,256]{1,0:T(8,128)(2,1)S(1)}, u32[]{:S(2)}, u32[]{:S(2)}) %collective-permute-start.19) | collective-permute-done | bytes 65568 | tf_op jit(solution)/shard_map/ppermute | solution.py:212
  67.6 0.0 collective-permute-done.20.refs_3_
  67.6 1.3 %unpack.1 = f32[256,256]{1,0:T(8,128)} custom-call(s32[1]{0:T(128)} %bitcast.2.me_ref, s32[1,256]{1,0:T(1,128)S(1)} %bitcast.10, bf16[128,256]{1,0:T(8,128)(2,1)S(1)} %get-tuple-element.24.refs_0_, bf16[128,256]{1,0:T(8,128)(2,1)S(1)} %collective-permute-done.18.refs_1_, bf16[128,256]{1,0:T(8,128)(2,1)S(1)} %collective-permute-done.19.refs_2_, ...), custom_call_target="tpu_custom_call" | custom-call | flops 1 | bytes 1 | tf_op jit(solution)/shard_map/unpack/pallas_call | solution.py:298
Async XLA Ops:
  0.6 0.7 copy-start.6
  1.3 1.0 %copy-start.3 = (bf16[256,1024]{1,0:T(8,128)(2,1)S(1)}, bf16[256,1024]{1,0:T(8,128)(2,1)}, u32[]{:S(2)}) copy-start(bf16[256,1024]{1,0:T(8,128)(2,1)} %points_ref.1) | copy-start | bytes 1572868
  2.4 26.7 %copy-start = (bf16[1,64,1024]{2,1,0:T(8,128)(2,1)S(1)}, bf16[1,64,1024]{2,1,0:T(8,128)(2,1)}, u32[]{:S(2)}) copy-start(bf16[1,64,1024]{2,1,0:T(8,128)(2,1)} %param.5) | copy-start | bytes 393220
  3.0 13.5 %collective-permute-start.6 = (bf16[128,1024]{1,0:T(8,128)(2,1)S(1)}, bf16[128,1024]{1,0:T(8,128)(2,1)S(1)}, u32[]{:S(2)}, u32[]{:S(2)}) collective-permute-start(bf16[128,1024]{1,0:T(8,128)(2,1)S(1)} %get-tuple-element.17), channel_id=1, source_target_pairs={{0,4},{4,0},{8,12},{12,8},{1,5},{5,1},{9,13},{13,9},{2,6},{6,2},{1... | collective-permute-start | bytes 786440 | tf_op jit(solution)/shard_map/ppermute | solution.py:212
  6.1 12.5 %collective-permute-start = (bf16[128,1024]{1,0:T(8,128)(2,1)S(1)}, bf16[128,1024]{1,0:T(8,128)(2,1)S(1)}, u32[]{:S(2)}, u32[]{:S(2)}) collective-permute-start(bf16[128,1024]{1,0:T(8,128)(2,1)S(1)} %get-tuple-element.15.refs_4_.refs_6_), channel_id=1, source_target_pairs={{0,2},{1,3},{2,0},{3,1},{4,6},{5,7},{6,4},{7,5},{8,10},{9,11},{10,... | collective-permute-start | bytes 786440 | tf_op jit(solution)/shard_map/ppermute | solution.py:212
  7.5 21.5 %collective-permute-start.10 = (bf16[128,1024]{1,0:T(8,128)(2,1)S(1)}, bf16[128,1024]{1,0:T(8,128)(2,1)}, u32[]{:S(2)}, u32[]{:S(2)}) collective-permute-start(bf16[128,1024]{1,0:T(8,128)(2,1)S(1)} %get-tuple-element.20), channel_id=1, source_target_pairs={{0,8},{4,12},{8,0},{12,4},{1,9},{5,13},{9,1},{13,5},{2,10},{6,14},... | collective-permute-start | bytes 786440 | tf_op jit(solution)/shard_map/ppermute | solution.py:212
  10.1 19.4 %collective-permute-start.14 = (bf16[128,1024]{1,0:T(8,128)(2,1)S(1)}, bf16[128,1024]{1,0:T(8,128)(2,1)}, u32[]{:S(2)}, u32[]{:S(2)}) collective-permute-start(bf16[128,1024]{1,0:T(8,128)(2,1)S(1)} %get-tuple-element.21), channel_id=1, source_target_pairs={{0,12},{4,8},{8,4},{12,0},{1,13},{5,9},{9,5},{13,1},{2,14},{6,10},... | collective-permute-start | bytes 786440 | tf_op jit(solution)/shard_map/ppermute | solution.py:212
  10.4 19.2 %collective-permute-start.4 = (bf16[128,1024]{1,0:T(8,128)(2,1)S(1)}, bf16[128,1024]{1,0:T(8,128)(2,1)S(1)}, u32[]{:S(2)}, u32[]{:S(2)}) collective-permute-start(bf16[128,1024]{1,0:T(8,128)(2,1)S(1)} %get-tuple-element.15.refs_4_.refs_6_), channel_id=1, source_target_pairs={{0,1},{1,0},{2,3},{3,2},{4,5},{5,4},{6,7},{7,6},{8,9},{9,8},{10,11... | collective-permute-start | bytes 786440 | tf_op jit(solution)/shard_map/ppermute | solution.py:212
  16.4 18.7 %collective-permute-start.8 = (bf16[128,1024]{1,0:T(8,128)(2,1)S(1)}, bf16[128,1024]{1,0:T(8,128)(2,1)S(1)}, u32[]{:S(2)}, u32[]{:S(2)}) collective-permute-start(bf16[128,1024]{1,0:T(8,128)(2,1)S(1)} %collective-permute-done.6.refs_8_.refs_10_), channel_id=1, source_target_pairs={{0,2},{1,3},{2,0},{3,1},{4,6},{5,7},{6,4},{7,5},{8,10},{9,11},{10,... | collective-permute-start | bytes 786440 | tf_op jit(solution)/shard_map/ppermute | solution.py:212
  18.6 17.0 %collective-permute-start.7 = (bf16[128,1024]{1,0:T(8,128)(2,1)S(1)}, bf16[128,1024]{1,0:T(8,128)(2,1)S(1)}, u32[]{:S(2)}, u32[]{:S(2)}) collective-permute-start(bf16[128,1024]{1,0:T(8,128)(2,1)S(1)} %collective-permute-done.6.refs_8_.refs_10_), channel_id=1, source_target_pairs={{0,1},{1,0},{2,3},{3,2},{4,5},{5,4},{6,7},{7,6},{8,9},{9,8},{10,11... | collective-permute-start | bytes 786440 | tf_op jit(solution)/shard_map/ppermute | solution.py:212
  29.0 6.1 %collective-permute-start.2 = (bf16[64,1024]{1,0:T(8,128)(2,1)S(1)}, bf16[64,1024]{1,0:T(8,128)(2,1)S(1)}, u32[]{:S(2)}, u32[]{:S(2)}) collective-permute-start(bf16[64,1024]{1,0:T(8,128)(2,1)S(1)} %bitcast.5), channel_id=1, source_target_pairs={{0,2},{1,3},{2,0},{3,1},{4,6},{5,7},{6,4},{7,5},{8,10},{9,11},{10,... | collective-permute-start | bytes 393224 | tf_op jit(solution)/shard_map/ppermute | solution.py:212
  29.6 6.0 %collective-permute-start.1 = (bf16[64,1024]{1,0:T(8,128)(2,1)S(1)}, bf16[64,1024]{1,0:T(8,128)(2,1)S(1)}, u32[]{:S(2)}, u32[]{:S(2)}) collective-permute-start(bf16[64,1024]{1,0:T(8,128)(2,1)S(1)} %bitcast.6), channel_id=1, source_target_pairs={{0,1},{1,0},{2,3},{3,2},{4,5},{5,4},{6,7},{7,6},{8,9},{9,8},{10,11... | collective-permute-start | bytes 393224 | tf_op jit(solution)/shard_map/ppermute | solution.py:212
  29.6 11.2 %collective-permute-start.12 = (bf16[128,1024]{1,0:T(8,128)(2,1)}, bf16[128,1024]{1,0:T(8,128)(2,1)}, u32[]{:S(2)}, u32[]{:S(2)}) collective-permute-start(bf16[128,1024]{1,0:T(8,128)(2,1)} %collective-permute-done.10.refs_14_), channel_id=1, source_target_pairs={{0,2},{1,3},{2,0},{3,1},{4,6},{5,7},{6,4},{7,5},{8,10},{9,11},{10,... | collective-permute-start | bytes 786440 | tf_op jit(solution)/shard_map/ppermute | solution.py:212
  35.1 6.2 %collective-permute-start.5 = (bf16[128,1024]{1,0:T(8,128)(2,1)S(1)}, bf16[128,1024]{1,0:T(8,128)(2,1)S(1)}, u32[]{:S(2)}, u32[]{:S(2)}) collective-permute-start(bf16[128,1024]{1,0:T(8,128)(2,1)S(1)} %collective-permute-done.refs_6_.refs_8_), channel_id=1, source_target_pairs={{0,1},{1,0},{2,3},{3,2},{4,5},{5,4},{6,7},{7,6},{8,9},{9,8},{10,11... | collective-permute-start | bytes 786440 | tf_op jit(solution)/shard_map/ppermute | solution.py:212
  35.1 6.3 %collective-permute-start.9 = (bf16[128,1024]{1,0:T(8,128)(2,1)S(1)}, bf16[128,1024]{1,0:T(8,128)(2,1)S(1)}, u32[]{:S(2)}, u32[]{:S(2)}) collective-permute-start(bf16[128,1024]{1,0:T(8,128)(2,1)S(1)} %collective-permute-done.8.refs_10_.refs_12_), channel_id=1, source_target_pairs={{0,1},{1,0},{2,3},{3,2},{4,5},{5,4},{6,7},{7,6},{8,9},{9,8},{10,11... | collective-permute-start | bytes 786440 | tf_op jit(solution)/shard_map/ppermute | solution.py:212
  35.6 9.7 %collective-permute-start.16 = (bf16[128,1024]{1,0:T(8,128)(2,1)}, bf16[128,1024]{1,0:T(8,128)(2,1)}, u32[]{:S(2)}, u32[]{:S(2)}) collective-permute-start(bf16[128,1024]{1,0:T(8,128)(2,1)} %collective-permute-done.14.refs_18_), channel_id=1, source_target_pairs={{0,2},{1,3},{2,0},{3,1},{4,6},{5,7},{6,4},{7,5},{8,10},{9,11},{10,... | collective-permute-start | bytes 786440 | tf_op jit(solution)/shard_map/ppermute | solution.py:212
  35.6 5.2 %collective-permute-start.3 = (bf16[64,1024]{1,0:T(8,128)(2,1)S(1)}, bf16[64,1024]{1,0:T(8,128)(2,1)S(1)}, u32[]{:S(2)}, u32[]{:S(2)}) collective-permute-start(bf16[64,1024]{1,0:T(8,128)(2,1)S(1)} %collective-permute-done.2.refs_2_), channel_id=1, source_target_pairs={{0,1},{1,0},{2,3},{3,2},{4,5},{5,4},{6,7},{7,6},{8,9},{9,8},{10,11... | collective-permute-start | bytes 393224 | tf_op jit(solution)/shard_map/ppermute | solution.py:212
  40.8 4.5 %collective-permute-start.11 = (bf16[128,1024]{1,0:T(8,128)(2,1)}, bf16[128,1024]{1,0:T(8,128)(2,1)}, u32[]{:S(2)}, u32[]{:S(2)}) collective-permute-start(bf16[128,1024]{1,0:T(8,128)(2,1)} %collective-permute-done.10.refs_14_), channel_id=1, source_target_pairs={{0,1},{1,0},{2,3},{3,2},{4,5},{5,4},{6,7},{7,6},{8,9},{9,8},{10,11... | collective-permute-start | bytes 786440 | tf_op jit(solution)/shard_map/ppermute | solution.py:212
  40.8 2.5 %copy-start.1 = (bf16[64,1024]{1,0:T(8,128)(2,1)}, bf16[64,1024]{1,0:T(8,128)(2,1)S(1)}, u32[]{:S(2)}) copy-start(bf16[64,1024]{1,0:T(8,128)(2,1)S(1)} %collective-permute-done.3.refs_3_) | copy-start | bytes 393220
  40.8 4.5 %collective-permute-start.15 = (bf16[128,1024]{1,0:T(8,128)(2,1)}, bf16[128,1024]{1,0:T(8,128)(2,1)}, u32[]{:S(2)}, u32[]{:S(2)}) collective-permute-start(bf16[128,1024]{1,0:T(8,128)(2,1)} %collective-permute-done.14.refs_18_), channel_id=1, source_target_pairs={{0,1},{1,0},{2,3},{3,2},{4,5},{5,4},{6,7},{7,6},{8,9},{9,8},{10,11... | collective-permute-start | bytes 786440 | tf_op jit(solution)/shard_map/ppermute | solution.py:212
  41.3 4.0 %collective-permute-start.13 = (bf16[128,1024]{1,0:T(8,128)(2,1)}, bf16[128,1024]{1,0:T(8,128)(2,1)}, u32[]{:S(2)}, u32[]{:S(2)}) collective-permute-start(bf16[128,1024]{1,0:T(8,128)(2,1)} %collective-permute-done.12.refs_16_), channel_id=1, source_target_pairs={{0,1},{1,0},{2,3},{3,2},{4,5},{5,4},{6,7},{7,6},{8,9},{9,8},{10,11... | collective-permute-start | bytes 786440 | tf_op jit(solution)/shard_map/ppermute | solution.py:212
  43.3 0.7 copy-start.4
  45.3 1.9 %collective-permute-start.17 = (bf16[128,1024]{1,0:T(8,128)(2,1)}, bf16[128,1024]{1,0:T(8,128)(2,1)}, u32[]{:S(2)}, u32[]{:S(2)}) collective-permute-start(bf16[128,1024]{1,0:T(8,128)(2,1)} %collective-permute-done.16.refs_20_), channel_id=1, source_target_pairs={{0,1},{1,0},{2,3},{3,2},{4,5},{5,4},{6,7},{7,6},{8,9},{9,8},{10,11... | collective-permute-start | bytes 786440 | tf_op jit(solution)/shard_map/ppermute | solution.py:212
  47.2 0.9 %copy-start.2 = (bf16[64,1024]{1,0:T(8,128)(2,1)S(1)}, bf16[64,1024]{1,0:T(8,128)(2,1)}, u32[]{:S(2)}) copy-start(bf16[64,1024]{1,0:T(8,128)(2,1)} %copy-done.1) | copy-start | bytes 393220
  48.1 0.9 %copy-start.5 = (f32[256,128]{1,0:T(8,128)S(1)}, f32[256,128]{1,0:T(8,128)}, u32[]{:S(2)}) copy-start(f32[256,128]{1,0:T(8,128)} %copy-done.4) | copy-start | bytes 393220
  56.4 5.4 %collective-permute-start.18 = (bf16[128,256]{1,0:T(8,128)(2,1)S(1)}, bf16[128,256]{1,0:T(8,128)(2,1)S(1)}, u32[]{:S(2)}, u32[]{:S(2)}) collective-permute-start(bf16[128,256]{1,0:T(8,128)(2,1)S(1)} %get-tuple-element.25), channel_id=1, source_target_pairs={{0,4},{4,0},{8,12},{12,8},{1,5},{5,1},{9,13},{13,9},{2,6},{6,2},{1... | collective-permute-start | bytes 196616 | tf_op jit(solution)/shard_map/ppermute | solution.py:212
  59.3 8.2 %collective-permute-start.19 = (bf16[128,256]{1,0:T(8,128)(2,1)S(1)}, bf16[128,256]{1,0:T(8,128)(2,1)S(1)}, u32[]{:S(2)}, u32[]{:S(2)}) collective-permute-start(bf16[128,256]{1,0:T(8,128)(2,1)S(1)} %get-tuple-element.26), channel_id=1, source_target_pairs={{0,8},{4,12},{8,0},{12,4},{1,9},{5,13},{9,1},{13,5},{2,10},{6,14},... | collective-permute-start | bytes 196616 | tf_op jit(solution)/shard_map/ppermute | solution.py:212
  60.4 7.1 %collective-permute-start.20 = (bf16[128,256]{1,0:T(8,128)(2,1)S(1)}, bf16[128,256]{1,0:T(8,128)(2,1)S(1)}, u32[]{:S(2)}, u32[]{:S(2)}) collective-permute-start(bf16[128,256]{1,0:T(8,128)(2,1)S(1)} %get-tuple-element.27), channel_id=1, source_target_pairs={{0,12},{4,8},{8,4},{12,0},{1,13},{5,9},{9,5},{13,1},{2,14},{6,10},... | collective-permute-start | bytes 196616 | tf_op jit(solution)/shard_map/ppermute | solution.py:212

commit v3 on v2

v3 whole, which is shorter than its diff:
```python
import functools
import math

import jax
import jax.numpy as jnp
from jax import lax
from jax.experimental import pallas as pl
from jax.experimental.pallas import tpu as pltpu
from jax.sharding import PartitionSpec as P

ITERS = 2
GROUPS = 4
TILE = 256

smoothing_factor = 16.0
prior_count = 1.0

EMPTY = 64.0
LIMIT = 32.0

BF = jnp.bfloat16
F32 = jnp.float32
TN = (((0,), (0,)), ((), ()))
NN = (((1,), (0,)), ((), ()))


def matmul(a, b, dims):
    return lax.dot_general(a, b, dims, preferred_element_type=F32)


def slots_of(me, cluster, depth, owners):
    count = cluster.shape[1]
    height = max(16, owners)
    offset = jnp.bitwise_xor(cluster, me)
    member = lax.broadcasted_iota(jnp.int32, (height, count), 0) == offset
    earlier = lax.broadcasted_iota(jnp.int32, (count, count), 0) < lax.broadcasted_iota(
        jnp.int32, (count, count), 1
    )
    member = jnp.where(member, 1.0, 0.0)
    before = matmul(member.astype(BF), jnp.where(earlier, 1.0, 0.0).astype(BF), NN)
    rank = jnp.sum(before * member, axis=0, keepdims=True).astype(jnp.int32)
    return offset * depth + rank, jnp.sum(member, axis=1, keepdims=True)


def fetch(refs, target, arrived):
    height = refs[0].shape[0]
    copies = [
        pltpu.make_async_copy(ref, target.at[i * height : (i + 1) * height], arrived.at[i])
        for i, ref in enumerate(refs)
    ]
    for copy in copies:
        copy.start()
    return copies


def settle(copies):
    for copy in copies:
        copy.wait()


def pack_kernel(depth, owners, me_ref, cluster_hbm, points_hbm, centres_hbm, *refs):
    *outs, cluster_ref, points_ref, arrived = refs
    names = pltpu.make_async_copy(cluster_hbm, cluster_ref, arrived.at[1])
    names.start()
    points = fetch([points_hbm], points_ref, arrived)
    height = outs[-1].shape[0]
    centres = fetch([centres_hbm], outs[0].at[height:], arrived.at[2:])
    names.wait()
    slot, tally = slots_of(me_ref[0], cluster_ref[...], depth, owners)
    settle(points)
    points = points_ref[...]
    per = height // depth
    for g, out in enumerate(outs):
        rows = lax.broadcasted_iota(jnp.int32, (height, points.shape[0]), 0) + g * height
        pick = jnp.where(rows == slot, 1.0, 0.0).astype(BF)
        block = matmul(pick, points, NN)
        for j in range(per):
            held = tally[g * per + j : g * per + j + 1, :].astype(jnp.int32)
            local = lax.broadcasted_iota(jnp.int32, (depth, 1), 0)
            part = block[j * depth : (j + 1) * depth]
            out[j * depth : (j + 1) * depth, :] = jnp.where(local < held, part, EMPTY).astype(BF)
    settle(centres)


def unpack_kernel(depth, owners, me_ref, cluster_ref, *refs):
    *logs, out = refs
    slot, _ = slots_of(me_ref[0], cluster_ref[...], depth, owners)
    count = slot.shape[1]
    column = jnp.broadcast_to(slot.astype(F32), (128, count)).T[:, 0:1].astype(jnp.int32)
    height = logs[0].shape[0]
    total = None
    for g, block in enumerate(logs):
        lanes = lax.broadcasted_iota(jnp.int32, (count, height), 1) + g * height
        pick = jnp.where(lanes == column, 1.0, 0.0).astype(BF)
        term = matmul(pick, block[...], NN)
        total = term if total is None else total + term
    out[...] = total


def square_norms(centres):
    wide = centres.astype(F32)
    column = jnp.sum(wide * wide, axis=1, keepdims=True)
    return jnp.broadcast_to(column, (column.shape[0], 128)).T[0:1]


def joined(parts):
    return parts[0] if len(parts) == 1 else jnp.concatenate(parts, axis=0)


def energies(turned, norms, rows):
    return matmul(rows, turned, NN) * (2.0 / smoothing_factor) - norms * (1.0 / smoothing_factor)


def accumulate(turned, norms, tiles, share_ref, state_ref, fresh):
    start = 0
    for rows in tiles:
        logits = energies(turned, norms, rows)
        top = jnp.max(logits, axis=1, keepdims=True)
        weight = jnp.exp(logits - top)
        live = jnp.where(rows[:, 0:1].astype(F32) < LIMIT, 1.0, 0.0)
        scale = live / jnp.sum(weight, axis=1, keepdims=True)
        share_ref[start : start + rows.shape[0], :] = (weight * scale).astype(BF)
        start += rows.shape[0]
    width = state_ref.shape[1] - 128
    start = 0
    for i, rows in enumerate(tiles):
        share = share_ref[start : start + rows.shape[0], :]
        mass = matmul(share, jnp.ones((rows.shape[0], 128), BF), TN)
        part = matmul(share, rows, TN)
        if fresh and i == 0:
            state_ref[:, width:] = mass
            state_ref[:, :width] = part
        else:
            state_ref[:, width:] += mass
            state_ref[:, :width] += part
        start += rows.shape[0]


def tiles_of(rows, first, last):
    return [rows[r : r + TILE, :] for r in range(first, last, TILE)]


def some_kernel(helpers, height, *refs):
    *given, out, state_ref, centres_ref, share_ref, rows, arrived, ready, kept = refs
    centres = fetch([ref.at[height:] for ref in given[:helpers]], centres_ref, ready)
    copies = fetch([ref.at[:height] for ref in given], rows, arrived)
    settle(centres)
    centres = centres_ref[...]
    norms = square_norms(centres)
    turned = centres.T
    settle(copies)
    accumulate(turned, norms, tiles_of(rows, 0, rows.shape[0]), share_ref, state_ref, True)
    settle(fetch([state_ref], out, kept))


def refine(centres, state_ref):
    width = centres.shape[1]
    mass = state_ref[:, width : width + 1]
    return (state_ref[:, :width] + prior_count * centres.astype(F32)) / (mass + prior_count)


def last_kernel(helpers, counts, share_rows, helper_ref, *refs):
    earlier, late, own = counts
    old, refs = refs[:1], refs[1:]
    given, refs = refs[: earlier + late], refs[earlier + late :]
    refined_ref, logs, refs = refs[0], refs[1 : 1 + own], refs[1 + own :]
    state_ref, ordered, share_ref, rows, arrived, ready, kept = refs
    height = given[-1].shape[0]
    held = earlier * height
    centres = fetch([ref.at[height:] for ref in given[:helpers]], ordered, ready)
    given = [ref.at[:height] for ref in given]
    later = fetch(given[earlier:], rows.at[held:], arrived.at[earlier:])
    sooner = fetch(given[:earlier], rows, arrived)
    state = fetch(old, state_ref, kept)
    helper = helper_ref[0]
    settle(centres)
    centres = ordered[...]
    norms = square_norms(centres)
    turned = centres.T
    settle(later + state)
    accumulate(turned, norms, tiles_of(rows, held, rows.shape[0]), share_ref, state_ref, False)
    settle(sooner)
    for turn in range(1, ITERS):
        centres = refine(centres, state_ref).astype(BF)
        norms = square_norms(centres)
        turned = centres.T
        accumulate(turned, norms, tiles_of(rows, 0, rows.shape[0]), share_ref, state_ref, True)
    refined = refine(centres, state_ref)
    refined_ref[...] = refined[0:share_rows]
    centres = refined.astype(BF)
    for j in range(helpers):
        place = pl.multiple_of(jnp.bitwise_xor(helper, j) * share_rows, share_rows)
        ordered[pl.ds(place, share_rows), :] = centres[j * share_rows : (j + 1) * share_rows]
    centres = ordered[...]
    norms = square_norms(centres)
    turned = centres.T
    for i, out in enumerate(logs):
        first = i * helpers * height
        logits = energies(turned, norms, rows[first : first + height, :])
        top = jnp.max(logits, axis=1, keepdims=True)
        total = jnp.log(jnp.sum(jnp.exp(logits - top), axis=1, keepdims=True))
        out[...] = (logits - (top + total)).astype(BF)


def vmem(n):
    return [pl.BlockSpec(memory_space=pltpu.VMEM)] * n


SMEM = pl.BlockSpec(memory_space=pltpu.SMEM)
HBM = pl.BlockSpec(memory_space=pltpu.HBM)
COST = pl.CostEstimate(flops=1, bytes_accessed=1, transcendentals=0)


def params(*arrays):
    held = sum(math.prod(a.shape) * a.dtype.itemsize for a in arrays)
    return pltpu.CompilerParams(vmem_limit_bytes=held + 8 * 1024 * 1024)


def in_hbm(value):
    return pltpu.with_memory_space_constraint(value, pltpu.HBM)


def after(value, *others):
    return lax.optimization_barrier((value,) + others)[0]


def hop(axis, size, step):
    pairs = [(i, i ^ step) for i in range(size)]
    return lambda x: lax.ppermute(x, axis, pairs)


def per_device(points, cluster_of, subcentroids):
    count, width = points.shape
    owners = lax.axis_size("own")
    helpers = lax.axis_size("hlp")
    depth = min(count // 2, 4 * count // owners)
    share_rows = subcentroids.shape[1]
    subs = share_rows * helpers
    groups = min(GROUPS, owners)
    per = owners // groups
    height = per * depth

    me = lax.axis_index("own").astype(jnp.int32).reshape(1)
    helper = lax.axis_index("hlp").astype(jnp.int32).reshape(1)
    cluster = cluster_of.reshape(1, count)

    blocks = [jax.ShapeDtypeStruct((height + (0 if g else share_rows), width), BF) for g in range(groups)]
    packed = pl.pallas_call(
        functools.partial(pack_kernel, depth, owners),
        out_shape=blocks,
        in_specs=[SMEM] + [HBM] * 3,
        out_specs=vmem(groups),
        scratch_shapes=[
            pltpu.VMEM(cluster.shape, jnp.int32),
            pltpu.VMEM(points.shape, BF),
            pltpu.SemaphoreType.DMA((3,)),
        ],
        compiler_params=params(points, *blocks),
        cost_estimate=COST,
        name="pack",
    )(me, in_hbm(cluster), in_hbm(points), in_hbm(subcentroids[0]))

    def across(block, g):
        if per == 1:
            return hop("own", owners, g)(block) if g else block
        done = []
        for j in range(per):
            step = g * per + j
            piece = block[j * depth : (j + 1) * depth]
            done.append(hop("own", owners, step)(piece) if step else piece)
        if block.shape[0] > height:
            done.append(block[height:])
        return joined(done)

    def over_chips(block):
        return [block] + [hop("hlp", helpers, step)(block) for step in range(2, helpers, 2)]

    def over_cores(held):
        return [x for block in held for x in (block, hop("hlp", helpers, 1)(block))]

    state = jax.ShapeDtypeStruct((subs, width + 128), F32)
    centre_table = jax.ShapeDtypeStruct((subs, width), BF)

    def scratch(n):
        return [
            state,
            centre_table,
            jax.ShapeDtypeStruct((n * height, subs), BF),
            jax.ShapeDtypeStruct((n * height, width), BF),
        ]

    def semaphores(*counts):
        return [pltpu.SemaphoreType.DMA((n,)) for n in counts]

    beside = hop("hlp", helpers, 1)
    moved = [packed[0]]
    for g in range(1, groups - 1):
        moved.append(across(packed[g], g))
    moved.append(across(after(packed[-1], moved[-1]) if groups > 1 else packed[-1], groups - 1))
    held = [over_chips(block) for block in moved]
    own_beside = beside(after(packed[0], held[0][1]))
    rows = [[moved[0], own_beside] + over_cores(held[0][1:])] + [over_cores(part) for part in held[1:-1]]
    given = [r for part in rows for r in part]
    own = scratch(len(given))
    sofar = pl.pallas_call(
        functools.partial(some_kernel, helpers, height),
        out_shape=state,
        in_specs=[HBM] * len(given),
        out_specs=HBM,
        scratch_shapes=[pltpu.VMEM(s.shape, s.dtype) for s in own] + semaphores(len(given), helpers, 1),
        compiler_params=params(*own),
        cost_estimate=COST,
        name="some_rows",
    )(*given)
    late = over_cores(held[-1][:-1] + [after(held[-1][-1], sofar)])
    earlier = [r for part in rows for r in part]
    logs = [jax.ShapeDtypeStruct((height, subs), BF)] * groups
    refined = jax.ShapeDtypeStruct((share_rows, width), F32)
    own = scratch(len(earlier) + len(late))
    refined, *logs = pl.pallas_call(
        functools.partial(last_kernel, helpers, (len(earlier), len(late), groups), share_rows),
        out_shape=[refined] + logs,
        in_specs=[SMEM] + [HBM] * (1 + len(earlier) + len(late)),
        out_specs=vmem(1 + groups),
        scratch_shapes=[pltpu.VMEM(s.shape, s.dtype) for s in own]
        + semaphores(len(earlier) + len(late), helpers, 1),
        compiler_params=params(*own, refined, *logs),
        cost_estimate=COST,
        name="rounds",
    )(helper, sofar, *[in_hbm(r) for r in earlier + late])

    back = [across(logs[g], g) for g in range(groups)]
    out = jax.ShapeDtypeStruct((count, subs), F32)
    log_resp = pl.pallas_call(
        functools.partial(unpack_kernel, depth, owners),
        out_shape=out,
        in_specs=[SMEM] + vmem(1 + groups),
        out_specs=pl.BlockSpec(memory_space=pltpu.VMEM),
        compiler_params=params(*back, out),
        cost_estimate=COST,
        name="unpack",
    )(me, cluster, *back)
    return (refined[None], log_resp)


def solution(mesh):
    in_specs = (
        P(("grp", "own", "hlp"), None),
        P(("grp", "own", "hlp")),
        P(("grp", "own"), "hlp", None),
    )
    out_specs = (P(("grp", "own"), "hlp", None), P(("grp", "own", "hlp"), None))
    return jax.shard_map(
        per_device, mesh=mesh, in_specs=in_specs, out_specs=out_specs, check_vma=False
    )
```

time: 69.1 us -> 62.6 us (0.906)
  waiting for transfers between devices: 34.5 us -> 25.3 us
  Pallas kernels: 11.2 us -> 15 us
  local copies, waits for them, and re-layouts: 4.18 us -> 0.75 us
  starting transfers between devices: 18.3 us -> 20.6 us
    ppermute x21 -> x18, waiting for transfers between devices: 34.5 us -> 25.3 us  [hop(): return lambda x: lax.ppermute(x, axis, pairs)]
    unnamed x14 -> x28, local copies, waits for them, and re-layouts: 4.18 us -> 0.75 us
    ppermute x21 -> x18, starting transfers between devices: 18.3 us -> 20.6 us  [hop(): return lambda x: lax.ppermute(x, axis, pairs)]
    pallas_call x1, Pallas kernels: 1.88 us -> 3.81 us  [per_device(): pl.pallas_call(functools.partial(some_kernel, helpers, height), out_shape...]
    pallas_call x1, Pallas kernels: 0.6 us -> 1.56 us  [per_device(): pl.pallas_call(functools.partial(pack_kernel, depth, owners), out_shape=b...]
    pallas_call x1, Pallas kernels: 7.39 us -> 8.31 us  [per_device(): pl.pallas_call(functools.partial(last_kernel, helpers, (len(earlier), len...]
  transfers between devices with their start and end apart: 21 -> 18, of which waited for: 7 -> 8; matrix products, arithmetic and copies ran while one was open for 0% -> 0% of each run, Pallas kernels for 3% -> 6%
where the time goes in v3:
time: 62.6 us; the launch traced here: 62.4 us
  waiting for transfers between devices  25.3 us (40%)
  starting transfers between devices  20.6 us (33%)
  Pallas kernels  15 us (24%)
  between operations  0.83 us (1%)
  local copies, waits for them, and re-layouts  0.75 us (1%)
    ppermute x18, waiting for transfers between devices, hop(): return lambda x: lax.ppermute(x, axis, pairs)  25.3 us
    ppermute x18, starting transfers between devices, hop(): return lambda x: lax.ppermute(x, axis, pairs)  20.6 us
    pallas_call x1, Pallas kernels, per_device(): pl.pallas_call(functools.partial(last_kernel, helpers, (len(earlier), len...  8.31 us
    pallas_call x1, Pallas kernels, per_device(): pl.pallas_call(functools.partial(some_kernel, helpers, height), out_shape...  3.81 us
    pallas_call x1, Pallas kernels, per_device(): pl.pallas_call(functools.partial(pack_kernel, depth, owners), out_shape=b...  1.56 us
    pallas_call x1, Pallas kernels, per_device(): pl.pallas_call(functools.partial(unpack_kernel, depth, owners), out_shape...  1.31 us
  transfers between devices with their start and end apart: 18, of which 8 were waited for; matrix products, arithmetic and copies ran while one was open for 0% of the time, Pallas kernels for 6%

profile of v3, /device:TPU:0, one launch (start us, length us, event | category | flops | bytes accessed | tf_op | source)
XLA Modules:
  0.0 62.4 jit_solution(4135317474705282981)
XLA Ops:
  0.6 1.6 %pack.1 = (bf16[192,1024]{1,0:T(8,128)(2,1)S(1)}, bf16[128,1024]{1,0:T(8,128)(2,1)S(1)}, bf16[128,1024]{1,0:T(8,128)(2,1)S(1)}, bf16[128,1024]{1,0:T(8,128)(2,1)S(1)}) custom-call(s32[1]{0:T(128)} %bitcast.1.me_ref, s32[1,256]{1,0:T(1,128)} %bitcast.5, bf16[256,1024]{1,0:T(8,128)(2,1)} %points_hbm.1, bf16[64,1024]{1,0:T(8,128)(2,1)} %bitcast.7), custom_call_target="tpu_custom_call" | custom-call | flops 1 | bytes 1 | tf_op jit(solution)/shard_map/pack/pallas_call | solution.py:248
  2.2 0.0 copy-start
  2.2 3.1 %collective-permute-start.3 = (bf16[128,1024]{1,0:T(8,128)(2,1)S(1)}, bf16[128,1024]{1,0:T(8,128)(2,1)S(1)}, u32[]{:S(2)}, u32[]{:S(2)}) collective-permute-start(bf16[128,1024]{1,0:T(8,128)(2,1)S(1)} %get-tuple-element.16), channel_id=1, source_target_pairs={{0,4},{4,0},{8,12},{12,8},{1,5},{5,1},{9,13},{13,9},{2,6},{6,2},{1... | collective-permute-start | bytes 786440 | tf_op jit(solution)/shard_map/ppermute | solution.py:229
  5.3 1.5 %collective-permute-start = (bf16[192,1024]{1,0:T(8,128)(2,1)S(1)}, bf16[192,1024]{1,0:T(8,128)(2,1)S(1)}, u32[]{:S(2)}, u32[]{:S(2)}) collective-permute-start(bf16[192,1024]{1,0:T(8,128)(2,1)S(1)} %get-tuple-element.15.refs_0_.refs_1_), channel_id=1, source_target_pairs={{0,2},{1,3},{2,0},{3,1},{4,6},{5,7},{6,4},{7,5},{8,10},{9,11},{10,... | collective-permute-start | bytes 1179656 | tf_op jit(solution)/shard_map/ppermute | solution.py:229
  6.8 2.6 %collective-permute-start.7 = (bf16[128,1024]{1,0:T(8,128)(2,1)S(1)}, bf16[128,1024]{1,0:T(8,128)(2,1)S(1)}, u32[]{:S(2)}, u32[]{:S(2)}) collective-permute-start(bf16[128,1024]{1,0:T(8,128)(2,1)S(1)} %get-tuple-element.17), channel_id=1, source_target_pairs={{0,8},{4,12},{8,0},{12,4},{1,9},{5,13},{9,1},{13,5},{2,10},{6,14},... | collective-permute-start | bytes 786440 | tf_op jit(solution)/shard_map/ppermute | solution.py:229
  9.4 6.5 %collective-permute-done.3.refs_4_.refs_5_ = bf16[128,1024]{1,0:T(8,128)(2,1)S(1)} collective-permute-done((bf16[128,1024]{1,0:T(8,128)(2,1)S(1)}, bf16[128,1024]{1,0:T(8,128)(2,1)S(1)}, u32[]{:S(2)}, u32[]{:S(2)}) %collective-permute-start.3) | collective-permute-done | bytes 262176 | tf_op jit(solution)/shard_map/ppermute | solution.py:229
  15.9 0.0 copy-start.4
  15.9 2.6 %collective-permute-start.5 = (bf16[128,1024]{1,0:T(8,128)(2,1)S(1)}, bf16[128,1024]{1,0:T(8,128)(2,1)S(1)}, u32[]{:S(2)}, u32[]{:S(2)}) collective-permute-start(bf16[128,1024]{1,0:T(8,128)(2,1)S(1)} %collective-permute-done.3.refs_4_.refs_5_), channel_id=1, source_target_pairs={{0,2},{1,3},{2,0},{3,1},{4,6},{5,7},{6,4},{7,5},{8,10},{9,11},{10,... | collective-permute-start | bytes 786440 | tf_op jit(solution)/shard_map/ppermute | solution.py:229
  18.5 0.0 collective-permute-start.4
  18.5 2.3 %collective-permute-done.7.refs_8_.refs_9_ = bf16[128,1024]{1,0:T(8,128)(2,1)S(1)} collective-permute-done((bf16[128,1024]{1,0:T(8,128)(2,1)S(1)}, bf16[128,1024]{1,0:T(8,128)(2,1)S(1)}, u32[]{:S(2)}, u32[]{:S(2)}) %collective-permute-start.7) | collective-permute-done | bytes 262176 | tf_op jit(solution)/shard_map/ppermute | solution.py:229
  20.8 0.0 copy-start.5
  20.8 2.6 %collective-permute-start.11 = (bf16[128,1024]{1,0:T(8,128)(2,1)S(1)}, bf16[128,1024]{1,0:T(8,128)(2,1)}, u32[]{:S(2)}, u32[]{:S(2)}) collective-permute-start(bf16[128,1024]{1,0:T(8,128)(2,1)S(1)} %get-tuple-element.19), channel_id=1, source_target_pairs={{0,12},{4,8},{8,4},{12,0},{1,13},{5,9},{9,5},{13,1},{2,14},{6,10},... | collective-permute-start | bytes 786440 | tf_op jit(solution)/shard_map/ppermute | solution.py:229
  23.5 0.4 collective-permute-start.9
  23.8 0.0 collective-permute-done.refs_2_.refs_3_
  23.9 0.0 copy-start.1
  23.9 0.0 collective-permute-start.8
  23.9 0.7 %collective-permute-done.5.refs_6_.refs_7_ = bf16[128,1024]{1,0:T(8,128)(2,1)S(1)} collective-permute-done((bf16[128,1024]{1,0:T(8,128)(2,1)S(1)}, bf16[128,1024]{1,0:T(8,128)(2,1)S(1)}, u32[]{:S(2)}, u32[]{:S(2)}) %collective-permute-start.5) | collective-permute-done | bytes 262176 | tf_op jit(solution)/shard_map/ppermute | solution.py:229
  24.5 0.0 copy-start.6
  24.5 0.0 collective-permute-start.1
  24.5 0.0 collective-permute-done.4.refs_5_.refs_6_
  24.5 0.0 copy-start.7
  24.5 0.5 collective-permute-start.2
  25.0 4.2 %collective-permute-done.11.refs_13_ = bf16[128,1024]{1,0:T(8,128)(2,1)} collective-permute-done((bf16[128,1024]{1,0:T(8,128)(2,1)S(1)}, bf16[128,1024]{1,0:T(8,128)(2,1)}, u32[]{:S(2)}, u32[]{:S(2)}) %collective-permute-start.11) | collective-permute-done | bytes 262176 | tf_op jit(solution)/shard_map/ppermute | solution.py:229
  29.3 0.0 collective-permute-start.6
  29.3 0.6 collective-permute-done.9.refs_10_.refs_11_
  29.9 0.0 copy-start.8
  29.9 0.0 collective-permute-start.10
  29.9 0.0 collective-permute-done.8.refs_9_.refs_10_
  29.9 0.0 copy-start.9
  29.9 1.5 %collective-permute-start.13 = (bf16[128,1024]{1,0:T(8,128)(2,1)}, bf16[128,1024]{1,0:T(8,128)(2,1)}, u32[]{:S(2)}, u32[]{:S(2)}) collective-permute-start(bf16[128,1024]{1,0:T(8,128)(2,1)} %collective-permute-done.11.refs_13_), channel_id=1, source_target_pairs={{0,2},{1,3},{2,0},{3,1},{4,6},{5,7},{6,4},{7,5},{8,10},{9,11},{10,... | collective-permute-start | bytes 786440 | tf_op jit(solution)/shard_map/ppermute | solution.py:229
  31.4 0.0 collective-permute-done.6.refs_7_.refs_8_
  31.4 0.2 collective-permute-start.12
  31.6 0.0 collective-permute-done.10.refs_11_.refs_12_
  31.6 0.0 collective-permute-done.1.refs_1_.refs_2_
  31.6 0.0 copy-start.2
  31.6 0.0 collective-permute-done.2.refs_3_.refs_4_
  31.6 0.0 copy-start.3
  31.6 3.8 %some_rows.1.refs_0_ = f32[256,1152]{1,0:T(8,128)S(1)} custom-call(bf16[192,1024]{1,0:T(8,128)(2,1)S(1)} %get-tuple-element.15.refs_0_.refs_1_, bf16[192,1024]{1,0:T(8,128)(2,1)S(1)} %collective-permute-done.1.refs_1_.refs_2_, bf16[192,1024]{1,0:T(8,128)(2,1)S(1)} %collective-permute-done.refs_2_.refs_3_, ...), custom_call_target="tpu_custom_call" | custom-call | flops 1 | bytes 1 | tf_op jit(solution)/shard_map/some_rows/pallas_call | solution.py:305
  35.4 0.0 copy-done
  35.4 0.0 copy-done.4
  35.4 0.0 copy-done.5
  35.5 0.0 copy-done.1
  35.5 0.0 copy-done.6
  35.5 0.0 copy-done.7
  35.5 0.0 copy-done.8
  35.5 0.0 copy-done.9
  35.5 0.0 copy-done.10
  35.5 0.0 copy-done.11
  35.5 0.0 copy-done.2
  35.5 0.0 copy-done.3
  35.5 3.4 %collective-permute-done.13.refs_15_ = bf16[128,1024]{1,0:T(8,128)(2,1)} collective-permute-done((bf16[128,1024]{1,0:T(8,128)(2,1)}, bf16[128,1024]{1,0:T(8,128)(2,1)}, u32[]{:S(2)}, u32[]{:S(2)}) %collective-permute-start.13) | collective-permute-done | bytes 262176 | tf_op jit(solution)/shard_map/ppermute | solution.py:229
  38.9 0.0 collective-permute-start.14
  38.9 0.0 collective-permute-done.12.refs_14_
  38.9 1.7 %collective-permute-done.14.refs_16_ = bf16[128,1024]{1,0:T(8,128)(2,1)S(1)} collective-permute-done((bf16[128,1024]{1,0:T(8,128)(2,1)}, bf16[128,1024]{1,0:T(8,128)(2,1)S(1)}, u32[]{:S(2)}, u32[]{:S(2)}) %collective-permute-start.14) | collective-permute-done | bytes 262176 | tf_op jit(solution)/shard_map/ppermute | solution.py:229
  40.7 0.7 %copy-done.13 = bf16[128,1024]{1,0:T(8,128)(2,1)} copy-done((bf16[128,1024]{1,0:T(8,128)(2,1)}, bf16[128,1024]{1,0:T(8,128)(2,1)S(1)}, u32[]{:S(2)}) %copy-start.13) | copy-done | bytes 262168
  41.4 8.3 %rounds.1 = (f32[64,1024]{1,0:T(8,128)}, bf16[128,256]{1,0:T(8,128)(2,1)S(1)}, bf16[128,256]{1,0:T(8,128)(2,1)S(1)}, bf16[128,256]{1,0:T(8,128)(2,1)S(1)}, bf16[128,256]{1,0:T(8,128)(2,1)S(1)}) custom-call(s32[1]{0:T(128)} %bitcast.helper_ref, f32[256,1152]{1,0:T(8,128)S(1)} %some_rows.1.refs_0_, bf16[192,1024]{1,0:T(8,128)(2,1)} %copy-done, ...), custom_call_target="tpu_custom_call" | custom-call | flops 1 | bytes 1 | tf_op jit(solution)/shard_map/rounds/pallas_call | solution.py:320
  49.7 3.2 %collective-permute-start.15 = (bf16[128,256]{1,0:T(8,128)(2,1)S(1)}, bf16[128,256]{1,0:T(8,128)(2,1)S(1)}, u32[]{:S(2)}, u32[]{:S(2)}) collective-permute-start(bf16[128,256]{1,0:T(8,128)(2,1)S(1)} %get-tuple-element.23), channel_id=1, source_target_pairs={{0,4},{4,0},{8,12},{12,8},{1,5},{5,1},{9,13},{13,9},{2,6},{6,2},{1... | collective-permute-start | bytes 196616 | tf_op jit(solution)/shard_map/ppermute | solution.py:229
  52.9 0.9 %collective-permute-start.16 = (bf16[128,256]{1,0:T(8,128)(2,1)S(1)}, bf16[128,256]{1,0:T(8,128)(2,1)S(1)}, u32[]{:S(2)}, u32[]{:S(2)}) collective-permute-start(bf16[128,256]{1,0:T(8,128)(2,1)S(1)} %get-tuple-element.24), channel_id=1, source_target_pairs={{0,8},{4,12},{8,0},{12,4},{1,9},{5,13},{9,1},{13,5},{2,10},{6,14},... | collective-permute-start | bytes 196616 | tf_op jit(solution)/shard_map/ppermute | solution.py:229
  53.8 1.5 %collective-permute-start.17 = (bf16[128,256]{1,0:T(8,128)(2,1)S(1)}, bf16[128,256]{1,0:T(8,128)(2,1)S(1)}, u32[]{:S(2)}, u32[]{:S(2)}) collective-permute-start(bf16[128,256]{1,0:T(8,128)(2,1)S(1)} %get-tuple-element.25), channel_id=1, source_target_pairs={{0,12},{4,8},{8,4},{12,0},{1,13},{5,9},{9,5},{13,1},{2,14},{6,10},... | collective-permute-start | bytes 196616 | tf_op jit(solution)/shard_map/ppermute | solution.py:229
  55.3 0.0 collective-permute-done.15.refs_1_
  55.3 5.8 %collective-permute-done.16.refs_2_ = bf16[128,256]{1,0:T(8,128)(2,1)S(1)} collective-permute-done((bf16[128,256]{1,0:T(8,128)(2,1)S(1)}, bf16[128,256]{1,0:T(8,128)(2,1)S(1)}, u32[]{:S(2)}, u32[]{:S(2)}) %collective-permute-start.16) | collective-permute-done | bytes 65568 | tf_op jit(solution)/shard_map/ppermute | solution.py:229
  61.1 0.0 collective-permute-done.17.refs_3_
  61.1 0.0 copy-done.12
  61.1 1.3 %unpack.1 = f32[256,256]{1,0:T(8,128)} custom-call(s32[1]{0:T(128)} %bitcast.1.me_ref, s32[1,256]{1,0:T(1,128)S(1)} %bitcast.6, bf16[128,256]{1,0:T(8,128)(2,1)S(1)} %get-tuple-element.22.refs_0_, bf16[128,256]{1,0:T(8,128)(2,1)S(1)} %collective-permute-done.15.refs_1_, bf16[128,256]{1,0:T(8,128)(2,1)S(1)} %collective-permute-done.16.refs_2_, ...), custom_call_target="tpu_custom_call" | custom-call | flops 1 | bytes 1 | tf_op jit(solution)/shard_map/unpack/pallas_call | solution.py:334
  (4 shorter events, 0.0 us)
Async XLA Ops:
  2.2 33.2 %copy-start = (bf16[192,1024]{1,0:T(8,128)(2,1)}, bf16[192,1024]{1,0:T(8,128)(2,1)S(1)}, u32[]{:S(2)}) copy-start(bf16[192,1024]{1,0:T(8,128)(2,1)S(1)} %get-tuple-element.15.refs_0_.refs_1_) | copy-start | bytes 1179652
  2.2 13.7 %collective-permute-start.3 = (bf16[128,1024]{1,0:T(8,128)(2,1)S(1)}, bf16[128,1024]{1,0:T(8,128)(2,1)S(1)}, u32[]{:S(2)}, u32[]{:S(2)}) collective-permute-start(bf16[128,1024]{1,0:T(8,128)(2,1)S(1)} %get-tuple-element.16), channel_id=1, source_target_pairs={{0,4},{4,0},{8,12},{12,8},{1,5},{5,1},{9,13},{13,9},{2,6},{6,2},{1... | collective-permute-start | bytes 786440 | tf_op jit(solution)/shard_map/ppermute | solution.py:229
  5.3 18.6 %collective-permute-start = (bf16[192,1024]{1,0:T(8,128)(2,1)S(1)}, bf16[192,1024]{1,0:T(8,128)(2,1)S(1)}, u32[]{:S(2)}, u32[]{:S(2)}) collective-permute-start(bf16[192,1024]{1,0:T(8,128)(2,1)S(1)} %get-tuple-element.15.refs_0_.refs_1_), channel_id=1, source_target_pairs={{0,2},{1,3},{2,0},{3,1},{4,6},{5,7},{6,4},{7,5},{8,10},{9,11},{10,... | collective-permute-start | bytes 1179656 | tf_op jit(solution)/shard_map/ppermute | solution.py:229
  6.8 14.0 %collective-permute-start.7 = (bf16[128,1024]{1,0:T(8,128)(2,1)S(1)}, bf16[128,1024]{1,0:T(8,128)(2,1)S(1)}, u32[]{:S(2)}, u32[]{:S(2)}) collective-permute-start(bf16[128,1024]{1,0:T(8,128)(2,1)S(1)} %get-tuple-element.17), channel_id=1, source_target_pairs={{0,8},{4,12},{8,0},{12,4},{1,9},{5,13},{9,1},{13,5},{2,10},{6,14},... | collective-permute-start | bytes 786440 | tf_op jit(solution)/shard_map/ppermute | solution.py:229
  15.9 19.5 %copy-start.4 = (bf16[128,1024]{1,0:T(8,128)(2,1)}, bf16[128,1024]{1,0:T(8,128)(2,1)S(1)}, u32[]{:S(2)}) copy-start(bf16[128,1024]{1,0:T(8,128)(2,1)S(1)} %collective-permute-done.3.refs_4_.refs_5_) | copy-start | bytes 786436
  15.9 8.6 %collective-permute-start.5 = (bf16[128,1024]{1,0:T(8,128)(2,1)S(1)}, bf16[128,1024]{1,0:T(8,128)(2,1)S(1)}, u32[]{:S(2)}, u32[]{:S(2)}) collective-permute-start(bf16[128,1024]{1,0:T(8,128)(2,1)S(1)} %collective-permute-done.3.refs_4_.refs_5_), channel_id=1, source_target_pairs={{0,2},{1,3},{2,0},{3,1},{4,6},{5,7},{6,4},{7,5},{8,10},{9,11},{10,... | collective-permute-start | bytes 786440 | tf_op jit(solution)/shard_map/ppermute | solution.py:229
  18.5 6.0 %collective-permute-start.4 = (bf16[128,1024]{1,0:T(8,128)(2,1)S(1)}, bf16[128,1024]{1,0:T(8,128)(2,1)S(1)}, u32[]{:S(2)}, u32[]{:S(2)}) collective-permute-start(bf16[128,1024]{1,0:T(8,128)(2,1)S(1)} %collective-permute-done.3.refs_4_.refs_5_), channel_id=1, source_target_pairs={{0,1},{1,0},{2,3},{3,2},{4,5},{5,4},{6,7},{7,6},{8,9},{9,8},{10,11... | collective-permute-start | bytes 786440 | tf_op jit(solution)/shard_map/ppermute | solution.py:229
  20.8 14.6 %copy-start.5 = (bf16[128,1024]{1,0:T(8,128)(2,1)}, bf16[128,1024]{1,0:T(8,128)(2,1)S(1)}, u32[]{:S(2)}) copy-start(bf16[128,1024]{1,0:T(8,128)(2,1)S(1)} %collective-permute-done.7.refs_8_.refs_9_) | copy-start | bytes 786436
  20.8 8.4 %collective-permute-start.11 = (bf16[128,1024]{1,0:T(8,128)(2,1)S(1)}, bf16[128,1024]{1,0:T(8,128)(2,1)}, u32[]{:S(2)}, u32[]{:S(2)}) collective-permute-start(bf16[128,1024]{1,0:T(8,128)(2,1)S(1)} %get-tuple-element.19), channel_id=1, source_target_pairs={{0,12},{4,8},{8,4},{12,0},{1,13},{5,9},{9,5},{13,1},{2,14},{6,10},... | collective-permute-start | bytes 786440 | tf_op jit(solution)/shard_map/ppermute | solution.py:229
  23.5 6.4 %collective-permute-start.9 = (bf16[128,1024]{1,0:T(8,128)(2,1)S(1)}, bf16[128,1024]{1,0:T(8,128)(2,1)S(1)}, u32[]{:S(2)}, u32[]{:S(2)}) collective-permute-start(bf16[128,1024]{1,0:T(8,128)(2,1)S(1)} %collective-permute-done.7.refs_8_.refs_9_), channel_id=1, source_target_pairs={{0,2},{1,3},{2,0},{3,1},{4,6},{5,7},{6,4},{7,5},{8,10},{9,11},{10,... | collective-permute-start | bytes 786440 | tf_op jit(solution)/shard_map/ppermute | solution.py:229
  23.9 11.6 %copy-start.1 = (bf16[192,1024]{1,0:T(8,128)(2,1)}, bf16[192,1024]{1,0:T(8,128)(2,1)S(1)}, u32[]{:S(2)}) copy-start(bf16[192,1024]{1,0:T(8,128)(2,1)S(1)} %collective-permute-done.refs_2_.refs_3_) | copy-start | bytes 1179652
  23.9 6.0 %collective-permute-start.8 = (bf16[128,1024]{1,0:T(8,128)(2,1)S(1)}, bf16[128,1024]{1,0:T(8,128)(2,1)S(1)}, u32[]{:S(2)}, u32[]{:S(2)}) collective-permute-start(bf16[128,1024]{1,0:T(8,128)(2,1)S(1)} %collective-permute-done.7.refs_8_.refs_9_), channel_id=1, source_target_pairs={{0,1},{1,0},{2,3},{3,2},{4,5},{5,4},{6,7},{7,6},{8,9},{9,8},{10,11... | collective-permute-start | bytes 786440 | tf_op jit(solution)/shard_map/ppermute | solution.py:229
  24.5 11.0 %copy-start.6 = (bf16[128,1024]{1,0:T(8,128)(2,1)}, bf16[128,1024]{1,0:T(8,128)(2,1)S(1)}, u32[]{:S(2)}) copy-start(bf16[128,1024]{1,0:T(8,128)(2,1)S(1)} %collective-permute-done.5.refs_6_.refs_7_) | copy-start | bytes 786436
  24.5 7.1 %collective-permute-start.1 = (bf16[192,1024]{1,0:T(8,128)(2,1)S(1)}, bf16[192,1024]{1,0:T(8,128)(2,1)S(1)}, u32[]{:S(2)}, u32[]{:S(2)}) collective-permute-start(bf16[192,1024]{1,0:T(8,128)(2,1)S(1)} %get-tuple-element.15.refs_0_.refs_1_), channel_id=1, source_target_pairs={{0,1},{1,0},{2,3},{3,2},{4,5},{5,4},{6,7},{7,6},{8,9},{9,8},{10,11... | collective-permute-start | bytes 1179656 | tf_op jit(solution)/shard_map/ppermute | solution.py:229
  24.5 11.0 %copy-start.7 = (bf16[128,1024]{1,0:T(8,128)(2,1)}, bf16[128,1024]{1,0:T(8,128)(2,1)S(1)}, u32[]{:S(2)}) copy-start(bf16[128,1024]{1,0:T(8,128)(2,1)S(1)} %collective-permute-done.4.refs_5_.refs_6_) | copy-start | bytes 786436
  24.5 7.1 %collective-permute-start.2 = (bf16[192,1024]{1,0:T(8,128)(2,1)S(1)}, bf16[192,1024]{1,0:T(8,128)(2,1)S(1)}, u32[]{:S(2)}, u32[]{:S(2)}) collective-permute-start(bf16[192,1024]{1,0:T(8,128)(2,1)S(1)} %collective-permute-done.refs_2_.refs_3_), channel_id=1, source_target_pairs={{0,1},{1,0},{2,3},{3,2},{4,5},{5,4},{6,7},{7,6},{8,9},{9,8},{10,11... | collective-permute-start | bytes 1179656 | tf_op jit(solution)/shard_map/ppermute | solution.py:229
  29.3 2.1 %collective-permute-start.6 = (bf16[128,1024]{1,0:T(8,128)(2,1)S(1)}, bf16[128,1024]{1,0:T(8,128)(2,1)S(1)}, u32[]{:S(2)}, u32[]{:S(2)}) collective-permute-start(bf16[128,1024]{1,0:T(8,128)(2,1)S(1)} %collective-permute-done.5.refs_6_.refs_7_), channel_id=1, source_target_pairs={{0,1},{1,0},{2,3},{3,2},{4,5},{5,4},{6,7},{7,6},{8,9},{9,8},{10,11... | collective-permute-start | bytes 786440 | tf_op jit(solution)/shard_map/ppermute | solution.py:229
  29.9 5.6 %copy-start.8 = (bf16[128,1024]{1,0:T(8,128)(2,1)}, bf16[128,1024]{1,0:T(8,128)(2,1)S(1)}, u32[]{:S(2)}) copy-start(bf16[128,1024]{1,0:T(8,128)(2,1)S(1)} %collective-permute-done.9.refs_10_.refs_11_) | copy-start | bytes 786436
  29.9 1.7 %collective-permute-start.10 = (bf16[128,1024]{1,0:T(8,128)(2,1)S(1)}, bf16[128,1024]{1,0:T(8,128)(2,1)S(1)}, u32[]{:S(2)}, u32[]{:S(2)}) collective-permute-start(bf16[128,1024]{1,0:T(8,128)(2,1)S(1)} %collective-permute-done.9.refs_10_.refs_11_), channel_id=1, source_target_pairs={{0,1},{1,0},{2,3},{3,2},{4,5},{5,4},{6,7},{7,6},{8,9},{9,8},{10,11... | collective-permute-start | bytes 786440 | tf_op jit(solution)/shard_map/ppermute | solution.py:229
  29.9 5.6 %copy-start.9 = (bf16[128,1024]{1,0:T(8,128)(2,1)}, bf16[128,1024]{1,0:T(8,128)(2,1)S(1)}, u32[]{:S(2)}) copy-start(bf16[128,1024]{1,0:T(8,128)(2,1)S(1)} %collective-permute-done.8.refs_9_.refs_10_) | copy-start | bytes 786436
  29.9 9.0 %collective-permute-start.13 = (bf16[128,1024]{1,0:T(8,128)(2,1)}, bf16[128,1024]{1,0:T(8,128)(2,1)}, u32[]{:S(2)}, u32[]{:S(2)}) collective-permute-start(bf16[128,1024]{1,0:T(8,128)(2,1)} %collective-permute-done.11.refs_13_), channel_id=1, source_target_pairs={{0,2},{1,3},{2,0},{3,1},{4,6},{5,7},{6,4},{7,5},{8,10},{9,11},{10,... | collective-permute-start | bytes 786440 | tf_op jit(solution)/shard_map/ppermute | solution.py:229
  31.4 4.1 %copy-start.10 = (bf16[128,1024]{1,0:T(8,128)(2,1)}, bf16[128,1024]{1,0:T(8,128)(2,1)S(1)}, u32[]{:S(2)}) copy-start(bf16[128,1024]{1,0:T(8,128)(2,1)S(1)} %collective-permute-done.6.refs_7_.refs_8_) | copy-start | bytes 786436
  31.4 7.5 %collective-permute-start.12 = (bf16[128,1024]{1,0:T(8,128)(2,1)}, bf16[128,1024]{1,0:T(8,128)(2,1)}, u32[]{:S(2)}, u32[]{:S(2)}) collective-permute-start(bf16[128,1024]{1,0:T(8,128)(2,1)} %collective-permute-done.11.refs_13_), channel_id=1, source_target_pairs={{0,1},{1,0},{2,3},{3,2},{4,5},{5,4},{6,7},{7,6},{8,9},{9,8},{10,11... | collective-permute-start | bytes 786440 | tf_op jit(solution)/shard_map/ppermute | solution.py:229
  31.6 4.0 %copy-start.11 = (bf16[128,1024]{1,0:T(8,128)(2,1)}, bf16[128,1024]{1,0:T(8,128)(2,1)S(1)}, u32[]{:S(2)}) copy-start(bf16[128,1024]{1,0:T(8,128)(2,1)S(1)} %collective-permute-done.10.refs_11_.refs_12_) | copy-start | bytes 786436
  31.6 4.0 %copy-start.2 = (bf16[192,1024]{1,0:T(8,128)(2,1)}, bf16[192,1024]{1,0:T(8,128)(2,1)S(1)}, u32[]{:S(2)}) copy-start(bf16[192,1024]{1,0:T(8,128)(2,1)S(1)} %collective-permute-done.1.refs_1_.refs_2_) | copy-start | bytes 1179652
  31.6 3.9 %copy-start.3 = (bf16[192,1024]{1,0:T(8,128)(2,1)}, bf16[192,1024]{1,0:T(8,128)(2,1)S(1)}, u32[]{:S(2)}) copy-start(bf16[192,1024]{1,0:T(8,128)(2,1)S(1)} %collective-permute-done.2.refs_3_.refs_4_) | copy-start | bytes 1179652
  38.9 1.7 %collective-permute-start.14 = (bf16[128,1024]{1,0:T(8,128)(2,1)}, bf16[128,1024]{1,0:T(8,128)(2,1)S(1)}, u32[]{:S(2)}, u32[]{:S(2)}) collective-permute-start(bf16[128,1024]{1,0:T(8,128)(2,1)} %collective-permute-done.13.refs_15_), channel_id=1, source_target_pairs={{0,1},{1,0},{2,3},{3,2},{4,5},{5,4},{6,7},{7,6},{8,9},{9,8},{10,11... | collective-permute-start | bytes 786440 | tf_op jit(solution)/shard_map/ppermute | solution.py:229
  40.7 0.7 %copy-start.13 = (bf16[128,1024]{1,0:T(8,128)(2,1)}, bf16[128,1024]{1,0:T(8,128)(2,1)S(1)}, u32[]{:S(2)}) copy-start(bf16[128,1024]{1,0:T(8,128)(2,1)S(1)} %collective-permute-done.14.refs_16_) | copy-start | bytes 786436
  41.4 19.8 %copy-start.12 = (s32[256]{0:T(256)S(1)}, s32[256]{0:T(256)}, u32[]{:S(2)}) copy-start(s32[256]{0:T(256)} %param.4) | copy-start | bytes 3076
  49.7 5.6 %collective-permute-start.15 = (bf16[128,256]{1,0:T(8,128)(2,1)S(1)}, bf16[128,256]{1,0:T(8,128)(2,1)S(1)}, u32[]{:S(2)}, u32[]{:S(2)}) collective-permute-start(bf16[128,256]{1,0:T(8,128)(2,1)S(1)} %get-tuple-element.23), channel_id=1, source_target_pairs={{0,4},{4,0},{8,12},{12,8},{1,5},{5,1},{9,13},{13,9},{2,6},{6,2},{1... | collective-permute-start | bytes 196616 | tf_op jit(solution)/shard_map/ppermute | solution.py:229
  52.9 8.3 %collective-permute-start.16 = (bf16[128,256]{1,0:T(8,128)(2,1)S(1)}, bf16[128,256]{1,0:T(8,128)(2,1)S(1)}, u32[]{:S(2)}, u32[]{:S(2)}) collective-permute-start(bf16[128,256]{1,0:T(8,128)(2,1)S(1)} %get-tuple-element.24), channel_id=1, source_target_pairs={{0,8},{4,12},{8,0},{12,4},{1,9},{5,13},{9,1},{13,5},{2,10},{6,14},... | collective-permute-start | bytes 196616 | tf_op jit(solution)/shard_map/ppermute | solution.py:229
  53.8 7.3 %collective-permute-start.17 = (bf16[128,256]{1,0:T(8,128)(2,1)S(1)}, bf16[128,256]{1,0:T(8,128)(2,1)S(1)}, u32[]{:S(2)}, u32[]{:S(2)}) collective-permute-start(bf16[128,256]{1,0:T(8,128)(2,1)S(1)} %get-tuple-element.25), channel_id=1, source_target_pairs={{0,12},{4,8},{8,4},{12,0},{1,13},{5,9},{9,5},{13,1},{2,14},{6,10},... | collective-permute-start | bytes 196616 | tf_op jit(solution)/shard_map/ppermute | solution.py:229

commit v4 on v3

--- a/solution.py
+++ b/solution.py
@@ -84,6 +84,7 @@
 
 def unpack_kernel(depth, owners, me_ref, cluster_ref, *refs):
     *logs, out = refs
+    logs = logs[::-1]
     slot, _ = slots_of(me_ref[0], cluster_ref[...], depth, owners)
     count = slot.shape[1]
     column = jnp.broadcast_to(slot.astype(F32), (128, count)).T[:, 0:1].astype(jnp.int32)
@@ -170,8 +171,8 @@
     centres = fetch([ref.at[height:] for ref in given[:helpers]], ordered, ready)
     given = [ref.at[:height] for ref in given]
     later = fetch(given[earlier:], rows.at[held:], arrived.at[earlier:])
+    state = fetch(old, state_ref, kept)
     sooner = fetch(given[:earlier], rows, arrived)
-    state = fetch(old, state_ref, kept)
     helper = helper_ref[0]
     settle(centres)
     centres = ordered[...]
@@ -194,12 +195,15 @@
     centres = ordered[...]
     norms = square_norms(centres)
     turned = centres.T
-    for i, out in enumerate(logs):
-        first = i * helpers * height
-        logits = energies(turned, norms, rows[first : first + height, :])
+    own_rows = [rows[g * helpers * height : g * helpers * height + height, :] for g in range(own)]
+    pair = 2 if 2 * height <= TILE and own % 2 == 0 else 1
+    for g in range(0, own, pair):
+        logits = energies(turned, norms, joined(own_rows[g : g + pair]))
         top = jnp.max(logits, axis=1, keepdims=True)
         total = jnp.log(jnp.sum(jnp.exp(logits - top), axis=1, keepdims=True))
-        out[...] = (logits - (top + total)).astype(BF)
+        result = (logits - (top + total)).astype(BF)
+        for i in range(pair):
+            logs[g + i][...] = result[i * height : (i + 1) * height]
 
 
 def vmem(n):
@@ -300,7 +304,7 @@
     held = [over_chips(block) for block in moved]
     own_beside = beside(after(packed[0], held[0][1]))
     rows = [[moved[0], own_beside] + over_cores(held[0][1:])] + [over_cores(part) for part in held[1:-1]]
-    given = [r for part in rows for r in part]
+    given = [r for part in rows for r in part] + over_cores(held[-1][:1])
     own = scratch(len(given))
     sofar = pl.pallas_call(
         functools.partial(some_kernel, helpers, height),
@@ -312,8 +316,8 @@
         cost_estimate=COST,
         name="some_rows",
     )(*given)
-    late = over_cores(held[-1][:-1] + [after(held[-1][-1], sofar)])
-    earlier = [r for part in rows for r in part]
+    late = over_cores(held[-1][1:-1] + [after(held[-1][-1], sofar)])
+    earlier = given
     logs = [jax.ShapeDtypeStruct((height, subs), BF)] * groups
     refined = jax.ShapeDtypeStruct((share_rows, width), F32)
     own = scratch(len(earlier) + len(late))
@@ -327,9 +331,9 @@
         compiler_params=params(*own, refined, *logs),
         cost_estimate=COST,
         name="rounds",
-    )(helper, sofar, *[in_hbm(r) for r in earlier + late])
-
-    back = [across(logs[g], g) for g in range(groups)]
+    )(helper, sofar, *[in_hbm(r) for r in earlier], *late)
+
+    back = [across(logs[g], g) for g in reversed(range(groups))]
     out = jax.ShapeDtypeStruct((count, subs), F32)
     log_resp = pl.pallas_call(
         functools.partial(unpack_kernel, depth, owners),

time: 62.6 us -> 58.9 us (0.941)
  Pallas kernels: 15 us -> 13.8 us
  waiting for transfers between devices: 25.3 us -> 24.3 us
  starting transfers between devices: 20.6 us -> 19.7 us
  local copies, waits for them, and re-layouts: 0.75 us -> 0.06 us
    pallas_call x1, Pallas kernels: 8.31 us -> 6.29 us  [per_device(): pl.pallas_call(functools.partial(last_kernel, helpers, (len(earlier), len...]
    ppermute x18, waiting for transfers between devices: 25.3 us -> 24.3 us  [hop(): return lambda x: lax.ppermute(x, axis, pairs)]
    ppermute x18, starting transfers between devices: 20.6 us -> 19.7 us  [hop(): return lambda x: lax.ppermute(x, axis, pairs)]
    pallas_call x1, Pallas kernels: 3.81 us -> 4.67 us  [per_device(): pl.pallas_call(functools.partial(some_kernel, helpers, height), out_shape...]
    unnamed x28 -> x30, local copies, waits for them, and re-layouts: 0.75 us -> 0.06 us
  transfers between devices with their start and end apart: 18 -> 18, of which waited for: 8 -> 9; matrix products, arithmetic and copies ran while one was open for 0% -> 0% of each run, Pallas kernels for 6% -> 8%
where the time goes in v4:
time: 58.9 us; the launch traced here: 58.7 us
  waiting for transfers between devices  24.3 us (41%)
  starting transfers between devices  19.7 us (33%)
  Pallas kernels  13.8 us (23%)
  between operations  0.84 us (1%)
    ppermute x18, waiting for transfers between devices, hop(): return lambda x: lax.ppermute(x, axis, pairs)  24.3 us
    ppermute x18, starting transfers between devices, hop(): return lambda x: lax.ppermute(x, axis, pairs)  19.7 us
    pallas_call x1, Pallas kernels, per_device(): pl.pallas_call(functools.partial(last_kernel, helpers, (len(earlier), len...  6.29 us
    pallas_call x1, Pallas kernels, per_device(): pl.pallas_call(functools.partial(some_kernel, helpers, height), out_shape...  4.67 us
    pallas_call x1, Pallas kernels, per_device(): pl.pallas_call(functools.partial(pack_kernel, depth, owners), out_shape=b...  1.56 us
    pallas_call x1, Pallas kernels, per_device(): pl.pallas_call(functools.partial(unpack_kernel, depth, owners), out_shape...  1.31 us
  transfers between devices with their start and end apart: 18, of which 9 were waited for; matrix products, arithmetic and copies ran while one was open for 0% of the time, Pallas kernels for 8%

profile of v4, /device:TPU:0, one launch (start us, length us, event | category | flops | bytes accessed | tf_op | source)
XLA Modules:
  0.0 58.7 jit_solution(8910734424093470926)
XLA Ops:
  0.6 1.6 %pack.1 = (bf16[192,1024]{1,0:T(8,128)(2,1)S(1)}, bf16[128,1024]{1,0:T(8,128)(2,1)S(1)}, bf16[128,1024]{1,0:T(8,128)(2,1)S(1)}, bf16[128,1024]{1,0:T(8,128)(2,1)S(1)}) custom-call(s32[1]{0:T(128)} %bitcast.1.me_ref, s32[1,256]{1,0:T(1,128)} %bitcast.5, bf16[256,1024]{1,0:T(8,128)(2,1)} %points_hbm.1, bf16[64,1024]{1,0:T(8,128)(2,1)} %bitcast.7), custom_call_target="tpu_custom_call" | custom-call | flops 1 | bytes 1 | tf_op jit(solution)/shard_map/pack/pallas_call | solution.py:252
  2.2 0.0 copy-start
  2.2 3.1 %collective-permute-start.3 = (bf16[128,1024]{1,0:T(8,128)(2,1)S(1)}, bf16[128,1024]{1,0:T(8,128)(2,1)S(1)}, u32[]{:S(2)}, u32[]{:S(2)}) collective-permute-start(bf16[128,1024]{1,0:T(8,128)(2,1)S(1)} %get-tuple-element.16), channel_id=1, source_target_pairs={{0,4},{4,0},{8,12},{12,8},{1,5},{5,1},{9,13},{13,9},{2,6},{6,2},{1... | collective-permute-start | bytes 786440 | tf_op jit(solution)/shard_map/ppermute | solution.py:233
  5.3 2.6 %collective-permute-start.7 = (bf16[128,1024]{1,0:T(8,128)(2,1)S(1)}, bf16[128,1024]{1,0:T(8,128)(2,1)S(1)}, u32[]{:S(2)}, u32[]{:S(2)}) collective-permute-start(bf16[128,1024]{1,0:T(8,128)(2,1)S(1)} %get-tuple-element.17), channel_id=1, source_target_pairs={{0,8},{4,12},{8,0},{12,4},{1,9},{5,13},{9,1},{13,5},{2,10},{6,14},... | collective-permute-start | bytes 786440 | tf_op jit(solution)/shard_map/ppermute | solution.py:233
  7.9 1.5 %collective-permute-start = (bf16[192,1024]{1,0:T(8,128)(2,1)S(1)}, bf16[192,1024]{1,0:T(8,128)(2,1)S(1)}, u32[]{:S(2)}, u32[]{:S(2)}) collective-permute-start(bf16[192,1024]{1,0:T(8,128)(2,1)S(1)} %get-tuple-element.15.refs_0_.refs_1_), channel_id=1, source_target_pairs={{0,2},{1,3},{2,0},{3,1},{4,6},{5,7},{6,4},{7,5},{8,10},{9,11},{10,... | collective-permute-start | bytes 1179656 | tf_op jit(solution)/shard_map/ppermute | solution.py:233
  9.4 7.7 %collective-permute-done.3.refs_4_.refs_5_ = bf16[128,1024]{1,0:T(8,128)(2,1)S(1)} collective-permute-done((bf16[128,1024]{1,0:T(8,128)(2,1)S(1)}, bf16[128,1024]{1,0:T(8,128)(2,1)S(1)}, u32[]{:S(2)}, u32[]{:S(2)}) %collective-permute-start.3) | collective-permute-done | bytes 262176 | tf_op jit(solution)/shard_map/ppermute | solution.py:233
  17.1 0.0 copy-start.4
  17.1 1.7 %collective-permute-start.5 = (bf16[128,1024]{1,0:T(8,128)(2,1)S(1)}, bf16[128,1024]{1,0:T(8,128)(2,1)S(1)}, u32[]{:S(2)}, u32[]{:S(2)}) collective-permute-start(bf16[128,1024]{1,0:T(8,128)(2,1)S(1)} %collective-permute-done.3.refs_4_.refs_5_), channel_id=1, source_target_pairs={{0,2},{1,3},{2,0},{3,1},{4,6},{5,7},{6,4},{7,5},{8,10},{9,11},{10,... | collective-permute-start | bytes 786440 | tf_op jit(solution)/shard_map/ppermute | solution.py:233
  18.8 0.0 collective-permute-start.4
  18.8 0.9 %collective-permute-done.7.refs_8_.refs_9_ = bf16[128,1024]{1,0:T(8,128)(2,1)S(1)} collective-permute-done((bf16[128,1024]{1,0:T(8,128)(2,1)S(1)}, bf16[128,1024]{1,0:T(8,128)(2,1)S(1)}, u32[]{:S(2)}, u32[]{:S(2)}) %collective-permute-start.7) | collective-permute-done | bytes 262176 | tf_op jit(solution)/shard_map/ppermute | solution.py:233
  19.6 0.0 copy-start.5
  19.6 2.5 %collective-permute-start.11 = (bf16[128,1024]{1,0:T(8,128)(2,1)S(1)}, bf16[128,1024]{1,0:T(8,128)(2,1)S(1)}, u32[]{:S(2)}, u32[]{:S(2)}) collective-permute-start(bf16[128,1024]{1,0:T(8,128)(2,1)S(1)} %get-tuple-element.19), channel_id=1, source_target_pairs={{0,12},{4,8},{8,4},{12,0},{1,13},{5,9},{9,5},{13,1},{2,14},{6,10},... | collective-permute-start | bytes 786440 | tf_op jit(solution)/shard_map/ppermute | solution.py:233
  22.1 1.5 %collective-permute-start.9 = (bf16[128,1024]{1,0:T(8,128)(2,1)S(1)}, bf16[128,1024]{1,0:T(8,128)(2,1)S(1)}, u32[]{:S(2)}, u32[]{:S(2)}) collective-permute-start(bf16[128,1024]{1,0:T(8,128)(2,1)S(1)} %collective-permute-done.7.refs_8_.refs_9_), channel_id=1, source_target_pairs={{0,2},{1,3},{2,0},{3,1},{4,6},{5,7},{6,4},{7,5},{8,10},{9,11},{10,... | collective-permute-start | bytes 786440 | tf_op jit(solution)/shard_map/ppermute | solution.py:233
  23.6 0.0 collective-permute-done.refs_2_.refs_3_
  23.6 0.0 copy-start.1
  23.6 0.0 collective-permute-start.8
  23.6 1.5 %collective-permute-done.5.refs_6_.refs_7_ = bf16[128,1024]{1,0:T(8,128)(2,1)S(1)} collective-permute-done((bf16[128,1024]{1,0:T(8,128)(2,1)S(1)}, bf16[128,1024]{1,0:T(8,128)(2,1)S(1)}, u32[]{:S(2)}, u32[]{:S(2)}) %collective-permute-start.5) | collective-permute-done | bytes 262176 | tf_op jit(solution)/shard_map/ppermute | solution.py:233
  25.1 0.0 copy-start.6
  25.1 0.0 collective-permute-start.6
  25.1 0.0 collective-permute-done.4.refs_5_.refs_6_
  25.1 0.0 copy-start.7
  25.1 0.5 collective-permute-start.1
  25.6 3.8 %collective-permute-done.11.refs_12_.refs_13_ = bf16[128,1024]{1,0:T(8,128)(2,1)S(1)} collective-permute-done((bf16[128,1024]{1,0:T(8,128)(2,1)S(1)}, bf16[128,1024]{1,0:T(8,128)(2,1)S(1)}, u32[]{:S(2)}, u32[]{:S(2)}) %collective-permute-start.11) | collective-permute-done | bytes 262176 | tf_op jit(solution)/shard_map/ppermute | solution.py:233
  29.4 0.0 copy-start.8
  29.4 0.0 collective-permute-start.2
  29.4 0.8 %collective-permute-done.9.refs_10_.refs_11_ = bf16[128,1024]{1,0:T(8,128)(2,1)S(1)} collective-permute-done((bf16[128,1024]{1,0:T(8,128)(2,1)S(1)}, bf16[128,1024]{1,0:T(8,128)(2,1)S(1)}, u32[]{:S(2)}, u32[]{:S(2)}) %collective-permute-start.9) | collective-permute-done | bytes 262176 | tf_op jit(solution)/shard_map/ppermute | solution.py:233
  30.2 0.0 collective-permute-start.12
  30.2 0.0 collective-permute-done.8.refs_9_.refs_10_
  30.2 0.0 copy-start.10
  30.2 0.5 collective-permute-start.10
  30.7 0.0 collective-permute-done.6.refs_7_.refs_8_
  30.7 1.3 %collective-permute-start.13 = (bf16[128,1024]{1,0:T(8,128)(2,1)S(1)}, bf16[128,1024]{1,0:T(8,128)(2,1)}, u32[]{:S(2)}, u32[]{:S(2)}) collective-permute-start(bf16[128,1024]{1,0:T(8,128)(2,1)S(1)} %collective-permute-done.11.refs_12_.refs_13_), channel_id=1, source_target_pairs={{0,2},{1,3},{2,0},{3,1},{4,6},{5,7},{6,4},{7,5},{8,10},{9,11},{10,... | collective-permute-start | bytes 786440 | tf_op jit(solution)/shard_map/ppermute | solution.py:233
  32.1 0.0 collective-permute-done.12.refs_13_.refs_14_
  32.1 0.0 collective-permute-done.10.refs_11_.refs_12_
  32.1 0.0 collective-permute-done.1.refs_1_.refs_2_
  32.1 0.0 collective-permute-done.2.refs_3_.refs_4_
  32.1 0.0 copy-start.3
  32.2 4.7 %some_rows.1.refs_0_ = f32[256,1152]{1,0:T(8,128)S(1)} custom-call(bf16[192,1024]{1,0:T(8,128)(2,1)S(1)} %get-tuple-element.15.refs_0_.refs_1_, bf16[192,1024]{1,0:T(8,128)(2,1)S(1)} %collective-permute-done.1.refs_1_.refs_2_, bf16[192,1024]{1,0:T(8,128)(2,1)S(1)} %collective-permute-done.refs_2_.refs_3_, ...), custom_call_target="tpu_custom_call" | custom-call | flops 1 | bytes 1 | tf_op jit(solution)/shard_map/some_rows/pallas_call | solution.py:309
  36.8 0.0 copy-done
  36.8 0.0 copy-done.4
  36.9 0.0 copy-done.5
  36.9 0.0 copy-done.1
  36.9 0.0 copy-done.6
  36.9 0.0 copy-done.7
  36.9 0.0 copy-done.8
  36.9 0.0 copy-done.9
  36.9 0.0 copy-done.10
  36.9 0.0 copy-done.11
  36.9 0.0 copy-done.12
  36.9 0.0 copy-done.13
  37.0 0.0 copy-done.2
  37.0 0.0 copy-done.3
  37.0 2.2 %collective-permute-done.13.refs_15_ = bf16[128,1024]{1,0:T(8,128)(2,1)} collective-permute-done((bf16[128,1024]{1,0:T(8,128)(2,1)S(1)}, bf16[128,1024]{1,0:T(8,128)(2,1)}, u32[]{:S(2)}, u32[]{:S(2)}) %collective-permute-start.13) | collective-permute-done | bytes 262176 | tf_op jit(solution)/shard_map/ppermute | solution.py:233
  39.1 0.0 collective-permute-start.14
  39.1 1.7 %collective-permute-done.14.refs_16_ = bf16[128,1024]{1,0:T(8,128)(2,1)S(1)} collective-permute-done((bf16[128,1024]{1,0:T(8,128)(2,1)}, bf16[128,1024]{1,0:T(8,128)(2,1)S(1)}, u32[]{:S(2)}, u32[]{:S(2)}) %collective-permute-start.14) | collective-permute-done | bytes 262176 | tf_op jit(solution)/shard_map/ppermute | solution.py:233
  40.9 6.3 %rounds.1 = (f32[64,1024]{1,0:T(8,128)}, bf16[128,256]{1,0:T(8,128)(2,1)S(1)}, bf16[128,256]{1,0:T(8,128)(2,1)S(1)}, bf16[128,256]{1,0:T(8,128)(2,1)S(1)}, bf16[128,256]{1,0:T(8,128)(2,1)S(1)}) custom-call(s32[1]{0:T(128)} %bitcast.helper_ref, f32[256,1152]{1,0:T(8,128)S(1)} %some_rows.1.refs_0_, bf16[192,1024]{1,0:T(8,128)(2,1)} %copy-done, ...), custom_call_target="tpu_custom_call" | custom-call | flops 1 | bytes 1 | tf_op jit(solution)/shard_map/rounds/pallas_call | solution.py:324
  47.2 2.4 %collective-permute-start.15 = (bf16[128,256]{1,0:T(8,128)(2,1)S(1)}, bf16[128,256]{1,0:T(8,128)(2,1)S(1)}, u32[]{:S(2)}, u32[]{:S(2)}) collective-permute-start(bf16[128,256]{1,0:T(8,128)(2,1)S(1)} %get-tuple-element.22), channel_id=1, source_target_pairs={{0,12},{4,8},{8,4},{12,0},{1,13},{5,9},{9,5},{13,1},{2,14},{6,10},... | collective-permute-start | bytes 196616 | tf_op jit(solution)/shard_map/ppermute | solution.py:233
  49.6 2.2 %collective-permute-start.16 = (bf16[128,256]{1,0:T(8,128)(2,1)S(1)}, bf16[128,256]{1,0:T(8,128)(2,1)S(1)}, u32[]{:S(2)}, u32[]{:S(2)}) collective-permute-start(bf16[128,256]{1,0:T(8,128)(2,1)S(1)} %get-tuple-element.23), channel_id=1, source_target_pairs={{0,8},{4,12},{8,0},{12,4},{1,9},{5,13},{9,1},{13,5},{2,10},{6,14},... | collective-permute-start | bytes 196616 | tf_op jit(solution)/shard_map/ppermute | solution.py:233
  51.8 0.0 collective-permute-start.17
  51.8 1.6 %collective-permute-done.15.refs_0_ = bf16[128,256]{1,0:T(8,128)(2,1)S(1)} collective-permute-done((bf16[128,256]{1,0:T(8,128)(2,1)S(1)}, bf16[128,256]{1,0:T(8,128)(2,1)S(1)}, u32[]{:S(2)}, u32[]{:S(2)}) %collective-permute-start.15) | collective-permute-done | bytes 65568 | tf_op jit(solution)/shard_map/ppermute | solution.py:233
  53.4 4.0 %collective-permute-done.16.refs_1_ = bf16[128,256]{1,0:T(8,128)(2,1)S(1)} collective-permute-done((bf16[128,256]{1,0:T(8,128)(2,1)S(1)}, bf16[128,256]{1,0:T(8,128)(2,1)S(1)}, u32[]{:S(2)}, u32[]{:S(2)}) %collective-permute-start.16) | collective-permute-done | bytes 65568 | tf_op jit(solution)/shard_map/ppermute | solution.py:233
  57.4 0.0 collective-permute-done.17.refs_2_
  57.4 0.0 copy-done.14
  57.4 1.3 %unpack.1 = f32[256,256]{1,0:T(8,128)} custom-call(s32[1]{0:T(128)} %bitcast.1.me_ref, s32[1,256]{1,0:T(1,128)S(1)} %bitcast.6, bf16[128,256]{1,0:T(8,128)(2,1)S(1)} %collective-permute-done.15.refs_0_, bf16[128,256]{1,0:T(8,128)(2,1)S(1)} %collective-permute-done.16.refs_1_, bf16[128,256]{1,0:T(8,128)(2,1)S(1)} %collective-permute-done.17.refs_2_, ...), custom_call_target="tpu_custom_call" | custom-call | flops 1 | bytes 1 | tf_op jit(solution)/shard_map/unpack/pallas_call | solution.py:338
  (6 shorter events, 0.0 us)
Async XLA Ops:
  2.2 34.6 %copy-start = (bf16[192,1024]{1,0:T(8,128)(2,1)}, bf16[192,1024]{1,0:T(8,128)(2,1)S(1)}, u32[]{:S(2)}) copy-start(bf16[192,1024]{1,0:T(8,128)(2,1)S(1)} %get-tuple-element.15.refs_0_.refs_1_) | copy-start | bytes 1179652
  2.2 14.9 %collective-permute-start.3 = (bf16[128,1024]{1,0:T(8,128)(2,1)S(1)}, bf16[128,1024]{1,0:T(8,128)(2,1)S(1)}, u32[]{:S(2)}, u32[]{:S(2)}) collective-permute-start(bf16[128,1024]{1,0:T(8,128)(2,1)S(1)} %get-tuple-element.16), channel_id=1, source_target_pairs={{0,4},{4,0},{8,12},{12,8},{1,5},{5,1},{9,13},{13,9},{2,6},{6,2},{1... | collective-permute-start | bytes 786440 | tf_op jit(solution)/shard_map/ppermute | solution.py:233
  5.3 14.3 %collective-permute-start.7 = (bf16[128,1024]{1,0:T(8,128)(2,1)S(1)}, bf16[128,1024]{1,0:T(8,128)(2,1)S(1)}, u32[]{:S(2)}, u32[]{:S(2)}) collective-permute-start(bf16[128,1024]{1,0:T(8,128)(2,1)S(1)} %get-tuple-element.17), channel_id=1, source_target_pairs={{0,8},{4,12},{8,0},{12,4},{1,9},{5,13},{9,1},{13,5},{2,10},{6,14},... | collective-permute-start | bytes 786440 | tf_op jit(solution)/shard_map/ppermute | solution.py:233
  7.9 15.7 %collective-permute-start = (bf16[192,1024]{1,0:T(8,128)(2,1)S(1)}, bf16[192,1024]{1,0:T(8,128)(2,1)S(1)}, u32[]{:S(2)}, u32[]{:S(2)}) collective-permute-start(bf16[192,1024]{1,0:T(8,128)(2,1)S(1)} %get-tuple-element.15.refs_0_.refs_1_), channel_id=1, source_target_pairs={{0,2},{1,3},{2,0},{3,1},{4,6},{5,7},{6,4},{7,5},{8,10},{9,11},{10,... | collective-permute-start | bytes 1179656 | tf_op jit(solution)/shard_map/ppermute | solution.py:233
  17.1 19.7 %copy-start.4 = (bf16[128,1024]{1,0:T(8,128)(2,1)}, bf16[128,1024]{1,0:T(8,128)(2,1)S(1)}, u32[]{:S(2)}) copy-start(bf16[128,1024]{1,0:T(8,128)(2,1)S(1)} %collective-permute-done.3.refs_4_.refs_5_) | copy-start | bytes 786436
  17.1 8.0 %collective-permute-start.5 = (bf16[128,1024]{1,0:T(8,128)(2,1)S(1)}, bf16[128,1024]{1,0:T(8,128)(2,1)S(1)}, u32[]{:S(2)}, u32[]{:S(2)}) collective-permute-start(bf16[128,1024]{1,0:T(8,128)(2,1)S(1)} %collective-permute-done.3.refs_4_.refs_5_), channel_id=1, source_target_pairs={{0,2},{1,3},{2,0},{3,1},{4,6},{5,7},{6,4},{7,5},{8,10},{9,11},{10,... | collective-permute-start | bytes 786440 | tf_op jit(solution)/shard_map/ppermute | solution.py:233
  18.8 6.3 %collective-permute-start.4 = (bf16[128,1024]{1,0:T(8,128)(2,1)S(1)}, bf16[128,1024]{1,0:T(8,128)(2,1)S(1)}, u32[]{:S(2)}, u32[]{:S(2)}) collective-permute-start(bf16[128,1024]{1,0:T(8,128)(2,1)S(1)} %collective-permute-done.3.refs_4_.refs_5_), channel_id=1, source_target_pairs={{0,1},{1,0},{2,3},{3,2},{4,5},{5,4},{6,7},{7,6},{8,9},{9,8},{10,11... | collective-permute-start | bytes 786440 | tf_op jit(solution)/shard_map/ppermute | solution.py:233
  19.6 17.2 %copy-start.5 = (bf16[128,1024]{1,0:T(8,128)(2,1)}, bf16[128,1024]{1,0:T(8,128)(2,1)S(1)}, u32[]{:S(2)}) copy-start(bf16[128,1024]{1,0:T(8,128)(2,1)S(1)} %collective-permute-done.7.refs_8_.refs_9_) | copy-start | bytes 786436
  19.6 9.8 %collective-permute-start.11 = (bf16[128,1024]{1,0:T(8,128)(2,1)S(1)}, bf16[128,1024]{1,0:T(8,128)(2,1)S(1)}, u32[]{:S(2)}, u32[]{:S(2)}) collective-permute-start(bf16[128,1024]{1,0:T(8,128)(2,1)S(1)} %get-tuple-element.19), channel_id=1, source_target_pairs={{0,12},{4,8},{8,4},{12,0},{1,13},{5,9},{9,5},{13,1},{2,14},{6,10},... | collective-permute-start | bytes 786440 | tf_op jit(solution)/shard_map/ppermute | solution.py:233
  22.1 8.1 %collective-permute-start.9 = (bf16[128,1024]{1,0:T(8,128)(2,1)S(1)}, bf16[128,1024]{1,0:T(8,128)(2,1)S(1)}, u32[]{:S(2)}, u32[]{:S(2)}) collective-permute-start(bf16[128,1024]{1,0:T(8,128)(2,1)S(1)} %collective-permute-done.7.refs_8_.refs_9_), channel_id=1, source_target_pairs={{0,2},{1,3},{2,0},{3,1},{4,6},{5,7},{6,4},{7,5},{8,10},{9,11},{10,... | collective-permute-start | bytes 786440 | tf_op jit(solution)/shard_map/ppermute | solution.py:233
  23.6 13.3 %copy-start.1 = (bf16[192,1024]{1,0:T(8,128)(2,1)}, bf16[192,1024]{1,0:T(8,128)(2,1)S(1)}, u32[]{:S(2)}) copy-start(bf16[192,1024]{1,0:T(8,128)(2,1)S(1)} %collective-permute-done.refs_2_.refs_3_) | copy-start | bytes 1179652
  23.6 6.6 %collective-permute-start.8 = (bf16[128,1024]{1,0:T(8,128)(2,1)S(1)}, bf16[128,1024]{1,0:T(8,128)(2,1)S(1)}, u32[]{:S(2)}, u32[]{:S(2)}) collective-permute-start(bf16[128,1024]{1,0:T(8,128)(2,1)S(1)} %collective-permute-done.7.refs_8_.refs_9_), channel_id=1, source_target_pairs={{0,1},{1,0},{2,3},{3,2},{4,5},{5,4},{6,7},{7,6},{8,9},{9,8},{10,11... | collective-permute-start | bytes 786440 | tf_op jit(solution)/shard_map/ppermute | solution.py:233
  25.1 11.8 %copy-start.6 = (bf16[128,1024]{1,0:T(8,128)(2,1)}, bf16[128,1024]{1,0:T(8,128)(2,1)S(1)}, u32[]{:S(2)}) copy-start(bf16[128,1024]{1,0:T(8,128)(2,1)S(1)} %collective-permute-done.5.refs_6_.refs_7_) | copy-start | bytes 786436
  25.1 5.7 %collective-permute-start.6 = (bf16[128,1024]{1,0:T(8,128)(2,1)S(1)}, bf16[128,1024]{1,0:T(8,128)(2,1)S(1)}, u32[]{:S(2)}, u32[]{:S(2)}) collective-permute-start(bf16[128,1024]{1,0:T(8,128)(2,1)S(1)} %collective-permute-done.5.refs_6_.refs_7_), channel_id=1, source_target_pairs={{0,1},{1,0},{2,3},{3,2},{4,5},{5,4},{6,7},{7,6},{8,9},{9,8},{10,11... | collective-permute-start | bytes 786440 | tf_op jit(solution)/shard_map/ppermute | solution.py:233
  25.1 11.8 %copy-start.7 = (bf16[128,1024]{1,0:T(8,128)(2,1)}, bf16[128,1024]{1,0:T(8,128)(2,1)S(1)}, u32[]{:S(2)}) copy-start(bf16[128,1024]{1,0:T(8,128)(2,1)S(1)} %collective-permute-done.4.refs_5_.refs_6_) | copy-start | bytes 786436
  25.1 7.1 %collective-permute-start.1 = (bf16[192,1024]{1,0:T(8,128)(2,1)S(1)}, bf16[192,1024]{1,0:T(8,128)(2,1)S(1)}, u32[]{:S(2)}, u32[]{:S(2)}) collective-permute-start(bf16[192,1024]{1,0:T(8,128)(2,1)S(1)} %get-tuple-element.15.refs_0_.refs_1_), channel_id=1, source_target_pairs={{0,1},{1,0},{2,3},{3,2},{4,5},{5,4},{6,7},{7,6},{8,9},{9,8},{10,11... | collective-permute-start | bytes 1179656 | tf_op jit(solution)/shard_map/ppermute | solution.py:233
  29.4 7.5 %copy-start.8 = (bf16[128,1024]{1,0:T(8,128)(2,1)}, bf16[128,1024]{1,0:T(8,128)(2,1)S(1)}, u32[]{:S(2)}) copy-start(bf16[128,1024]{1,0:T(8,128)(2,1)S(1)} %collective-permute-done.11.refs_12_.refs_13_) | copy-start | bytes 786436
  29.4 2.7 %collective-permute-start.2 = (bf16[192,1024]{1,0:T(8,128)(2,1)S(1)}, bf16[192,1024]{1,0:T(8,128)(2,1)S(1)}, u32[]{:S(2)}, u32[]{:S(2)}) collective-permute-start(bf16[192,1024]{1,0:T(8,128)(2,1)S(1)} %collective-permute-done.refs_2_.refs_3_), channel_id=1, source_target_pairs={{0,1},{1,0},{2,3},{3,2},{4,5},{5,4},{6,7},{7,6},{8,9},{9,8},{10,11... | collective-permute-start | bytes 1179656 | tf_op jit(solution)/shard_map/ppermute | solution.py:233
  30.2 6.7 %copy-start.9 = (bf16[128,1024]{1,0:T(8,128)(2,1)}, bf16[128,1024]{1,0:T(8,128)(2,1)S(1)}, u32[]{:S(2)}) copy-start(bf16[128,1024]{1,0:T(8,128)(2,1)S(1)} %collective-permute-done.9.refs_10_.refs_11_) | copy-start | bytes 786436
  30.2 1.9 %collective-permute-start.12 = (bf16[128,1024]{1,0:T(8,128)(2,1)S(1)}, bf16[128,1024]{1,0:T(8,128)(2,1)S(1)}, u32[]{:S(2)}, u32[]{:S(2)}) collective-permute-start(bf16[128,1024]{1,0:T(8,128)(2,1)S(1)} %collective-permute-done.11.refs_12_.refs_13_), channel_id=1, source_target_pairs={{0,1},{1,0},{2,3},{3,2},{4,5},{5,4},{6,7},{7,6},{8,9},{9,8},{10,11... | collective-permute-start | bytes 786440 | tf_op jit(solution)/shard_map/ppermute | solution.py:233
  30.2 6.7 %copy-start.10 = (bf16[128,1024]{1,0:T(8,128)(2,1)}, bf16[128,1024]{1,0:T(8,128)(2,1)S(1)}, u32[]{:S(2)}) copy-start(bf16[128,1024]{1,0:T(8,128)(2,1)S(1)} %collective-permute-done.8.refs_9_.refs_10_) | copy-start | bytes 786436
  30.2 1.9 %collective-permute-start.10 = (bf16[128,1024]{1,0:T(8,128)(2,1)S(1)}, bf16[128,1024]{1,0:T(8,128)(2,1)S(1)}, u32[]{:S(2)}, u32[]{:S(2)}) collective-permute-start(bf16[128,1024]{1,0:T(8,128)(2,1)S(1)} %collective-permute-done.9.refs_10_.refs_11_), channel_id=1, source_target_pairs={{0,1},{1,0},{2,3},{3,2},{4,5},{5,4},{6,7},{7,6},{8,9},{9,8},{10,11... | collective-permute-start | bytes 786440 | tf_op jit(solution)/shard_map/ppermute | solution.py:233
  30.7 6.2 %copy-start.11 = (bf16[128,1024]{1,0:T(8,128)(2,1)}, bf16[128,1024]{1,0:T(8,128)(2,1)S(1)}, u32[]{:S(2)}) copy-start(bf16[128,1024]{1,0:T(8,128)(2,1)S(1)} %collective-permute-done.6.refs_7_.refs_8_) | copy-start | bytes 786436
  30.7 8.4 %collective-permute-start.13 = (bf16[128,1024]{1,0:T(8,128)(2,1)S(1)}, bf16[128,1024]{1,0:T(8,128)(2,1)}, u32[]{:S(2)}, u32[]{:S(2)}) collective-permute-start(bf16[128,1024]{1,0:T(8,128)(2,1)S(1)} %collective-permute-done.11.refs_12_.refs_13_), channel_id=1, source_target_pairs={{0,2},{1,3},{2,0},{3,1},{4,6},{5,7},{6,4},{7,5},{8,10},{9,11},{10,... | collective-permute-start | bytes 786440 | tf_op jit(solution)/shard_map/ppermute | solution.py:233
  32.1 4.8 %copy-start.12 = (bf16[128,1024]{1,0:T(8,128)(2,1)}, bf16[128,1024]{1,0:T(8,128)(2,1)S(1)}, u32[]{:S(2)}) copy-start(bf16[128,1024]{1,0:T(8,128)(2,1)S(1)} %collective-permute-done.12.refs_13_.refs_14_) | copy-start | bytes 786436
  32.1 4.8 %copy-start.13 = (bf16[128,1024]{1,0:T(8,128)(2,1)}, bf16[128,1024]{1,0:T(8,128)(2,1)S(1)}, u32[]{:S(2)}) copy-start(bf16[128,1024]{1,0:T(8,128)(2,1)S(1)} %collective-permute-done.10.refs_11_.refs_12_) | copy-start | bytes 786436
  32.1 4.8 %copy-start.2 = (bf16[192,1024]{1,0:T(8,128)(2,1)}, bf16[192,1024]{1,0:T(8,128)(2,1)S(1)}, u32[]{:S(2)}) copy-start(bf16[192,1024]{1,0:T(8,128)(2,1)S(1)} %collective-permute-done.1.refs_1_.refs_2_) | copy-start | bytes 1179652
  32.1 4.8 %copy-start.3 = (bf16[192,1024]{1,0:T(8,128)(2,1)}, bf16[192,1024]{1,0:T(8,128)(2,1)S(1)}, u32[]{:S(2)}) copy-start(bf16[192,1024]{1,0:T(8,128)(2,1)S(1)} %collective-permute-done.2.refs_3_.refs_4_) | copy-start | bytes 1179652
  39.1 1.7 %collective-permute-start.14 = (bf16[128,1024]{1,0:T(8,128)(2,1)}, bf16[128,1024]{1,0:T(8,128)(2,1)S(1)}, u32[]{:S(2)}, u32[]{:S(2)}) collective-permute-start(bf16[128,1024]{1,0:T(8,128)(2,1)} %collective-permute-done.13.refs_15_), channel_id=1, source_target_pairs={{0,1},{1,0},{2,3},{3,2},{4,5},{5,4},{6,7},{7,6},{8,9},{9,8},{10,11... | collective-permute-start | bytes 786440 | tf_op jit(solution)/shard_map/ppermute | solution.py:233
  40.9 16.5 %copy-start.14 = (s32[256]{0:T(256)S(1)}, s32[256]{0:T(256)}, u32[]{:S(2)}) copy-start(s32[256]{0:T(256)} %param.4) | copy-start | bytes 3076
  47.2 6.2 %collective-permute-start.15 = (bf16[128,256]{1,0:T(8,128)(2,1)S(1)}, bf16[128,256]{1,0:T(8,128)(2,1)S(1)}, u32[]{:S(2)}, u32[]{:S(2)}) collective-permute-start(bf16[128,256]{1,0:T(8,128)(2,1)S(1)} %get-tuple-element.22), channel_id=1, source_target_pairs={{0,12},{4,8},{8,4},{12,0},{1,13},{5,9},{9,5},{13,1},{2,14},{6,10},... | collective-permute-start | bytes 196616 | tf_op jit(solution)/shard_map/ppermute | solution.py:233
  49.6 7.8 %collective-permute-start.16 = (bf16[128,256]{1,0:T(8,128)(2,1)S(1)}, bf16[128,256]{1,0:T(8,128)(2,1)S(1)}, u32[]{:S(2)}, u32[]{:S(2)}) collective-permute-start(bf16[128,256]{1,0:T(8,128)(2,1)S(1)} %get-tuple-element.23), channel_id=1, source_target_pairs={{0,8},{4,12},{8,0},{12,4},{1,9},{5,13},{9,1},{13,5},{2,10},{6,14},... | collective-permute-start | bytes 196616 | tf_op jit(solution)/shard_map/ppermute | solution.py:233
  51.8 5.6 %collective-permute-start.17 = (bf16[128,256]{1,0:T(8,128)(2,1)S(1)}, bf16[128,256]{1,0:T(8,128)(2,1)S(1)}, u32[]{:S(2)}, u32[]{:S(2)}) collective-permute-start(bf16[128,256]{1,0:T(8,128)(2,1)S(1)} %get-tuple-element.24), channel_id=1, source_target_pairs={{0,4},{4,0},{8,12},{12,8},{1,5},{5,1},{9,13},{13,9},{2,6},{6,2},{1... | collective-permute-start | bytes 196616 | tf_op jit(solution)/shard_map/ppermute | solution.py:233

commit v5 on v4

--- a/solution.py
+++ b/solution.py
@@ -28,16 +28,20 @@
     return lax.dot_general(a, b, dims, preferred_element_type=F32)
 
 
-def slots_of(me, cluster, depth, owners):
-    count = cluster.shape[1]
-    height = max(16, owners)
-    offset = jnp.bitwise_xor(cluster, me)
-    member = lax.broadcasted_iota(jnp.int32, (height, count), 0) == offset
+def precedes(count):
     earlier = lax.broadcasted_iota(jnp.int32, (count, count), 0) < lax.broadcasted_iota(
         jnp.int32, (count, count), 1
     )
+    return jnp.where(earlier, 1.0, 0.0).astype(BF)
+
+
+def slots_of(cluster, earlier, depth, owners):
+    count = cluster.shape[1]
+    height = max(16, owners)
+    offset = jnp.bitwise_xor(cluster, lax.axis_index("own").astype(jnp.int32))
+    member = lax.broadcasted_iota(jnp.int32, (height, count), 0) == offset
     member = jnp.where(member, 1.0, 0.0)
-    before = matmul(member.astype(BF), jnp.where(earlier, 1.0, 0.0).astype(BF), NN)
+    before = matmul(member.astype(BF), earlier, NN)
     rank = jnp.sum(before * member, axis=0, keepdims=True).astype(jnp.int32)
     return offset * depth + rank, jnp.sum(member, axis=1, keepdims=True)
 
@@ -58,15 +62,16 @@
         copy.wait()
 
 
-def pack_kernel(depth, owners, me_ref, cluster_hbm, points_hbm, centres_hbm, *refs):
+def pack_kernel(depth, owners, cluster_hbm, points_hbm, centres_hbm, *refs):
     *outs, cluster_ref, points_ref, arrived = refs
     names = pltpu.make_async_copy(cluster_hbm, cluster_ref, arrived.at[1])
     names.start()
     points = fetch([points_hbm], points_ref, arrived)
     height = outs[-1].shape[0]
     centres = fetch([centres_hbm], outs[0].at[height:], arrived.at[2:])
+    earlier = precedes(cluster_ref.shape[1])
     names.wait()
-    slot, tally = slots_of(me_ref[0], cluster_ref[...], depth, owners)
+    slot, tally = slots_of(cluster_ref[...], earlier, depth, owners)
     settle(points)
     points = points_ref[...]
     per = height // depth
@@ -82,18 +87,20 @@
     settle(centres)
 
 
-def unpack_kernel(depth, owners, me_ref, cluster_ref, *refs):
+def places_kernel(depth, owners, cluster_ref, out):
+    count, slots = out.shape
+    slot, _ = slots_of(cluster_ref[...], precedes(count), depth, owners)
+    column = jnp.broadcast_to(slot.astype(F32), (128, count)).T[:, 0:1].astype(jnp.int32)
+    lanes = lax.broadcasted_iota(jnp.int32, (count, slots), 1)
+    out[...] = jnp.where(lanes == column, 1.0, 0.0).astype(BF)
+
+
+def unpack_kernel(places_ref, *refs):
     *logs, out = refs
-    logs = logs[::-1]
-    slot, _ = slots_of(me_ref[0], cluster_ref[...], depth, owners)
-    count = slot.shape[1]
-    column = jnp.broadcast_to(slot.astype(F32), (128, count)).T[:, 0:1].astype(jnp.int32)
     height = logs[0].shape[0]
     total = None
-    for g, block in enumerate(logs):
-        lanes = lax.broadcasted_iota(jnp.int32, (count, height), 1) + g * height
-        pick = jnp.where(lanes == column, 1.0, 0.0).astype(BF)
-        term = matmul(pick, block[...], NN)
+    for g, block in enumerate(logs[::-1]):
+        term = matmul(places_ref[:, g * height : (g + 1) * height], block[...], NN)
         total = term if total is None else total + term
     out[...] = total
 
@@ -154,40 +161,47 @@
     settle(fetch([state_ref], out, kept))
 
 
-def refine(centres, state_ref):
+def refine(centres, *states):
     width = centres.shape[1]
-    mass = state_ref[:, width : width + 1]
-    return (state_ref[:, :width] + prior_count * centres.astype(F32)) / (mass + prior_count)
-
-
-def last_kernel(helpers, counts, share_rows, helper_ref, *refs):
+    sums = prior_count * centres.astype(F32)
+    mass = prior_count
+    for state_ref in states:
+        sums = sums + state_ref[:, :width]
+        mass = mass + state_ref[:, width : width + 1]
+    return sums / mass
+
+
+def last_kernel(helpers, counts, share_rows, *refs):
     earlier, late, own = counts
     old, refs = refs[:1], refs[1:]
     given, refs = refs[: earlier + late], refs[earlier + late :]
     refined_ref, logs, refs = refs[0], refs[1 : 1 + own], refs[1 + own :]
-    state_ref, ordered, share_ref, rows, arrived, ready, kept = refs
+    state_ref, ordered, share_ref, rows, old_ref, whole_ref, arrived, ready, kept = refs
     height = given[-1].shape[0]
     held = earlier * height
     centres = fetch([ref.at[height:] for ref in given[:helpers]], ordered, ready)
     given = [ref.at[:height] for ref in given]
     later = fetch(given[earlier:], rows.at[held:], arrived.at[earlier:])
-    state = fetch(old, state_ref, kept)
+    state = fetch(old, old_ref, kept)
     sooner = fetch(given[:earlier], rows, arrived)
-    helper = helper_ref[0]
+    helper = lax.axis_index("hlp").astype(jnp.int32)
     settle(centres)
     centres = ordered[...]
     norms = square_norms(centres)
     turned = centres.T
-    settle(later + state)
-    accumulate(turned, norms, tiles_of(rows, held, rows.shape[0]), share_ref, state_ref, False)
-    settle(sooner)
+    settle(later)
+    accumulate(turned, norms, tiles_of(rows, held, rows.shape[0]), share_ref, state_ref, True)
+    settle(state + sooner)
+    states = (state_ref, old_ref)
     for turn in range(1, ITERS):
-        centres = refine(centres, state_ref).astype(BF)
+        centres = refine(centres, *states).astype(BF)
+        states = (state_ref,)
         norms = square_norms(centres)
         turned = centres.T
         accumulate(turned, norms, tiles_of(rows, 0, rows.shape[0]), share_ref, state_ref, True)
-    refined = refine(centres, state_ref)
-    refined_ref[...] = refined[0:share_rows]
+    refined = refine(centres, *states)
+    whole_ref[...] = refined[0:share_rows]
+    written = fetch([whole_ref], refined_ref, kept)
     centres = refined.astype(BF)
     for j in range(helpers):
         place = pl.multiple_of(jnp.bitwise_xor(helper, j) * share_rows, share_rows)
@@ -204,13 +218,13 @@
         result = (logits - (top + total)).astype(BF)
         for i in range(pair):
             logs[g + i][...] = result[i * height : (i + 1) * height]
+    settle(written)
 
 
 def vmem(n):
     return [pl.BlockSpec(memory_space=pltpu.VMEM)] * n
 
 
-SMEM = pl.BlockSpec(memory_space=pltpu.SMEM)
 HBM = pl.BlockSpec(memory_space=pltpu.HBM)
 COST = pl.CostEstimate(flops=1, bytes_accessed=1, transcendentals=0)
 
@@ -244,15 +258,13 @@
     per = owners // groups
     height = per * depth
 
-    me = lax.axis_index("own").astype(jnp.int32).reshape(1)
-    helper = lax.axis_index("hlp").astype(jnp.int32).reshape(1)
     cluster = cluster_of.reshape(1, count)
 
     blocks = [jax.ShapeDtypeStruct((height + (0 if g else share_rows), width), BF) for g in range(groups)]
     packed = pl.pallas_call(
         functools.partial(pack_kernel, depth, owners),
         out_shape=blocks,
-        in_specs=[SMEM] + [HBM] * 3,
+        in_specs=[HBM] * 3,
         out_specs=vmem(groups),
         scratch_shapes=[
             pltpu.VMEM(cluster.shape, jnp.int32),
@@ -262,7 +274,7 @@
         compiler_params=params(points, *blocks),
         cost_estimate=COST,
         name="pack",
-    )(me, in_hbm(cluster), in_hbm(points), in_hbm(subcentroids[0]))
+    )(in_hbm(cluster), in_hbm(points), in_hbm(subcentroids[0]))
 
     def across(block, g):
         if per == 1:
@@ -320,30 +332,40 @@
     earlier = given
     logs = [jax.ShapeDtypeStruct((height, subs), BF)] * groups
     refined = jax.ShapeDtypeStruct((share_rows, width), F32)
-    own = scratch(len(earlier) + len(late))
+    own = scratch(len(earlier) + len(late)) + [state, refined]
     refined, *logs = pl.pallas_call(
         functools.partial(last_kernel, helpers, (len(earlier), len(late), groups), share_rows),
         out_shape=[refined] + logs,
-        in_specs=[SMEM] + [HBM] * (1 + len(earlier) + len(late)),
-        out_specs=vmem(1 + groups),
+        in_specs=[HBM] * (1 + len(earlier) + len(late)),
+        out_specs=[HBM] + vmem(groups),
         scratch_shapes=[pltpu.VMEM(s.shape, s.dtype) for s in own]
         + semaphores(len(earlier) + len(late), helpers, 1),
-        compiler_params=params(*own, refined, *logs),
+        compiler_params=params(*own, *logs),
         cost_estimate=COST,
         name="rounds",
-    )(helper, sofar, *[in_hbm(r) for r in earlier], *late)
+    )(sofar, *[in_hbm(r) for r in earlier], *late)
 
     back = [across(logs[g], g) for g in reversed(range(groups))]
+    places = jax.ShapeDtypeStruct((count, groups * height), BF)
     out = jax.ShapeDtypeStruct((count, subs), F32)
+    where = pl.pallas_call(
+        functools.partial(places_kernel, depth, owners),
+        out_shape=places,
+        in_specs=vmem(1),
+        out_specs=pl.BlockSpec(memory_space=pltpu.VMEM),
+        compiler_params=params(places),
+        cost_estimate=COST,
+        name="places",
+    )(after(cluster, refined))
     log_resp = pl.pallas_call(
-        functools.partial(unpack_kernel, depth, owners),
+        unpack_kernel,
         out_shape=out,
-        in_specs=[SMEM] + vmem(1 + groups),
+        in_specs=vmem(1 + groups),
         out_specs=pl.BlockSpec(memory_space=pltpu.VMEM),
-        compiler_params=params(*back, out),
+        compiler_params=params(places, *back, out),
         cost_estimate=COST,
         name="unpack",
-    )(me, cluster, *back)
+    )(where, *back)
     return (refined[None], log_resp)
 
 

time: 58.9 us -> 58.2 us (0.988)
  waiting for transfers between devices: 24.3 us -> 23.6 us
    ppermute x18, waiting for transfers between devices: 24.3 us -> 23.6 us  [hop(): return lambda x: lax.ppermute(x, axis, pairs)]
    pallas_call x1 -> x2, Pallas kernels: 1.31 us -> 1.34 us  [the longest x1 0.99 us: per_device(): pl.pallas_call(unpack_kernel, out_shape=out, in_specs=vmem(1 + groups), o...]
  transfers between devices with their start and end apart: 18 -> 18, of which waited for: 9 -> 9; matrix products, arithmetic and copies ran while one was open for 0% -> 0% of each run, Pallas kernels for 8% -> 9%
where the time goes in v5:
time: 58.2 us; the launch traced here: 58 us
  waiting for transfers between devices  23.6 us (41%)
  starting transfers between devices  19.7 us (34%)
  Pallas kernels  13.8 us (24%)
  between operations  0.85 us (1%)
    ppermute x18, waiting for transfers between devices, hop(): return lambda x: lax.ppermute(x, axis, pairs)  23.6 us
    ppermute x18, starting transfers between devices, hop(): return lambda x: lax.ppermute(x, axis, pairs)  19.7 us
    pallas_call x1, Pallas kernels, per_device(): pl.pallas_call(functools.partial(last_kernel, helpers, (len(earlier), len...  6.27 us
    pallas_call x1, Pallas kernels, per_device(): pl.pallas_call(functools.partial(some_kernel, helpers, height), out_shape...  4.67 us
    pallas_call x1, Pallas kernels, per_device(): pl.pallas_call(functools.partial(pack_kernel, depth, owners), out_shape=b...  1.56 us
  transfers between devices with their start and end apart: 18, of which 9 were waited for; matrix products, arithmetic and copies ran while one was open for 0% of the time, Pallas kernels for 9%

profile of v5, /device:TPU:0, one launch (start us, length us, event | category | flops | bytes accessed | tf_op | source)
XLA Modules:
  0.0 58.0 jit_solution(18144310649674527606)
XLA Ops:
  0.6 1.6 %pack.1 = (bf16[192,1024]{1,0:T(8,128)(2,1)S(1)}, bf16[128,1024]{1,0:T(8,128)(2,1)S(1)}, bf16[128,1024]{1,0:T(8,128)(2,1)S(1)}, bf16[128,1024]{1,0:T(8,128)(2,1)S(1)}) custom-call(s32[1,256]{1,0:T(1,128)} %bitcast.3, bf16[256,1024]{1,0:T(8,128)(2,1)} %points_hbm.1, bf16[64,1024]{1,0:T(8,128)(2,1)} %bitcast.5), custom_call_target="tpu_custom_call" | custom-call | flops 1 | bytes 1 | tf_op jit(solution)/shard_map/pack/pallas_call | solution.py:264
  2.2 0.0 copy-start
  2.2 3.1 %collective-permute-start.3 = (bf16[128,1024]{1,0:T(8,128)(2,1)S(1)}, bf16[128,1024]{1,0:T(8,128)(2,1)S(1)}, u32[]{:S(2)}, u32[]{:S(2)}) collective-permute-start(bf16[128,1024]{1,0:T(8,128)(2,1)S(1)} %get-tuple-element.17), channel_id=1, source_target_pairs={{0,4},{4,0},{8,12},{12,8},{1,5},{5,1},{9,13},{13,9},{2,6},{6,2},{1... | collective-permute-start | bytes 786440 | tf_op jit(solution)/shard_map/ppermute | solution.py:247
  5.3 2.6 %collective-permute-start.7 = (bf16[128,1024]{1,0:T(8,128)(2,1)S(1)}, bf16[128,1024]{1,0:T(8,128)(2,1)S(1)}, u32[]{:S(2)}, u32[]{:S(2)}) collective-permute-start(bf16[128,1024]{1,0:T(8,128)(2,1)S(1)} %get-tuple-element.18), channel_id=1, source_target_pairs={{0,8},{4,12},{8,0},{12,4},{1,9},{5,13},{9,1},{13,5},{2,10},{6,14},... | collective-permute-start | bytes 786440 | tf_op jit(solution)/shard_map/ppermute | solution.py:247
  7.9 1.5 %collective-permute-start = (bf16[192,1024]{1,0:T(8,128)(2,1)S(1)}, bf16[192,1024]{1,0:T(8,128)(2,1)S(1)}, u32[]{:S(2)}, u32[]{:S(2)}) collective-permute-start(bf16[192,1024]{1,0:T(8,128)(2,1)S(1)} %get-tuple-element.16.refs_0_.refs_1_), channel_id=1, source_target_pairs={{0,2},{1,3},{2,0},{3,1},{4,6},{5,7},{6,4},{7,5},{8,10},{9,11},{10,... | collective-permute-start | bytes 1179656 | tf_op jit(solution)/shard_map/ppermute | solution.py:247
  9.4 7.7 %collective-permute-done.3.refs_4_.refs_5_ = bf16[128,1024]{1,0:T(8,128)(2,1)S(1)} collective-permute-done((bf16[128,1024]{1,0:T(8,128)(2,1)S(1)}, bf16[128,1024]{1,0:T(8,128)(2,1)S(1)}, u32[]{:S(2)}, u32[]{:S(2)}) %collective-permute-start.3) | collective-permute-done | bytes 262176 | tf_op jit(solution)/shard_map/ppermute | solution.py:247
  17.1 0.0 copy-start.4
  17.1 1.7 %collective-permute-start.5 = (bf16[128,1024]{1,0:T(8,128)(2,1)S(1)}, bf16[128,1024]{1,0:T(8,128)(2,1)S(1)}, u32[]{:S(2)}, u32[]{:S(2)}) collective-permute-start(bf16[128,1024]{1,0:T(8,128)(2,1)S(1)} %collective-permute-done.3.refs_4_.refs_5_), channel_id=1, source_target_pairs={{0,2},{1,3},{2,0},{3,1},{4,6},{5,7},{6,4},{7,5},{8,10},{9,11},{10,... | collective-permute-start | bytes 786440 | tf_op jit(solution)/shard_map/ppermute | solution.py:247
  18.8 0.0 collective-permute-start.4
  18.8 0.9 %collective-permute-done.7.refs_8_.refs_9_ = bf16[128,1024]{1,0:T(8,128)(2,1)S(1)} collective-permute-done((bf16[128,1024]{1,0:T(8,128)(2,1)S(1)}, bf16[128,1024]{1,0:T(8,128)(2,1)S(1)}, u32[]{:S(2)}, u32[]{:S(2)}) %collective-permute-start.7) | collective-permute-done | bytes 262176 | tf_op jit(solution)/shard_map/ppermute | solution.py:247
  19.6 2.5 %collective-permute-start.11 = (bf16[128,1024]{1,0:T(8,128)(2,1)S(1)}, bf16[128,1024]{1,0:T(8,128)(2,1)S(1)}, u32[]{:S(2)}, u32[]{:S(2)}) collective-permute-start(bf16[128,1024]{1,0:T(8,128)(2,1)S(1)} %get-tuple-element.20), channel_id=1, source_target_pairs={{0,12},{4,8},{8,4},{12,0},{1,13},{5,9},{9,5},{13,1},{2,14},{6,10},... | collective-permute-start | bytes 786440 | tf_op jit(solution)/shard_map/ppermute | solution.py:247
  22.1 1.5 %collective-permute-start.9 = (bf16[128,1024]{1,0:T(8,128)(2,1)S(1)}, bf16[128,1024]{1,0:T(8,128)(2,1)S(1)}, u32[]{:S(2)}, u32[]{:S(2)}) collective-permute-start(bf16[128,1024]{1,0:T(8,128)(2,1)S(1)} %collective-permute-done.7.refs_8_.refs_9_), channel_id=1, source_target_pairs={{0,2},{1,3},{2,0},{3,1},{4,6},{5,7},{6,4},{7,5},{8,10},{9,11},{10,... | collective-permute-start | bytes 786440 | tf_op jit(solution)/shard_map/ppermute | solution.py:247
  23.6 0.0 collective-permute-done.refs_2_.refs_3_
  23.6 0.0 copy-start.1
  23.6 0.0 collective-permute-start.8
  23.6 1.4 %collective-permute-done.5.refs_6_.refs_7_ = bf16[128,1024]{1,0:T(8,128)(2,1)S(1)} collective-permute-done((bf16[128,1024]{1,0:T(8,128)(2,1)S(1)}, bf16[128,1024]{1,0:T(8,128)(2,1)S(1)}, u32[]{:S(2)}, u32[]{:S(2)}) %collective-permute-start.5) | collective-permute-done | bytes 262176 | tf_op jit(solution)/shard_map/ppermute | solution.py:247
  25.0 0.0 copy-start.6
  25.0 0.0 collective-permute-start.6
  25.0 0.0 collective-permute-done.4.refs_5_.refs_6_
  25.0 0.0 copy-start.7
  25.1 0.5 collective-permute-start.1
  25.6 3.8 %collective-permute-done.11.refs_12_.refs_13_ = bf16[128,1024]{1,0:T(8,128)(2,1)S(1)} collective-permute-done((bf16[128,1024]{1,0:T(8,128)(2,1)S(1)}, bf16[128,1024]{1,0:T(8,128)(2,1)S(1)}, u32[]{:S(2)}, u32[]{:S(2)}) %collective-permute-start.11) | collective-permute-done | bytes 262176 | tf_op jit(solution)/shard_map/ppermute | solution.py:247
  29.4 0.0 collective-permute-start.2
  29.4 0.8 %collective-permute-done.9.refs_10_.refs_11_ = bf16[128,1024]{1,0:T(8,128)(2,1)S(1)} collective-permute-done((bf16[128,1024]{1,0:T(8,128)(2,1)S(1)}, bf16[128,1024]{1,0:T(8,128)(2,1)S(1)}, u32[]{:S(2)}, u32[]{:S(2)}) %collective-permute-start.9) | collective-permute-done | bytes 262176 | tf_op jit(solution)/shard_map/ppermute | solution.py:247
  30.2 0.0 collective-permute-start.12
  30.2 0.0 collective-permute-done.8.refs_9_.refs_10_
  30.2 0.0 copy-start.10
  30.2 0.5 collective-permute-start.10
  30.7 0.0 collective-permute-done.6.refs_7_.refs_8_
  30.7 1.3 %collective-permute-start.13 = (bf16[128,1024]{1,0:T(8,128)(2,1)S(1)}, bf16[128,1024]{1,0:T(8,128)(2,1)S(1)}, u32[]{:S(2)}, u32[]{:S(2)}) collective-permute-start(bf16[128,1024]{1,0:T(8,128)(2,1)S(1)} %collective-permute-done.11.refs_12_.refs_13_), channel_id=1, source_target_pairs={{0,2},{1,3},{2,0},{3,1},{4,6},{5,7},{6,4},{7,5},{8,10},{9,11},{10,... | collective-permute-start | bytes 786440 | tf_op jit(solution)/shard_map/ppermute | solution.py:247
  32.1 0.0 collective-permute-done.12.refs_13_.refs_14_
  32.1 0.0 collective-permute-done.10.refs_11_.refs_12_
  32.1 0.0 collective-permute-done.1.refs_1_.refs_2_
  32.1 0.0 collective-permute-done.2.refs_3_.refs_4_
  32.1 0.0 copy-start.3
  32.1 4.7 %some_rows.1.refs_0_ = f32[256,1152]{1,0:T(8,128)S(1)} custom-call(bf16[192,1024]{1,0:T(8,128)(2,1)S(1)} %get-tuple-element.16.refs_0_.refs_1_, bf16[192,1024]{1,0:T(8,128)(2,1)S(1)} %collective-permute-done.1.refs_1_.refs_2_, bf16[192,1024]{1,0:T(8,128)(2,1)S(1)} %collective-permute-done.refs_2_.refs_3_, ...), custom_call_target="tpu_custom_call" | custom-call | flops 1 | bytes 1 | tf_op jit(solution)/shard_map/some_rows/pallas_call | solution.py:321
  36.8 0.0 copy-done
  36.8 0.0 copy-done.4
  36.8 0.0 copy-done.5
  36.9 0.0 copy-done.1
  36.9 0.0 copy-done.6
  36.9 0.0 copy-done.7
  36.9 0.0 copy-done.8
  36.9 0.0 copy-done.9
  36.9 0.0 copy-done.10
  36.9 0.0 copy-done.11
  36.9 0.0 copy-done.12
  36.9 0.0 copy-done.13
  36.9 0.0 copy-done.2
  37.0 0.0 copy-done.3
  37.0 0.0 copy-start.14
  37.0 2.0 %collective-permute-done.13.refs_15_ = bf16[128,1024]{1,0:T(8,128)(2,1)S(1)} collective-permute-done((bf16[128,1024]{1,0:T(8,128)(2,1)S(1)}, bf16[128,1024]{1,0:T(8,128)(2,1)S(1)}, u32[]{:S(2)}, u32[]{:S(2)}) %collective-permute-start.13) | collective-permute-done | bytes 262176 | tf_op jit(solution)/shard_map/ppermute | solution.py:247
  39.0 0.0 collective-permute-start.14
  39.0 1.5 %collective-permute-done.14.refs_16_ = bf16[128,1024]{1,0:T(8,128)(2,1)S(1)} collective-permute-done((bf16[128,1024]{1,0:T(8,128)(2,1)S(1)}, bf16[128,1024]{1,0:T(8,128)(2,1)S(1)}, u32[]{:S(2)}, u32[]{:S(2)}) %collective-permute-start.14) | collective-permute-done | bytes 262176 | tf_op jit(solution)/shard_map/ppermute | solution.py:247
  40.6 6.3 %rounds.1 = (f32[64,1024]{1,0:T(8,128)}, bf16[128,256]{1,0:T(8,128)(2,1)S(1)}, bf16[128,256]{1,0:T(8,128)(2,1)S(1)}, bf16[128,256]{1,0:T(8,128)(2,1)S(1)}, bf16[128,256]{1,0:T(8,128)(2,1)S(1)}) custom-call(f32[256,1152]{1,0:T(8,128)S(1)} %some_rows.1.refs_0_, bf16[192,1024]{1,0:T(8,128)(2,1)} %copy-done, bf16[192,1024]{1,0:T(8,128)(2,1)} %copy-done.2, ...), custom_call_target="tpu_custom_call" | custom-call | flops 1 | bytes 1 | tf_op jit(solution)/shard_map/rounds/pallas_call | solution.py:336
  46.8 2.4 %collective-permute-start.15 = (bf16[128,256]{1,0:T(8,128)(2,1)S(1)}, bf16[128,256]{1,0:T(8,128)(2,1)S(1)}, u32[]{:S(2)}, u32[]{:S(2)}) collective-permute-start(bf16[128,256]{1,0:T(8,128)(2,1)S(1)} %get-tuple-element.24), channel_id=1, source_target_pairs={{0,12},{4,8},{8,4},{12,0},{1,13},{5,9},{9,5},{13,1},{2,14},{6,10},... | collective-permute-start | bytes 196616 | tf_op jit(solution)/shard_map/ppermute | solution.py:247
  49.2 2.2 %collective-permute-start.16 = (bf16[128,256]{1,0:T(8,128)(2,1)S(1)}, bf16[128,256]{1,0:T(8,128)(2,1)S(1)}, u32[]{:S(2)}, u32[]{:S(2)}) collective-permute-start(bf16[128,256]{1,0:T(8,128)(2,1)S(1)} %get-tuple-element.25), channel_id=1, source_target_pairs={{0,8},{4,12},{8,0},{12,4},{1,9},{5,13},{9,1},{13,5},{2,10},{6,14},... | collective-permute-start | bytes 196616 | tf_op jit(solution)/shard_map/ppermute | solution.py:247
  51.4 0.0 collective-permute-start.17
  51.4 0.0 copy-done.14
  51.4 0.3 places.1.places_ref
  51.8 1.3 %collective-permute-done.15.refs_0_ = bf16[128,256]{1,0:T(8,128)(2,1)S(1)} collective-permute-done((bf16[128,256]{1,0:T(8,128)(2,1)S(1)}, bf16[128,256]{1,0:T(8,128)(2,1)S(1)}, u32[]{:S(2)}, u32[]{:S(2)}) %collective-permute-start.15) | collective-permute-done | bytes 65568 | tf_op jit(solution)/shard_map/ppermute | solution.py:247
  53.0 4.0 %collective-permute-done.16.refs_1_ = bf16[128,256]{1,0:T(8,128)(2,1)S(1)} collective-permute-done((bf16[128,256]{1,0:T(8,128)(2,1)S(1)}, bf16[128,256]{1,0:T(8,128)(2,1)S(1)}, u32[]{:S(2)}, u32[]{:S(2)}) %collective-permute-start.16) | collective-permute-done | bytes 65568 | tf_op jit(solution)/shard_map/ppermute | solution.py:247
  57.1 0.0 collective-permute-done.17.refs_2_
  57.1 1.0 %unpack.1 = f32[256,256]{1,0:T(8,128)} custom-call(bf16[256,512]{1,0:T(8,128)(2,1)S(1)} %places.1.places_ref, bf16[128,256]{1,0:T(8,128)(2,1)S(1)} %collective-permute-done.15.refs_0_, bf16[128,256]{1,0:T(8,128)(2,1)S(1)} %collective-permute-done.16.refs_1_, bf16[128,256]{1,0:T(8,128)(2,1)S(1)} %collective-permute-done.17.refs_2_, ...), custom_call_target="tpu_custom_call" | custom-call | flops 1 | bytes 1 | tf_op jit(solution)/shard_map/unpack/pallas_call | solution.py:360
  (7 shorter events, 0.0 us)
Async XLA Ops:
  2.2 34.6 %copy-start = (bf16[192,1024]{1,0:T(8,128)(2,1)}, bf16[192,1024]{1,0:T(8,128)(2,1)S(1)}, u32[]{:S(2)}) copy-start(bf16[192,1024]{1,0:T(8,128)(2,1)S(1)} %get-tuple-element.16.refs_0_.refs_1_) | copy-start | bytes 1179652
  2.2 14.9 %collective-permute-start.3 = (bf16[128,1024]{1,0:T(8,128)(2,1)S(1)}, bf16[128,1024]{1,0:T(8,128)(2,1)S(1)}, u32[]{:S(2)}, u32[]{:S(2)}) collective-permute-start(bf16[128,1024]{1,0:T(8,128)(2,1)S(1)} %get-tuple-element.17), channel_id=1, source_target_pairs={{0,4},{4,0},{8,12},{12,8},{1,5},{5,1},{9,13},{13,9},{2,6},{6,2},{1... | collective-permute-start | bytes 786440 | tf_op jit(solution)/shard_map/ppermute | solution.py:247
  5.3 14.3 %collective-permute-start.7 = (bf16[128,1024]{1,0:T(8,128)(2,1)S(1)}, bf16[128,1024]{1,0:T(8,128)(2,1)S(1)}, u32[]{:S(2)}, u32[]{:S(2)}) collective-permute-start(bf16[128,1024]{1,0:T(8,128)(2,1)S(1)} %get-tuple-element.18), channel_id=1, source_target_pairs={{0,8},{4,12},{8,0},{12,4},{1,9},{5,13},{9,1},{13,5},{2,10},{6,14},... | collective-permute-start | bytes 786440 | tf_op jit(solution)/shard_map/ppermute | solution.py:247
  7.9 15.7 %collective-permute-start = (bf16[192,1024]{1,0:T(8,128)(2,1)S(1)}, bf16[192,1024]{1,0:T(8,128)(2,1)S(1)}, u32[]{:S(2)}, u32[]{:S(2)}) collective-permute-start(bf16[192,1024]{1,0:T(8,128)(2,1)S(1)} %get-tuple-element.16.refs_0_.refs_1_), channel_id=1, source_target_pairs={{0,2},{1,3},{2,0},{3,1},{4,6},{5,7},{6,4},{7,5},{8,10},{9,11},{10,... | collective-permute-start | bytes 1179656 | tf_op jit(solution)/shard_map/ppermute | solution.py:247
  17.1 19.7 %copy-start.4 = (bf16[128,1024]{1,0:T(8,128)(2,1)}, bf16[128,1024]{1,0:T(8,128)(2,1)S(1)}, u32[]{:S(2)}) copy-start(bf16[128,1024]{1,0:T(8,128)(2,1)S(1)} %collective-permute-done.3.refs_4_.refs_5_) | copy-start | bytes 786436
  17.1 7.9 %collective-permute-start.5 = (bf16[128,1024]{1,0:T(8,128)(2,1)S(1)}, bf16[128,1024]{1,0:T(8,128)(2,1)S(1)}, u32[]{:S(2)}, u32[]{:S(2)}) collective-permute-start(bf16[128,1024]{1,0:T(8,128)(2,1)S(1)} %collective-permute-done.3.refs_4_.refs_5_), channel_id=1, source_target_pairs={{0,2},{1,3},{2,0},{3,1},{4,6},{5,7},{6,4},{7,5},{8,10},{9,11},{10,... | collective-permute-start | bytes 786440 | tf_op jit(solution)/shard_map/ppermute | solution.py:247
  18.8 6.3 %collective-permute-start.4 = (bf16[128,1024]{1,0:T(8,128)(2,1)S(1)}, bf16[128,1024]{1,0:T(8,128)(2,1)S(1)}, u32[]{:S(2)}, u32[]{:S(2)}) collective-permute-start(bf16[128,1024]{1,0:T(8,128)(2,1)S(1)} %collective-permute-done.3.refs_4_.refs_5_), channel_id=1, source_target_pairs={{0,1},{1,0},{2,3},{3,2},{4,5},{5,4},{6,7},{7,6},{8,9},{9,8},{10,11... | collective-permute-start | bytes 786440 | tf_op jit(solution)/shard_map/ppermute | solution.py:247
  19.6 17.2 %copy-start.5 = (bf16[128,1024]{1,0:T(8,128)(2,1)}, bf16[128,1024]{1,0:T(8,128)(2,1)S(1)}, u32[]{:S(2)}) copy-start(bf16[128,1024]{1,0:T(8,128)(2,1)S(1)} %collective-permute-done.7.refs_8_.refs_9_) | copy-start | bytes 786436
  19.6 9.8 %collective-permute-start.11 = (bf16[128,1024]{1,0:T(8,128)(2,1)S(1)}, bf16[128,1024]{1,0:T(8,128)(2,1)S(1)}, u32[]{:S(2)}, u32[]{:S(2)}) collective-permute-start(bf16[128,1024]{1,0:T(8,128)(2,1)S(1)} %get-tuple-element.20), channel_id=1, source_target_pairs={{0,12},{4,8},{8,4},{12,0},{1,13},{5,9},{9,5},{13,1},{2,14},{6,10},... | collective-permute-start | bytes 786440 | tf_op jit(solution)/shard_map/ppermute | solution.py:247
  22.1 8.1 %collective-permute-start.9 = (bf16[128,1024]{1,0:T(8,128)(2,1)S(1)}, bf16[128,1024]{1,0:T(8,128)(2,1)S(1)}, u32[]{:S(2)}, u32[]{:S(2)}) collective-permute-start(bf16[128,1024]{1,0:T(8,128)(2,1)S(1)} %collective-permute-done.7.refs_8_.refs_9_), channel_id=1, source_target_pairs={{0,2},{1,3},{2,0},{3,1},{4,6},{5,7},{6,4},{7,5},{8,10},{9,11},{10,... | collective-permute-start | bytes 786440 | tf_op jit(solution)/shard_map/ppermute | solution.py:247
  23.6 13.3 %copy-start.1 = (bf16[192,1024]{1,0:T(8,128)(2,1)}, bf16[192,1024]{1,0:T(8,128)(2,1)S(1)}, u32[]{:S(2)}) copy-start(bf16[192,1024]{1,0:T(8,128)(2,1)S(1)} %collective-permute-done.refs_2_.refs_3_) | copy-start | bytes 1179652
  23.6 6.6 %collective-permute-start.8 = (bf16[128,1024]{1,0:T(8,128)(2,1)S(1)}, bf16[128,1024]{1,0:T(8,128)(2,1)S(1)}, u32[]{:S(2)}, u32[]{:S(2)}) collective-permute-start(bf16[128,1024]{1,0:T(8,128)(2,1)S(1)} %collective-permute-done.7.refs_8_.refs_9_), channel_id=1, source_target_pairs={{0,1},{1,0},{2,3},{3,2},{4,5},{5,4},{6,7},{7,6},{8,9},{9,8},{10,11... | collective-permute-start | bytes 786440 | tf_op jit(solution)/shard_map/ppermute | solution.py:247
  25.0 11.8 %copy-start.6 = (bf16[128,1024]{1,0:T(8,128)(2,1)}, bf16[128,1024]{1,0:T(8,128)(2,1)S(1)}, u32[]{:S(2)}) copy-start(bf16[128,1024]{1,0:T(8,128)(2,1)S(1)} %collective-permute-done.5.refs_6_.refs_7_) | copy-start | bytes 786436
  25.0 5.7 %collective-permute-start.6 = (bf16[128,1024]{1,0:T(8,128)(2,1)S(1)}, bf16[128,1024]{1,0:T(8,128)(2,1)S(1)}, u32[]{:S(2)}, u32[]{:S(2)}) collective-permute-start(bf16[128,1024]{1,0:T(8,128)(2,1)S(1)} %collective-permute-done.5.refs_6_.refs_7_), channel_id=1, source_target_pairs={{0,1},{1,0},{2,3},{3,2},{4,5},{5,4},{6,7},{7,6},{8,9},{9,8},{10,11... | collective-permute-start | bytes 786440 | tf_op jit(solution)/shard_map/ppermute | solution.py:247
  25.0 11.8 %copy-start.7 = (bf16[128,1024]{1,0:T(8,128)(2,1)}, bf16[128,1024]{1,0:T(8,128)(2,1)S(1)}, u32[]{:S(2)}) copy-start(bf16[128,1024]{1,0:T(8,128)(2,1)S(1)} %collective-permute-done.4.refs_5_.refs_6_) | copy-start | bytes 786436
  25.1 7.1 %collective-permute-start.1 = (bf16[192,1024]{1,0:T(8,128)(2,1)S(1)}, bf16[192,1024]{1,0:T(8,128)(2,1)S(1)}, u32[]{:S(2)}, u32[]{:S(2)}) collective-permute-start(bf16[192,1024]{1,0:T(8,128)(2,1)S(1)} %get-tuple-element.16.refs_0_.refs_1_), channel_id=1, source_target_pairs={{0,1},{1,0},{2,3},{3,2},{4,5},{5,4},{6,7},{7,6},{8,9},{9,8},{10,11... | collective-permute-start | bytes 1179656 | tf_op jit(solution)/shard_map/ppermute | solution.py:247
  29.4 7.5 %copy-start.8 = (bf16[128,1024]{1,0:T(8,128)(2,1)}, bf16[128,1024]{1,0:T(8,128)(2,1)S(1)}, u32[]{:S(2)}) copy-start(bf16[128,1024]{1,0:T(8,128)(2,1)S(1)} %collective-permute-done.11.refs_12_.refs_13_) | copy-start | bytes 786436
  29.4 2.7 %collective-permute-start.2 = (bf16[192,1024]{1,0:T(8,128)(2,1)S(1)}, bf16[192,1024]{1,0:T(8,128)(2,1)S(1)}, u32[]{:S(2)}, u32[]{:S(2)}) collective-permute-start(bf16[192,1024]{1,0:T(8,128)(2,1)S(1)} %collective-permute-done.refs_2_.refs_3_), channel_id=1, source_target_pairs={{0,1},{1,0},{2,3},{3,2},{4,5},{5,4},{6,7},{7,6},{8,9},{9,8},{10,11... | collective-permute-start | bytes 1179656 | tf_op jit(solution)/shard_map/ppermute | solution.py:247
  30.2 6.7 %copy-start.9 = (bf16[128,1024]{1,0:T(8,128)(2,1)}, bf16[128,1024]{1,0:T(8,128)(2,1)S(1)}, u32[]{:S(2)}) copy-start(bf16[128,1024]{1,0:T(8,128)(2,1)S(1)} %collective-permute-done.9.refs_10_.refs_11_) | copy-start | bytes 786436
  30.2 1.9 %collective-permute-start.12 = (bf16[128,1024]{1,0:T(8,128)(2,1)S(1)}, bf16[128,1024]{1,0:T(8,128)(2,1)S(1)}, u32[]{:S(2)}, u32[]{:S(2)}) collective-permute-start(bf16[128,1024]{1,0:T(8,128)(2,1)S(1)} %collective-permute-done.11.refs_12_.refs_13_), channel_id=1, source_target_pairs={{0,1},{1,0},{2,3},{3,2},{4,5},{5,4},{6,7},{7,6},{8,9},{9,8},{10,11... | collective-permute-start | bytes 786440 | tf_op jit(solution)/shard_map/ppermute | solution.py:247
  30.2 6.7 %copy-start.10 = (bf16[128,1024]{1,0:T(8,128)(2,1)}, bf16[128,1024]{1,0:T(8,128)(2,1)S(1)}, u32[]{:S(2)}) copy-start(bf16[128,1024]{1,0:T(8,128)(2,1)S(1)} %collective-permute-done.8.refs_9_.refs_10_) | copy-start | bytes 786436
  30.2 1.9 %collective-permute-start.10 = (bf16[128,1024]{1,0:T(8,128)(2,1)S(1)}, bf16[128,1024]{1,0:T(8,128)(2,1)S(1)}, u32[]{:S(2)}, u32[]{:S(2)}) collective-permute-start(bf16[128,1024]{1,0:T(8,128)(2,1)S(1)} %collective-permute-done.9.refs_10_.refs_11_), channel_id=1, source_target_pairs={{0,1},{1,0},{2,3},{3,2},{4,5},{5,4},{6,7},{7,6},{8,9},{9,8},{10,11... | collective-permute-start | bytes 786440 | tf_op jit(solution)/shard_map/ppermute | solution.py:247
  30.7 6.2 %copy-start.11 = (bf16[128,1024]{1,0:T(8,128)(2,1)}, bf16[128,1024]{1,0:T(8,128)(2,1)S(1)}, u32[]{:S(2)}) copy-start(bf16[128,1024]{1,0:T(8,128)(2,1)S(1)} %collective-permute-done.6.refs_7_.refs_8_) | copy-start | bytes 786436
  30.7 8.3 %collective-permute-start.13 = (bf16[128,1024]{1,0:T(8,128)(2,1)S(1)}, bf16[128,1024]{1,0:T(8,128)(2,1)S(1)}, u32[]{:S(2)}, u32[]{:S(2)}) collective-permute-start(bf16[128,1024]{1,0:T(8,128)(2,1)S(1)} %collective-permute-done.11.refs_12_.refs_13_), channel_id=1, source_target_pairs={{0,2},{1,3},{2,0},{3,1},{4,6},{5,7},{6,4},{7,5},{8,10},{9,11},{10,... | collective-permute-start | bytes 786440 | tf_op jit(solution)/shard_map/ppermute | solution.py:247
  32.1 4.8 %copy-start.12 = (bf16[128,1024]{1,0:T(8,128)(2,1)}, bf16[128,1024]{1,0:T(8,128)(2,1)S(1)}, u32[]{:S(2)}) copy-start(bf16[128,1024]{1,0:T(8,128)(2,1)S(1)} %collective-permute-done.12.refs_13_.refs_14_) | copy-start | bytes 786436
  32.1 4.8 %copy-start.13 = (bf16[128,1024]{1,0:T(8,128)(2,1)}, bf16[128,1024]{1,0:T(8,128)(2,1)S(1)}, u32[]{:S(2)}) copy-start(bf16[128,1024]{1,0:T(8,128)(2,1)S(1)} %collective-permute-done.10.refs_11_.refs_12_) | copy-start | bytes 786436
  32.1 4.8 %copy-start.2 = (bf16[192,1024]{1,0:T(8,128)(2,1)}, bf16[192,1024]{1,0:T(8,128)(2,1)S(1)}, u32[]{:S(2)}) copy-start(bf16[192,1024]{1,0:T(8,128)(2,1)S(1)} %collective-permute-done.1.refs_1_.refs_2_) | copy-start | bytes 1179652
  32.1 4.8 %copy-start.3 = (bf16[192,1024]{1,0:T(8,128)(2,1)}, bf16[192,1024]{1,0:T(8,128)(2,1)S(1)}, u32[]{:S(2)}) copy-start(bf16[192,1024]{1,0:T(8,128)(2,1)S(1)} %collective-permute-done.2.refs_3_.refs_4_) | copy-start | bytes 1179652
  37.0 14.4 %copy-start.14 = (s32[256]{0:T(256)S(1)}, s32[256]{0:T(256)}, u32[]{:S(2)}) copy-start(s32[256]{0:T(256)} %param.4) | copy-start | bytes 3076
  39.0 1.5 %collective-permute-start.14 = (bf16[128,1024]{1,0:T(8,128)(2,1)S(1)}, bf16[128,1024]{1,0:T(8,128)(2,1)S(1)}, u32[]{:S(2)}, u32[]{:S(2)}) collective-permute-start(bf16[128,1024]{1,0:T(8,128)(2,1)S(1)} %collective-permute-done.13.refs_15_), channel_id=1, source_target_pairs={{0,1},{1,0},{2,3},{3,2},{4,5},{5,4},{6,7},{7,6},{8,9},{9,8},{10,11... | collective-permute-start | bytes 786440 | tf_op jit(solution)/shard_map/ppermute | solution.py:247
  46.8 6.2 %collective-permute-start.15 = (bf16[128,256]{1,0:T(8,128)(2,1)S(1)}, bf16[128,256]{1,0:T(8,128)(2,1)S(1)}, u32[]{:S(2)}, u32[]{:S(2)}) collective-permute-start(bf16[128,256]{1,0:T(8,128)(2,1)S(1)} %get-tuple-element.24), channel_id=1, source_target_pairs={{0,12},{4,8},{8,4},{12,0},{1,13},{5,9},{9,5},{13,1},{2,14},{6,10},... | collective-permute-start | bytes 196616 | tf_op jit(solution)/shard_map/ppermute | solution.py:247
  49.2 7.8 %collective-permute-start.16 = (bf16[128,256]{1,0:T(8,128)(2,1)S(1)}, bf16[128,256]{1,0:T(8,128)(2,1)S(1)}, u32[]{:S(2)}, u32[]{:S(2)}) collective-permute-start(bf16[128,256]{1,0:T(8,128)(2,1)S(1)} %get-tuple-element.25), channel_id=1, source_target_pairs={{0,8},{4,12},{8,0},{12,4},{1,9},{5,13},{9,1},{13,5},{2,10},{6,14},... | collective-permute-start | bytes 196616 | tf_op jit(solution)/shard_map/ppermute | solution.py:247
  51.4 5.7 %collective-permute-start.17 = (bf16[128,256]{1,0:T(8,128)(2,1)S(1)}, bf16[128,256]{1,0:T(8,128)(2,1)S(1)}, u32[]{:S(2)}, u32[]{:S(2)}) collective-permute-start(bf16[128,256]{1,0:T(8,128)(2,1)S(1)} %get-tuple-element.26), channel_id=1, source_target_pairs={{0,4},{4,0},{8,12},{12,8},{1,5},{5,1},{9,13},{13,9},{2,6},{6,2},{1... | collective-permute-start | bytes 196616 | tf_op jit(solution)/shard_map/ppermute | solution.py:247

commit v6 on v5

--- a/solution.py
+++ b/solution.py
@@ -21,6 +21,7 @@
 BF = jnp.bfloat16
 F32 = jnp.float32
 TN = (((0,), (0,)), ((), ()))
+NT = (((1,), (1,)), ((), ()))
 NN = (((1,), (0,)), ((), ()))
 
 
@@ -115,32 +116,32 @@
     return parts[0] if len(parts) == 1 else jnp.concatenate(parts, axis=0)
 
 
-def energies(turned, norms, rows):
-    return matmul(rows, turned, NN) * (2.0 / smoothing_factor) - norms * (1.0 / smoothing_factor)
-
-
-def accumulate(turned, norms, tiles, share_ref, state_ref, fresh):
+def energies(centres, norms, rows):
+    return matmul(rows, centres, NT) * (2.0 / smoothing_factor) - norms * (1.0 / smoothing_factor)
+
+
+def accumulate(centres, norms, tiles, share_ref, state_ref, fresh):
     start = 0
     for rows in tiles:
-        logits = energies(turned, norms, rows)
+        logits = energies(centres, norms, rows)
         top = jnp.max(logits, axis=1, keepdims=True)
         weight = jnp.exp(logits - top)
         live = jnp.where(rows[:, 0:1].astype(F32) < LIMIT, 1.0, 0.0)
         scale = live / jnp.sum(weight, axis=1, keepdims=True)
         share_ref[start : start + rows.shape[0], :] = (weight * scale).astype(BF)
         start += rows.shape[0]
-    width = state_ref.shape[1] - 128
+    subs, width = centres.shape
     start = 0
     for i, rows in enumerate(tiles):
         share = share_ref[start : start + rows.shape[0], :]
         mass = matmul(share, jnp.ones((rows.shape[0], 128), BF), TN)
         part = matmul(share, rows, TN)
         if fresh and i == 0:
-            state_ref[:, width:] = mass
-            state_ref[:, :width] = part
+            state_ref[:subs, width:] = mass
+            state_ref[:subs, :width] = part
         else:
-            state_ref[:, width:] += mass
-            state_ref[:, :width] += part
+            state_ref[:subs, width:] += mass
+            state_ref[:subs, :width] += part
         start += rows.shape[0]
 
 
@@ -155,19 +156,20 @@
     settle(centres)
     centres = centres_ref[...]
     norms = square_norms(centres)
-    turned = centres.T
     settle(copies)
-    accumulate(turned, norms, tiles_of(rows, 0, rows.shape[0]), share_ref, state_ref, True)
+    accumulate(centres, norms, tiles_of(rows, 0, rows.shape[0]), share_ref, state_ref, True)
+    subs = centres.shape[0]
+    state_ref[subs:, :subs] = jnp.broadcast_to(norms, (8, subs))
     settle(fetch([state_ref], out, kept))
 
 
 def refine(centres, *states):
-    width = centres.shape[1]
+    subs, width = centres.shape
     sums = prior_count * centres.astype(F32)
     mass = prior_count
     for state_ref in states:
-        sums = sums + state_ref[:, :width]
-        mass = mass + state_ref[:, width : width + 1]
+        sums = sums + state_ref[:subs, :width]
+        mass = mass + state_ref[:subs, width : width + 1]
     return sums / mass
 
 
@@ -185,20 +187,17 @@
     state = fetch(old, old_ref, kept)
     sooner = fetch(given[:earlier], rows, arrived)
     helper = lax.axis_index("hlp").astype(jnp.int32)
-    settle(centres)
+    settle(centres + state + later)
     centres = ordered[...]
-    norms = square_norms(centres)
-    turned = centres.T
-    settle(later)
-    accumulate(turned, norms, tiles_of(rows, held, rows.shape[0]), share_ref, state_ref, True)
-    settle(state + sooner)
+    norms = old_ref[centres.shape[0] : centres.shape[0] + 1, : centres.shape[0]]
+    accumulate(centres, norms, tiles_of(rows, held, rows.shape[0]), share_ref, state_ref, True)
+    settle(sooner)
     states = (state_ref, old_ref)
     for turn in range(1, ITERS):
         centres = refine(centres, *states).astype(BF)
         states = (state_ref,)
         norms = square_norms(centres)
-        turned = centres.T
-        accumulate(turned, norms, tiles_of(rows, 0, rows.shape[0]), share_ref, state_ref, True)
+        accumulate(centres, norms, tiles_of(rows, 0, rows.shape[0]), share_ref, state_ref, True)
     refined = refine(centres, *states)
     whole_ref[...] = refined[0:share_rows]
     written = fetch([whole_ref], refined_ref, kept)
@@ -208,11 +207,10 @@
         ordered[pl.ds(place, share_rows), :] = centres[j * share_rows : (j + 1) * share_rows]
     centres = ordered[...]
     norms = square_norms(centres)
-    turned = centres.T
     own_rows = [rows[g * helpers * height : g * helpers * height + height, :] for g in range(own)]
     pair = 2 if 2 * height <= TILE and own % 2 == 0 else 1
     for g in range(0, own, pair):
-        logits = energies(turned, norms, joined(own_rows[g : g + pair]))
+        logits = energies(centres, norms, joined(own_rows[g : g + pair]))
         top = jnp.max(logits, axis=1, keepdims=True)
         total = jnp.log(jnp.sum(jnp.exp(logits - top), axis=1, keepdims=True))
         result = (logits - (top + total)).astype(BF)
@@ -294,7 +292,7 @@
     def over_cores(held):
         return [x for block in held for x in (block, hop("hlp", helpers, 1)(block))]
 
-    state = jax.ShapeDtypeStruct((subs, width + 128), F32)
+    state = jax.ShapeDtypeStruct((subs + 8, width + 128), F32)
     centre_table = jax.ShapeDtypeStruct((subs, width), BF)
 
     def scratch(n):
@@ -309,12 +307,12 @@
         return [pltpu.SemaphoreType.DMA((n,)) for n in counts]
 
     beside = hop("hlp", helpers, 1)
-    moved = [packed[0]]
+    moved = [across(packed[0], 0)]
     for g in range(1, groups - 1):
         moved.append(across(packed[g], g))
     moved.append(across(after(packed[-1], moved[-1]) if groups > 1 else packed[-1], groups - 1))
     held = [over_chips(block) for block in moved]
-    own_beside = beside(after(packed[0], held[0][1]))
+    own_beside = beside(after(moved[0], held[0][1]))
     rows = [[moved[0], own_beside] + over_cores(held[0][1:])] + [over_cores(part) for part in held[1:-1]]
     given = [r for part in rows for r in part] + over_cores(held[-1][:1])
     own = scratch(len(given))

time: 58.2 us -> 58 us (level)
  no operation moved by 1% of the time
where the time goes in v6:
time: 58 us; the launch traced here: 57.9 us
  waiting for transfers between devices  23.5 us (41%)
  starting transfers between devices  19.7 us (34%)
  Pallas kernels  13.7 us (24%)
  between operations  0.85 us (1%)
    ppermute x18, waiting for transfers between devices, hop(): return lambda x: lax.ppermute(x, axis, pairs)  23.5 us
    ppermute x18, starting transfers between devices, hop(): return lambda x: lax.ppermute(x, axis, pairs)  19.7 us
    pallas_call x1, Pallas kernels, per_device(): pl.pallas_call(functools.partial(last_kernel, helpers, (len(earlier), len...  6.11 us
    pallas_call x1, Pallas kernels, per_device(): pl.pallas_call(functools.partial(some_kernel, helpers, height), out_shape...  4.72 us
    pallas_call x1, Pallas kernels, per_device(): pl.pallas_call(functools.partial(pack_kernel, depth, owners), out_shape=b...  1.56 us
  transfers between devices with their start and end apart: 18, of which 9 were waited for; matrix products, arithmetic and copies ran while one was open for 0% of the time, Pallas kernels for 9%

profile of v6, /device:TPU:0, one launch (start us, length us, event | category | flops | bytes accessed | tf_op | source)
XLA Modules:
  0.0 57.9 jit_solution(4587337697607696198)
XLA Ops:
  0.6 1.6 %pack.1 = (bf16[192,1024]{1,0:T(8,128)(2,1)S(1)}, bf16[128,1024]{1,0:T(8,128)(2,1)S(1)}, bf16[128,1024]{1,0:T(8,128)(2,1)S(1)}, bf16[128,1024]{1,0:T(8,128)(2,1)S(1)}) custom-call(s32[1,256]{1,0:T(1,128)} %bitcast.3, bf16[256,1024]{1,0:T(8,128)(2,1)} %points_hbm.1, bf16[64,1024]{1,0:T(8,128)(2,1)} %bitcast.5), custom_call_target="tpu_custom_call" | custom-call | flops 1 | bytes 1 | tf_op jit(solution)/shard_map/pack/pallas_call | solution.py:262
  2.2 0.0 copy-start
  2.2 3.1 %collective-permute-start.3 = (bf16[128,1024]{1,0:T(8,128)(2,1)S(1)}, bf16[128,1024]{1,0:T(8,128)(2,1)S(1)}, u32[]{:S(2)}, u32[]{:S(2)}) collective-permute-start(bf16[128,1024]{1,0:T(8,128)(2,1)S(1)} %get-tuple-element.17), channel_id=1, source_target_pairs={{0,4},{4,0},{8,12},{12,8},{1,5},{5,1},{9,13},{13,9},{2,6},{6,2},{1... | collective-permute-start | bytes 786440 | tf_op jit(solution)/shard_map/ppermute | solution.py:245
  5.3 2.6 %collective-permute-start.7 = (bf16[128,1024]{1,0:T(8,128)(2,1)S(1)}, bf16[128,1024]{1,0:T(8,128)(2,1)S(1)}, u32[]{:S(2)}, u32[]{:S(2)}) collective-permute-start(bf16[128,1024]{1,0:T(8,128)(2,1)S(1)} %get-tuple-element.18), channel_id=1, source_target_pairs={{0,8},{4,12},{8,0},{12,4},{1,9},{5,13},{9,1},{13,5},{2,10},{6,14},... | collective-permute-start | bytes 786440 | tf_op jit(solution)/shard_map/ppermute | solution.py:245
  7.9 1.5 %collective-permute-start = (bf16[192,1024]{1,0:T(8,128)(2,1)S(1)}, bf16[192,1024]{1,0:T(8,128)(2,1)S(1)}, u32[]{:S(2)}, u32[]{:S(2)}) collective-permute-start(bf16[192,1024]{1,0:T(8,128)(2,1)S(1)} %get-tuple-element.16.refs_0_.refs_1_), channel_id=1, source_target_pairs={{0,2},{1,3},{2,0},{3,1},{4,6},{5,7},{6,4},{7,5},{8,10},{9,11},{10,... | collective-permute-start | bytes 1179656 | tf_op jit(solution)/shard_map/ppermute | solution.py:245
  9.4 7.7 %collective-permute-done.3.refs_4_.refs_5_ = bf16[128,1024]{1,0:T(8,128)(2,1)S(1)} collective-permute-done((bf16[128,1024]{1,0:T(8,128)(2,1)S(1)}, bf16[128,1024]{1,0:T(8,128)(2,1)S(1)}, u32[]{:S(2)}, u32[]{:S(2)}) %collective-permute-start.3) | collective-permute-done | bytes 262176 | tf_op jit(solution)/shard_map/ppermute | solution.py:245
  17.1 0.0 copy-start.4
  17.1 1.7 %collective-permute-start.5 = (bf16[128,1024]{1,0:T(8,128)(2,1)S(1)}, bf16[128,1024]{1,0:T(8,128)(2,1)S(1)}, u32[]{:S(2)}, u32[]{:S(2)}) collective-permute-start(bf16[128,1024]{1,0:T(8,128)(2,1)S(1)} %collective-permute-done.3.refs_4_.refs_5_), channel_id=1, source_target_pairs={{0,2},{1,3},{2,0},{3,1},{4,6},{5,7},{6,4},{7,5},{8,10},{9,11},{10,... | collective-permute-start | bytes 786440 | tf_op jit(solution)/shard_map/ppermute | solution.py:245
  18.8 0.0 collective-permute-start.4
  18.8 0.9 %collective-permute-done.7.refs_8_.refs_9_ = bf16[128,1024]{1,0:T(8,128)(2,1)S(1)} collective-permute-done((bf16[128,1024]{1,0:T(8,128)(2,1)S(1)}, bf16[128,1024]{1,0:T(8,128)(2,1)S(1)}, u32[]{:S(2)}, u32[]{:S(2)}) %collective-permute-start.7) | collective-permute-done | bytes 262176 | tf_op jit(solution)/shard_map/ppermute | solution.py:245
  19.6 0.0 copy-start.5
  19.6 2.5 %collective-permute-start.11 = (bf16[128,1024]{1,0:T(8,128)(2,1)S(1)}, bf16[128,1024]{1,0:T(8,128)(2,1)S(1)}, u32[]{:S(2)}, u32[]{:S(2)}) collective-permute-start(bf16[128,1024]{1,0:T(8,128)(2,1)S(1)} %get-tuple-element.20), channel_id=1, source_target_pairs={{0,12},{4,8},{8,4},{12,0},{1,13},{5,9},{9,5},{13,1},{2,14},{6,10},... | collective-permute-start | bytes 786440 | tf_op jit(solution)/shard_map/ppermute | solution.py:245
  22.1 1.5 %collective-permute-start.9 = (bf16[128,1024]{1,0:T(8,128)(2,1)S(1)}, bf16[128,1024]{1,0:T(8,128)(2,1)S(1)}, u32[]{:S(2)}, u32[]{:S(2)}) collective-permute-start(bf16[128,1024]{1,0:T(8,128)(2,1)S(1)} %collective-permute-done.7.refs_8_.refs_9_), channel_id=1, source_target_pairs={{0,2},{1,3},{2,0},{3,1},{4,6},{5,7},{6,4},{7,5},{8,10},{9,11},{10,... | collective-permute-start | bytes 786440 | tf_op jit(solution)/shard_map/ppermute | solution.py:245
  23.6 0.0 collective-permute-done.refs_2_.refs_3_
  23.6 0.0 copy-start.1
  23.6 0.0 collective-permute-start.8
  23.6 1.4 %collective-permute-done.5.refs_6_.refs_7_ = bf16[128,1024]{1,0:T(8,128)(2,1)S(1)} collective-permute-done((bf16[128,1024]{1,0:T(8,128)(2,1)S(1)}, bf16[128,1024]{1,0:T(8,128)(2,1)S(1)}, u32[]{:S(2)}, u32[]{:S(2)}) %collective-permute-start.5) | collective-permute-done | bytes 262176 | tf_op jit(solution)/shard_map/ppermute | solution.py:245
  25.0 0.0 collective-permute-start.6
  25.0 0.0 collective-permute-done.4.refs_5_.refs_6_
  25.0 0.0 copy-start.7
  25.1 0.5 collective-permute-start.1
  25.6 3.8 %collective-permute-done.11.refs_12_.refs_13_ = bf16[128,1024]{1,0:T(8,128)(2,1)S(1)} collective-permute-done((bf16[128,1024]{1,0:T(8,128)(2,1)S(1)}, bf16[128,1024]{1,0:T(8,128)(2,1)S(1)}, u32[]{:S(2)}, u32[]{:S(2)}) %collective-permute-start.11) | collective-permute-done | bytes 262176 | tf_op jit(solution)/shard_map/ppermute | solution.py:245
  29.4 0.0 collective-permute-start.2
  29.4 0.8 %collective-permute-done.9.refs_10_.refs_11_ = bf16[128,1024]{1,0:T(8,128)(2,1)S(1)} collective-permute-done((bf16[128,1024]{1,0:T(8,128)(2,1)S(1)}, bf16[128,1024]{1,0:T(8,128)(2,1)S(1)}, u32[]{:S(2)}, u32[]{:S(2)}) %collective-permute-start.9) | collective-permute-done | bytes 262176 | tf_op jit(solution)/shard_map/ppermute | solution.py:245
  30.2 0.0 collective-permute-start.12
  30.2 0.0 collective-permute-done.8.refs_9_.refs_10_
  30.2 0.0 copy-start.10
  30.2 0.5 collective-permute-start.10
  30.7 0.0 collective-permute-done.6.refs_7_.refs_8_
  30.7 1.3 %collective-permute-start.13 = (bf16[128,1024]{1,0:T(8,128)(2,1)S(1)}, bf16[128,1024]{1,0:T(8,128)(2,1)S(1)}, u32[]{:S(2)}, u32[]{:S(2)}) collective-permute-start(bf16[128,1024]{1,0:T(8,128)(2,1)S(1)} %collective-permute-done.11.refs_12_.refs_13_), channel_id=1, source_target_pairs={{0,2},{1,3},{2,0},{3,1},{4,6},{5,7},{6,4},{7,5},{8,10},{9,11},{10,... | collective-permute-start | bytes 786440 | tf_op jit(solution)/shard_map/ppermute | solution.py:245
  32.1 0.0 collective-permute-done.12.refs_13_.refs_14_
  32.1 0.0 collective-permute-done.10.refs_11_.refs_12_
  32.1 0.0 collective-permute-done.1.refs_1_.refs_2_
  32.1 0.0 collective-permute-done.2.refs_3_.refs_4_
  32.1 0.0 copy-start.3
  32.1 4.7 %some_rows.1.refs_0_ = f32[264,1152]{1,0:T(8,128)S(1)} custom-call(bf16[192,1024]{1,0:T(8,128)(2,1)S(1)} %get-tuple-element.16.refs_0_.refs_1_, bf16[192,1024]{1,0:T(8,128)(2,1)S(1)} %collective-permute-done.1.refs_1_.refs_2_, bf16[192,1024]{1,0:T(8,128)(2,1)S(1)} %collective-permute-done.refs_2_.refs_3_, ...), custom_call_target="tpu_custom_call" | custom-call | flops 1 | bytes 1 | tf_op jit(solution)/shard_map/some_rows/pallas_call | solution.py:319
  36.9 0.0 copy-done
  36.9 0.0 copy-done.4
  36.9 0.0 copy-done.5
  36.9 0.0 copy-done.1
  36.9 0.0 copy-done.6
  36.9 0.0 copy-done.7
  36.9 0.0 copy-done.8
  36.9 0.0 copy-done.9
  37.0 0.0 copy-done.10
  37.0 0.0 copy-done.11
  37.0 0.0 copy-done.12
  37.0 0.0 copy-done.13
  37.0 0.0 copy-done.2
  37.0 0.0 copy-done.3
  37.0 0.0 copy-start.14
  37.0 2.0 %collective-permute-done.13.refs_15_ = bf16[128,1024]{1,0:T(8,128)(2,1)S(1)} collective-permute-done((bf16[128,1024]{1,0:T(8,128)(2,1)S(1)}, bf16[128,1024]{1,0:T(8,128)(2,1)S(1)}, u32[]{:S(2)}, u32[]{:S(2)}) %collective-permute-start.13) | collective-permute-done | bytes 262176 | tf_op jit(solution)/shard_map/ppermute | solution.py:245
  39.0 0.0 collective-permute-start.14
  39.0 1.5 %collective-permute-done.14.refs_16_ = bf16[128,1024]{1,0:T(8,128)(2,1)S(1)} collective-permute-done((bf16[128,1024]{1,0:T(8,128)(2,1)S(1)}, bf16[128,1024]{1,0:T(8,128)(2,1)S(1)}, u32[]{:S(2)}, u32[]{:S(2)}) %collective-permute-start.14) | collective-permute-done | bytes 262176 | tf_op jit(solution)/shard_map/ppermute | solution.py:245
  40.6 6.1 %rounds.1 = (f32[64,1024]{1,0:T(8,128)}, bf16[128,256]{1,0:T(8,128)(2,1)S(1)}, bf16[128,256]{1,0:T(8,128)(2,1)S(1)}, bf16[128,256]{1,0:T(8,128)(2,1)S(1)}, bf16[128,256]{1,0:T(8,128)(2,1)S(1)}) custom-call(f32[264,1152]{1,0:T(8,128)S(1)} %some_rows.1.refs_0_, bf16[192,1024]{1,0:T(8,128)(2,1)} %copy-done, bf16[192,1024]{1,0:T(8,128)(2,1)} %copy-done.2, ...), custom_call_target="tpu_custom_call" | custom-call | flops 1 | bytes 1 | tf_op jit(solution)/shard_map/rounds/pallas_call | solution.py:334
  46.7 2.4 %collective-permute-start.15 = (bf16[128,256]{1,0:T(8,128)(2,1)S(1)}, bf16[128,256]{1,0:T(8,128)(2,1)S(1)}, u32[]{:S(2)}, u32[]{:S(2)}) collective-permute-start(bf16[128,256]{1,0:T(8,128)(2,1)S(1)} %get-tuple-element.24), channel_id=1, source_target_pairs={{0,12},{4,8},{8,4},{12,0},{1,13},{5,9},{9,5},{13,1},{2,14},{6,10},... | collective-permute-start | bytes 196616 | tf_op jit(solution)/shard_map/ppermute | solution.py:245
  49.1 2.2 %collective-permute-start.16 = (bf16[128,256]{1,0:T(8,128)(2,1)S(1)}, bf16[128,256]{1,0:T(8,128)(2,1)S(1)}, u32[]{:S(2)}, u32[]{:S(2)}) collective-permute-start(bf16[128,256]{1,0:T(8,128)(2,1)S(1)} %get-tuple-element.25), channel_id=1, source_target_pairs={{0,8},{4,12},{8,0},{12,4},{1,9},{5,13},{9,1},{13,5},{2,10},{6,14},... | collective-permute-start | bytes 196616 | tf_op jit(solution)/shard_map/ppermute | solution.py:245
  51.2 0.0 collective-permute-start.17
  51.2 0.0 copy-done.14
  51.3 0.3 places.1.places_ref
  51.6 1.3 %collective-permute-done.15.refs_0_ = bf16[128,256]{1,0:T(8,128)(2,1)S(1)} collective-permute-done((bf16[128,256]{1,0:T(8,128)(2,1)S(1)}, bf16[128,256]{1,0:T(8,128)(2,1)S(1)}, u32[]{:S(2)}, u32[]{:S(2)}) %collective-permute-start.15) | collective-permute-done | bytes 65568 | tf_op jit(solution)/shard_map/ppermute | solution.py:245
  52.9 4.0 %collective-permute-done.16.refs_1_ = bf16[128,256]{1,0:T(8,128)(2,1)S(1)} collective-permute-done((bf16[128,256]{1,0:T(8,128)(2,1)S(1)}, bf16[128,256]{1,0:T(8,128)(2,1)S(1)}, u32[]{:S(2)}, u32[]{:S(2)}) %collective-permute-start.16) | collective-permute-done | bytes 65568 | tf_op jit(solution)/shard_map/ppermute | solution.py:245
  56.9 0.0 collective-permute-done.17.refs_2_
  56.9 1.0 %unpack.1 = f32[256,256]{1,0:T(8,128)} custom-call(bf16[256,512]{1,0:T(8,128)(2,1)S(1)} %places.1.places_ref, bf16[128,256]{1,0:T(8,128)(2,1)S(1)} %collective-permute-done.15.refs_0_, bf16[128,256]{1,0:T(8,128)(2,1)S(1)} %collective-permute-done.16.refs_1_, bf16[128,256]{1,0:T(8,128)(2,1)S(1)} %collective-permute-done.17.refs_2_, ...), custom_call_target="tpu_custom_call" | custom-call | flops 1 | bytes 1 | tf_op jit(solution)/shard_map/unpack/pallas_call | solution.py:358
  (7 shorter events, 0.0 us)
Async XLA Ops:
  2.2 34.7 %copy-start = (bf16[192,1024]{1,0:T(8,128)(2,1)}, bf16[192,1024]{1,0:T(8,128)(2,1)S(1)}, u32[]{:S(2)}) copy-start(bf16[192,1024]{1,0:T(8,128)(2,1)S(1)} %get-tuple-element.16.refs_0_.refs_1_) | copy-start | bytes 1179652
  2.2 14.9 %collective-permute-start.3 = (bf16[128,1024]{1,0:T(8,128)(2,1)S(1)}, bf16[128,1024]{1,0:T(8,128)(2,1)S(1)}, u32[]{:S(2)}, u32[]{:S(2)}) collective-permute-start(bf16[128,1024]{1,0:T(8,128)(2,1)S(1)} %get-tuple-element.17), channel_id=1, source_target_pairs={{0,4},{4,0},{8,12},{12,8},{1,5},{5,1},{9,13},{13,9},{2,6},{6,2},{1... | collective-permute-start | bytes 786440 | tf_op jit(solution)/shard_map/ppermute | solution.py:245
  5.3 14.3 %collective-permute-start.7 = (bf16[128,1024]{1,0:T(8,128)(2,1)S(1)}, bf16[128,1024]{1,0:T(8,128)(2,1)S(1)}, u32[]{:S(2)}, u32[]{:S(2)}) collective-permute-start(bf16[128,1024]{1,0:T(8,128)(2,1)S(1)} %get-tuple-element.18), channel_id=1, source_target_pairs={{0,8},{4,12},{8,0},{12,4},{1,9},{5,13},{9,1},{13,5},{2,10},{6,14},... | collective-permute-start | bytes 786440 | tf_op jit(solution)/shard_map/ppermute | solution.py:245
  7.9 15.7 %collective-permute-start = (bf16[192,1024]{1,0:T(8,128)(2,1)S(1)}, bf16[192,1024]{1,0:T(8,128)(2,1)S(1)}, u32[]{:S(2)}, u32[]{:S(2)}) collective-permute-start(bf16[192,1024]{1,0:T(8,128)(2,1)S(1)} %get-tuple-element.16.refs_0_.refs_1_), channel_id=1, source_target_pairs={{0,2},{1,3},{2,0},{3,1},{4,6},{5,7},{6,4},{7,5},{8,10},{9,11},{10,... | collective-permute-start | bytes 1179656 | tf_op jit(solution)/shard_map/ppermute | solution.py:245
  17.1 19.8 %copy-start.4 = (bf16[128,1024]{1,0:T(8,128)(2,1)}, bf16[128,1024]{1,0:T(8,128)(2,1)S(1)}, u32[]{:S(2)}) copy-start(bf16[128,1024]{1,0:T(8,128)(2,1)S(1)} %collective-permute-done.3.refs_4_.refs_5_) | copy-start | bytes 786436
  17.1 7.9 %collective-permute-start.5 = (bf16[128,1024]{1,0:T(8,128)(2,1)S(1)}, bf16[128,1024]{1,0:T(8,128)(2,1)S(1)}, u32[]{:S(2)}, u32[]{:S(2)}) collective-permute-start(bf16[128,1024]{1,0:T(8,128)(2,1)S(1)} %collective-permute-done.3.refs_4_.refs_5_), channel_id=1, source_target_pairs={{0,2},{1,3},{2,0},{3,1},{4,6},{5,7},{6,4},{7,5},{8,10},{9,11},{10,... | collective-permute-start | bytes 786440 | tf_op jit(solution)/shard_map/ppermute | solution.py:245
  18.8 6.3 %collective-permute-start.4 = (bf16[128,1024]{1,0:T(8,128)(2,1)S(1)}, bf16[128,1024]{1,0:T(8,128)(2,1)S(1)}, u32[]{:S(2)}, u32[]{:S(2)}) collective-permute-start(bf16[128,1024]{1,0:T(8,128)(2,1)S(1)} %collective-permute-done.3.refs_4_.refs_5_), channel_id=1, source_target_pairs={{0,1},{1,0},{2,3},{3,2},{4,5},{5,4},{6,7},{7,6},{8,9},{9,8},{10,11... | collective-permute-start | bytes 786440 | tf_op jit(solution)/shard_map/ppermute | solution.py:245
  19.6 17.3 %copy-start.5 = (bf16[128,1024]{1,0:T(8,128)(2,1)}, bf16[128,1024]{1,0:T(8,128)(2,1)S(1)}, u32[]{:S(2)}) copy-start(bf16[128,1024]{1,0:T(8,128)(2,1)S(1)} %collective-permute-done.7.refs_8_.refs_9_) | copy-start | bytes 786436
  19.6 9.8 %collective-permute-start.11 = (bf16[128,1024]{1,0:T(8,128)(2,1)S(1)}, bf16[128,1024]{1,0:T(8,128)(2,1)S(1)}, u32[]{:S(2)}, u32[]{:S(2)}) collective-permute-start(bf16[128,1024]{1,0:T(8,128)(2,1)S(1)} %get-tuple-element.20), channel_id=1, source_target_pairs={{0,12},{4,8},{8,4},{12,0},{1,13},{5,9},{9,5},{13,1},{2,14},{6,10},... | collective-permute-start | bytes 786440 | tf_op jit(solution)/shard_map/ppermute | solution.py:245
  22.1 8.1 %collective-permute-start.9 = (bf16[128,1024]{1,0:T(8,128)(2,1)S(1)}, bf16[128,1024]{1,0:T(8,128)(2,1)S(1)}, u32[]{:S(2)}, u32[]{:S(2)}) collective-permute-start(bf16[128,1024]{1,0:T(8,128)(2,1)S(1)} %collective-permute-done.7.refs_8_.refs_9_), channel_id=1, source_target_pairs={{0,2},{1,3},{2,0},{3,1},{4,6},{5,7},{6,4},{7,5},{8,10},{9,11},{10,... | collective-permute-start | bytes 786440 | tf_op jit(solution)/shard_map/ppermute | solution.py:245
  23.6 13.3 %copy-start.1 = (bf16[192,1024]{1,0:T(8,128)(2,1)}, bf16[192,1024]{1,0:T(8,128)(2,1)S(1)}, u32[]{:S(2)}) copy-start(bf16[192,1024]{1,0:T(8,128)(2,1)S(1)} %collective-permute-done.refs_2_.refs_3_) | copy-start | bytes 1179652
  23.6 6.6 %collective-permute-start.8 = (bf16[128,1024]{1,0:T(8,128)(2,1)S(1)}, bf16[128,1024]{1,0:T(8,128)(2,1)S(1)}, u32[]{:S(2)}, u32[]{:S(2)}) collective-permute-start(bf16[128,1024]{1,0:T(8,128)(2,1)S(1)} %collective-permute-done.7.refs_8_.refs_9_), channel_id=1, source_target_pairs={{0,1},{1,0},{2,3},{3,2},{4,5},{5,4},{6,7},{7,6},{8,9},{9,8},{10,11... | collective-permute-start | bytes 786440 | tf_op jit(solution)/shard_map/ppermute | solution.py:245
  25.0 11.9 %copy-start.6 = (bf16[128,1024]{1,0:T(8,128)(2,1)}, bf16[128,1024]{1,0:T(8,128)(2,1)S(1)}, u32[]{:S(2)}) copy-start(bf16[128,1024]{1,0:T(8,128)(2,1)S(1)} %collective-permute-done.5.refs_6_.refs_7_) | copy-start | bytes 786436
  25.0 5.7 %collective-permute-start.6 = (bf16[128,1024]{1,0:T(8,128)(2,1)S(1)}, bf16[128,1024]{1,0:T(8,128)(2,1)S(1)}, u32[]{:S(2)}, u32[]{:S(2)}) collective-permute-start(bf16[128,1024]{1,0:T(8,128)(2,1)S(1)} %collective-permute-done.5.refs_6_.refs_7_), channel_id=1, source_target_pairs={{0,1},{1,0},{2,3},{3,2},{4,5},{5,4},{6,7},{7,6},{8,9},{9,8},{10,11... | collective-permute-start | bytes 786440 | tf_op jit(solution)/shard_map/ppermute | solution.py:245
  25.0 11.9 %copy-start.7 = (bf16[128,1024]{1,0:T(8,128)(2,1)}, bf16[128,1024]{1,0:T(8,128)(2,1)S(1)}, u32[]{:S(2)}) copy-start(bf16[128,1024]{1,0:T(8,128)(2,1)S(1)} %collective-permute-done.4.refs_5_.refs_6_) | copy-start | bytes 786436
  25.1 7.1 %collective-permute-start.1 = (bf16[192,1024]{1,0:T(8,128)(2,1)S(1)}, bf16[192,1024]{1,0:T(8,128)(2,1)S(1)}, u32[]{:S(2)}, u32[]{:S(2)}) collective-permute-start(bf16[192,1024]{1,0:T(8,128)(2,1)S(1)} %get-tuple-element.16.refs_0_.refs_1_), channel_id=1, source_target_pairs={{0,1},{1,0},{2,3},{3,2},{4,5},{5,4},{6,7},{7,6},{8,9},{9,8},{10,11... | collective-permute-start | bytes 1179656 | tf_op jit(solution)/shard_map/ppermute | solution.py:245
  29.4 7.5 %copy-start.8 = (bf16[128,1024]{1,0:T(8,128)(2,1)}, bf16[128,1024]{1,0:T(8,128)(2,1)S(1)}, u32[]{:S(2)}) copy-start(bf16[128,1024]{1,0:T(8,128)(2,1)S(1)} %collective-permute-done.11.refs_12_.refs_13_) | copy-start | bytes 786436
  29.4 2.7 %collective-permute-start.2 = (bf16[192,1024]{1,0:T(8,128)(2,1)S(1)}, bf16[192,1024]{1,0:T(8,128)(2,1)S(1)}, u32[]{:S(2)}, u32[]{:S(2)}) collective-permute-start(bf16[192,1024]{1,0:T(8,128)(2,1)S(1)} %collective-permute-done.refs_2_.refs_3_), channel_id=1, source_target_pairs={{0,1},{1,0},{2,3},{3,2},{4,5},{5,4},{6,7},{7,6},{8,9},{9,8},{10,11... | collective-permute-start | bytes 1179656 | tf_op jit(solution)/shard_map/ppermute | solution.py:245
  30.2 6.7 %copy-start.9 = (bf16[128,1024]{1,0:T(8,128)(2,1)}, bf16[128,1024]{1,0:T(8,128)(2,1)S(1)}, u32[]{:S(2)}) copy-start(bf16[128,1024]{1,0:T(8,128)(2,1)S(1)} %collective-permute-done.9.refs_10_.refs_11_) | copy-start | bytes 786436
  30.2 1.9 %collective-permute-start.12 = (bf16[128,1024]{1,0:T(8,128)(2,1)S(1)}, bf16[128,1024]{1,0:T(8,128)(2,1)S(1)}, u32[]{:S(2)}, u32[]{:S(2)}) collective-permute-start(bf16[128,1024]{1,0:T(8,128)(2,1)S(1)} %collective-permute-done.11.refs_12_.refs_13_), channel_id=1, source_target_pairs={{0,1},{1,0},{2,3},{3,2},{4,5},{5,4},{6,7},{7,6},{8,9},{9,8},{10,11... | collective-permute-start | bytes 786440 | tf_op jit(solution)/shard_map/ppermute | solution.py:245
  30.2 6.7 %copy-start.10 = (bf16[128,1024]{1,0:T(8,128)(2,1)}, bf16[128,1024]{1,0:T(8,128)(2,1)S(1)}, u32[]{:S(2)}) copy-start(bf16[128,1024]{1,0:T(8,128)(2,1)S(1)} %collective-permute-done.8.refs_9_.refs_10_) | copy-start | bytes 786436
  30.2 1.9 %collective-permute-start.10 = (bf16[128,1024]{1,0:T(8,128)(2,1)S(1)}, bf16[128,1024]{1,0:T(8,128)(2,1)S(1)}, u32[]{:S(2)}, u32[]{:S(2)}) collective-permute-start(bf16[128,1024]{1,0:T(8,128)(2,1)S(1)} %collective-permute-done.9.refs_10_.refs_11_), channel_id=1, source_target_pairs={{0,1},{1,0},{2,3},{3,2},{4,5},{5,4},{6,7},{7,6},{8,9},{9,8},{10,11... | collective-permute-start | bytes 786440 | tf_op jit(solution)/shard_map/ppermute | solution.py:245
  30.7 6.2 %copy-start.11 = (bf16[128,1024]{1,0:T(8,128)(2,1)}, bf16[128,1024]{1,0:T(8,128)(2,1)S(1)}, u32[]{:S(2)}) copy-start(bf16[128,1024]{1,0:T(8,128)(2,1)S(1)} %collective-permute-done.6.refs_7_.refs_8_) | copy-start | bytes 786436
  30.7 8.3 %collective-permute-start.13 = (bf16[128,1024]{1,0:T(8,128)(2,1)S(1)}, bf16[128,1024]{1,0:T(8,128)(2,1)S(1)}, u32[]{:S(2)}, u32[]{:S(2)}) collective-permute-start(bf16[128,1024]{1,0:T(8,128)(2,1)S(1)} %collective-permute-done.11.refs_12_.refs_13_), channel_id=1, source_target_pairs={{0,2},{1,3},{2,0},{3,1},{4,6},{5,7},{6,4},{7,5},{8,10},{9,11},{10,... | collective-permute-start | bytes 786440 | tf_op jit(solution)/shard_map/ppermute | solution.py:245
  32.1 4.9 %copy-start.12 = (bf16[128,1024]{1,0:T(8,128)(2,1)}, bf16[128,1024]{1,0:T(8,128)(2,1)S(1)}, u32[]{:S(2)}) copy-start(bf16[128,1024]{1,0:T(8,128)(2,1)S(1)} %collective-permute-done.12.refs_13_.refs_14_) | copy-start | bytes 786436
  32.1 4.9 %copy-start.13 = (bf16[128,1024]{1,0:T(8,128)(2,1)}, bf16[128,1024]{1,0:T(8,128)(2,1)S(1)}, u32[]{:S(2)}) copy-start(bf16[128,1024]{1,0:T(8,128)(2,1)S(1)} %collective-permute-done.10.refs_11_.refs_12_) | copy-start | bytes 786436
  32.1 4.9 %copy-start.2 = (bf16[192,1024]{1,0:T(8,128)(2,1)}, bf16[192,1024]{1,0:T(8,128)(2,1)S(1)}, u32[]{:S(2)}) copy-start(bf16[192,1024]{1,0:T(8,128)(2,1)S(1)} %collective-permute-done.1.refs_1_.refs_2_) | copy-start | bytes 1179652
  32.1 4.9 %copy-start.3 = (bf16[192,1024]{1,0:T(8,128)(2,1)}, bf16[192,1024]{1,0:T(8,128)(2,1)S(1)}, u32[]{:S(2)}) copy-start(bf16[192,1024]{1,0:T(8,128)(2,1)S(1)} %collective-permute-done.2.refs_3_.refs_4_) | copy-start | bytes 1179652
  37.0 14.2 %copy-start.14 = (s32[256]{0:T(256)S(1)}, s32[256]{0:T(256)}, u32[]{:S(2)}) copy-start(s32[256]{0:T(256)} %param.4) | copy-start | bytes 3076
  39.0 1.5 %collective-permute-start.14 = (bf16[128,1024]{1,0:T(8,128)(2,1)S(1)}, bf16[128,1024]{1,0:T(8,128)(2,1)S(1)}, u32[]{:S(2)}, u32[]{:S(2)}) collective-permute-start(bf16[128,1024]{1,0:T(8,128)(2,1)S(1)} %collective-permute-done.13.refs_15_), channel_id=1, source_target_pairs={{0,1},{1,0},{2,3},{3,2},{4,5},{5,4},{6,7},{7,6},{8,9},{9,8},{10,11... | collective-permute-start | bytes 786440 | tf_op jit(solution)/shard_map/ppermute | solution.py:245
  46.7 6.2 %collective-permute-start.15 = (bf16[128,256]{1,0:T(8,128)(2,1)S(1)}, bf16[128,256]{1,0:T(8,128)(2,1)S(1)}, u32[]{:S(2)}, u32[]{:S(2)}) collective-permute-start(bf16[128,256]{1,0:T(8,128)(2,1)S(1)} %get-tuple-element.24), channel_id=1, source_target_pairs={{0,12},{4,8},{8,4},{12,0},{1,13},{5,9},{9,5},{13,1},{2,14},{6,10},... | collective-permute-start | bytes 196616 | tf_op jit(solution)/shard_map/ppermute | solution.py:245
  49.1 7.8 %collective-permute-start.16 = (bf16[128,256]{1,0:T(8,128)(2,1)S(1)}, bf16[128,256]{1,0:T(8,128)(2,1)S(1)}, u32[]{:S(2)}, u32[]{:S(2)}) collective-permute-start(bf16[128,256]{1,0:T(8,128)(2,1)S(1)} %get-tuple-element.25), channel_id=1, source_target_pairs={{0,8},{4,12},{8,0},{12,4},{1,9},{5,13},{9,1},{13,5},{2,10},{6,14},... | collective-permute-start | bytes 196616 | tf_op jit(solution)/shard_map/ppermute | solution.py:245
  51.2 5.6 %collective-permute-start.17 = (bf16[128,256]{1,0:T(8,128)(2,1)S(1)}, bf16[128,256]{1,0:T(8,128)(2,1)S(1)}, u32[]{:S(2)}, u32[]{:S(2)}) collective-permute-start(bf16[128,256]{1,0:T(8,128)(2,1)S(1)} %get-tuple-element.26), channel_id=1, source_target_pairs={{0,4},{4,0},{8,12},{12,8},{1,5},{5,1},{9,13},{13,9},{2,6},{6,2},{1... | collective-permute-start | bytes 196616 | tf_op jit(solution)/shard_map/ppermute | solution.py:245

commit v7 on v6

--- a/solution.py
+++ b/solution.py
@@ -181,17 +181,19 @@
     state_ref, ordered, share_ref, rows, old_ref, whole_ref, arrived, ready, kept = refs
     height = given[-1].shape[0]
     held = earlier * height
+    subs = helpers * share_rows
     centres = fetch([ref.at[height:] for ref in given[:helpers]], ordered, ready)
     given = [ref.at[:height] for ref in given]
+    norms = fetch([old[0].at[subs:]], old_ref.at[subs:], kept.at[1:])
     later = fetch(given[earlier:], rows.at[held:], arrived.at[earlier:])
-    state = fetch(old, old_ref, kept)
+    state = fetch([old[0].at[:subs]], old_ref.at[:subs], kept)
     sooner = fetch(given[:earlier], rows, arrived)
     helper = lax.axis_index("hlp").astype(jnp.int32)
-    settle(centres + state + later)
+    settle(centres + norms + later)
     centres = ordered[...]
-    norms = old_ref[centres.shape[0] : centres.shape[0] + 1, : centres.shape[0]]
+    norms = old_ref[subs : subs + 1, :subs]
     accumulate(centres, norms, tiles_of(rows, held, rows.shape[0]), share_ref, state_ref, True)
-    settle(sooner)
+    settle(state + sooner)
     states = (state_ref, old_ref)
     for turn in range(1, ITERS):
         centres = refine(centres, *states).astype(BF)
@@ -337,11 +339,11 @@
         in_specs=[HBM] * (1 + len(earlier) + len(late)),
         out_specs=[HBM] + vmem(groups),
         scratch_shapes=[pltpu.VMEM(s.shape, s.dtype) for s in own]
-        + semaphores(len(earlier) + len(late), helpers, 1),
+        + semaphores(len(earlier) + len(late), helpers, 2),
         compiler_params=params(*own, *logs),
         cost_estimate=COST,
         name="rounds",
-    )(sofar, *[in_hbm(r) for r in earlier], *late)
+    )(sofar, *[in_hbm(r) for r in earlier[: 3 * helpers - 2]], *earlier[3 * helpers - 2 :], *late)
 
     back = [across(logs[g], g) for g in reversed(range(groups))]
     places = jax.ShapeDtypeStruct((count, groups * height), BF)

time: 58 us -> 58 us (level)
  no operation moved by 1% of the time
where the time goes in v7:
time: 58 us; the launch traced here: 57.8 us
  waiting for transfers between devices  23.6 us (41%)
  starting transfers between devices  19.7 us (34%)
  Pallas kernels  13.7 us (24%)
  between operations  0.8 us (1%)
    ppermute x18, waiting for transfers between devices, hop(): return lambda x: lax.ppermute(x, axis, pairs)  23.6 us
    ppermute x18, starting transfers between devices, hop(): return lambda x: lax.ppermute(x, axis, pairs)  19.7 us
    pallas_call x1, Pallas kernels, per_device(): pl.pallas_call(functools.partial(last_kernel, helpers, (len(earlier), len...  6.05 us
    pallas_call x1, Pallas kernels, per_device(): pl.pallas_call(functools.partial(some_kernel, helpers, height), out_shape...  4.72 us
    pallas_call x1, Pallas kernels, per_device(): pl.pallas_call(functools.partial(pack_kernel, depth, owners), out_shape=b...  1.56 us
  transfers between devices with their start and end apart: 18, of which 9 were waited for; matrix products, arithmetic and copies ran while one was open for 0% of the time, Pallas kernels for 9%

profile of v7, /device:TPU:0, one launch (start us, length us, event | category | flops | bytes accessed | tf_op | source)
XLA Modules:
  0.0 57.8 jit_solution(15367230901009980570)
XLA Ops:
  0.6 1.6 %pack.1 = (bf16[192,1024]{1,0:T(8,128)(2,1)S(1)}, bf16[128,1024]{1,0:T(8,128)(2,1)S(1)}, bf16[128,1024]{1,0:T(8,128)(2,1)S(1)}, bf16[128,1024]{1,0:T(8,128)(2,1)S(1)}) custom-call(s32[1,256]{1,0:T(1,128)} %bitcast.3, bf16[256,1024]{1,0:T(8,128)(2,1)} %points_hbm.1, bf16[64,1024]{1,0:T(8,128)(2,1)} %bitcast.5), custom_call_target="tpu_custom_call" | custom-call | flops 1 | bytes 1 | tf_op jit(solution)/shard_map/pack/pallas_call | solution.py:264
  2.2 0.0 copy-start
  2.2 3.1 %collective-permute-start.3 = (bf16[128,1024]{1,0:T(8,128)(2,1)S(1)}, bf16[128,1024]{1,0:T(8,128)(2,1)S(1)}, u32[]{:S(2)}, u32[]{:S(2)}) collective-permute-start(bf16[128,1024]{1,0:T(8,128)(2,1)S(1)} %get-tuple-element.17), channel_id=1, source_target_pairs={{0,4},{4,0},{8,12},{12,8},{1,5},{5,1},{9,13},{13,9},{2,6},{6,2},{1... | collective-permute-start | bytes 786440 | tf_op jit(solution)/shard_map/ppermute | solution.py:247
  5.3 2.6 %collective-permute-start.7 = (bf16[128,1024]{1,0:T(8,128)(2,1)S(1)}, bf16[128,1024]{1,0:T(8,128)(2,1)S(1)}, u32[]{:S(2)}, u32[]{:S(2)}) collective-permute-start(bf16[128,1024]{1,0:T(8,128)(2,1)S(1)} %get-tuple-element.18), channel_id=1, source_target_pairs={{0,8},{4,12},{8,0},{12,4},{1,9},{5,13},{9,1},{13,5},{2,10},{6,14},... | collective-permute-start | bytes 786440 | tf_op jit(solution)/shard_map/ppermute | solution.py:247
  7.9 1.5 %collective-permute-start = (bf16[192,1024]{1,0:T(8,128)(2,1)S(1)}, bf16[192,1024]{1,0:T(8,128)(2,1)S(1)}, u32[]{:S(2)}, u32[]{:S(2)}) collective-permute-start(bf16[192,1024]{1,0:T(8,128)(2,1)S(1)} %get-tuple-element.16.refs_0_.refs_1_), channel_id=1, source_target_pairs={{0,2},{1,3},{2,0},{3,1},{4,6},{5,7},{6,4},{7,5},{8,10},{9,11},{10,... | collective-permute-start | bytes 1179656 | tf_op jit(solution)/shard_map/ppermute | solution.py:247
  9.4 7.7 %collective-permute-done.3.refs_4_.refs_5_ = bf16[128,1024]{1,0:T(8,128)(2,1)S(1)} collective-permute-done((bf16[128,1024]{1,0:T(8,128)(2,1)S(1)}, bf16[128,1024]{1,0:T(8,128)(2,1)S(1)}, u32[]{:S(2)}, u32[]{:S(2)}) %collective-permute-start.3) | collective-permute-done | bytes 262176 | tf_op jit(solution)/shard_map/ppermute | solution.py:247
  17.1 0.0 copy-start.4
  17.1 1.7 %collective-permute-start.5 = (bf16[128,1024]{1,0:T(8,128)(2,1)S(1)}, bf16[128,1024]{1,0:T(8,128)(2,1)S(1)}, u32[]{:S(2)}, u32[]{:S(2)}) collective-permute-start(bf16[128,1024]{1,0:T(8,128)(2,1)S(1)} %collective-permute-done.3.refs_4_.refs_5_), channel_id=1, source_target_pairs={{0,2},{1,3},{2,0},{3,1},{4,6},{5,7},{6,4},{7,5},{8,10},{9,11},{10,... | collective-permute-start | bytes 786440 | tf_op jit(solution)/shard_map/ppermute | solution.py:247
  18.8 0.0 collective-permute-start.4
  18.8 0.9 %collective-permute-done.7.refs_8_.refs_9_ = bf16[128,1024]{1,0:T(8,128)(2,1)S(1)} collective-permute-done((bf16[128,1024]{1,0:T(8,128)(2,1)S(1)}, bf16[128,1024]{1,0:T(8,128)(2,1)S(1)}, u32[]{:S(2)}, u32[]{:S(2)}) %collective-permute-start.7) | collective-permute-done | bytes 262176 | tf_op jit(solution)/shard_map/ppermute | solution.py:247
  19.6 0.0 copy-start.5
  19.6 2.5 %collective-permute-start.11 = (bf16[128,1024]{1,0:T(8,128)(2,1)S(1)}, bf16[128,1024]{1,0:T(8,128)(2,1)S(1)}, u32[]{:S(2)}, u32[]{:S(2)}) collective-permute-start(bf16[128,1024]{1,0:T(8,128)(2,1)S(1)} %get-tuple-element.20), channel_id=1, source_target_pairs={{0,12},{4,8},{8,4},{12,0},{1,13},{5,9},{9,5},{13,1},{2,14},{6,10},... | collective-permute-start | bytes 786440 | tf_op jit(solution)/shard_map/ppermute | solution.py:247
  22.1 1.5 %collective-permute-start.9 = (bf16[128,1024]{1,0:T(8,128)(2,1)S(1)}, bf16[128,1024]{1,0:T(8,128)(2,1)S(1)}, u32[]{:S(2)}, u32[]{:S(2)}) collective-permute-start(bf16[128,1024]{1,0:T(8,128)(2,1)S(1)} %collective-permute-done.7.refs_8_.refs_9_), channel_id=1, source_target_pairs={{0,2},{1,3},{2,0},{3,1},{4,6},{5,7},{6,4},{7,5},{8,10},{9,11},{10,... | collective-permute-start | bytes 786440 | tf_op jit(solution)/shard_map/ppermute | solution.py:247
  23.6 0.0 collective-permute-done.refs_2_.refs_3_
  23.6 0.0 copy-start.1
  23.6 0.0 collective-permute-start.8
  23.6 1.4 %collective-permute-done.5.refs_6_.refs_7_ = bf16[128,1024]{1,0:T(8,128)(2,1)S(1)} collective-permute-done((bf16[128,1024]{1,0:T(8,128)(2,1)S(1)}, bf16[128,1024]{1,0:T(8,128)(2,1)S(1)}, u32[]{:S(2)}, u32[]{:S(2)}) %collective-permute-start.5) | collective-permute-done | bytes 262176 | tf_op jit(solution)/shard_map/ppermute | solution.py:247
  25.0 0.0 copy-start.6
  25.0 0.0 collective-permute-start.6
  25.0 0.0 collective-permute-done.4.refs_5_.refs_6_
  25.0 0.0 copy-start.7
  25.1 0.5 collective-permute-start.1
  25.6 3.8 %collective-permute-done.11.refs_12_.refs_13_ = bf16[128,1024]{1,0:T(8,128)(2,1)S(1)} collective-permute-done((bf16[128,1024]{1,0:T(8,128)(2,1)S(1)}, bf16[128,1024]{1,0:T(8,128)(2,1)S(1)}, u32[]{:S(2)}, u32[]{:S(2)}) %collective-permute-start.11) | collective-permute-done | bytes 262176 | tf_op jit(solution)/shard_map/ppermute | solution.py:247
  29.4 0.0 collective-permute-start.2
  29.4 0.8 %collective-permute-done.9.refs_10_.refs_11_ = bf16[128,1024]{1,0:T(8,128)(2,1)S(1)} collective-permute-done((bf16[128,1024]{1,0:T(8,128)(2,1)S(1)}, bf16[128,1024]{1,0:T(8,128)(2,1)S(1)}, u32[]{:S(2)}, u32[]{:S(2)}) %collective-permute-start.9) | collective-permute-done | bytes 262176 | tf_op jit(solution)/shard_map/ppermute | solution.py:247
  30.2 0.0 collective-permute-start.12
  30.2 0.0 collective-permute-done.8.refs_9_.refs_10_
  30.2 0.0 copy-start.8
  30.2 0.5 collective-permute-start.10
  30.7 0.0 collective-permute-done.6.refs_7_.refs_8_
  30.7 0.0 copy-start.9
  30.7 1.3 %collective-permute-start.13 = (bf16[128,1024]{1,0:T(8,128)(2,1)S(1)}, bf16[128,1024]{1,0:T(8,128)(2,1)S(1)}, u32[]{:S(2)}, u32[]{:S(2)}) collective-permute-start(bf16[128,1024]{1,0:T(8,128)(2,1)S(1)} %collective-permute-done.11.refs_12_.refs_13_), channel_id=1, source_target_pairs={{0,2},{1,3},{2,0},{3,1},{4,6},{5,7},{6,4},{7,5},{8,10},{9,11},{10,... | collective-permute-start | bytes 786440 | tf_op jit(solution)/shard_map/ppermute | solution.py:247
  32.1 0.0 collective-permute-done.12.refs_13_.refs_14_
  32.1 0.0 collective-permute-done.10.refs_11_.refs_12_
  32.1 0.0 collective-permute-done.1.refs_1_.refs_2_
  32.1 0.0 copy-start.2
  32.1 0.0 collective-permute-done.2.refs_3_.refs_4_
  32.1 0.0 copy-start.3
  32.1 4.7 %some_rows.1.refs_0_ = f32[264,1152]{1,0:T(8,128)S(1)} custom-call(bf16[192,1024]{1,0:T(8,128)(2,1)S(1)} %get-tuple-element.16.refs_0_.refs_1_, bf16[192,1024]{1,0:T(8,128)(2,1)S(1)} %collective-permute-done.1.refs_1_.refs_2_, bf16[192,1024]{1,0:T(8,128)(2,1)S(1)} %collective-permute-done.refs_2_.refs_3_, ...), custom_call_target="tpu_custom_call" | custom-call | flops 1 | bytes 1 | tf_op jit(solution)/shard_map/some_rows/pallas_call | solution.py:321
  36.9 0.0 copy-done
  36.9 0.0 copy-done.4
  36.9 0.0 copy-done.5
  36.9 0.0 copy-done.1
  36.9 0.0 copy-done.6
  36.9 0.0 copy-done.7
  36.9 0.0 copy-done.8
  36.9 0.0 copy-done.9
  36.9 0.0 copy-done.2
  37.0 0.0 copy-done.3
  37.0 0.0 copy-start.10
  37.0 2.0 %collective-permute-done.13.refs_15_ = bf16[128,1024]{1,0:T(8,128)(2,1)S(1)} collective-permute-done((bf16[128,1024]{1,0:T(8,128)(2,1)S(1)}, bf16[128,1024]{1,0:T(8,128)(2,1)S(1)}, u32[]{:S(2)}, u32[]{:S(2)}) %collective-permute-start.13) | collective-permute-done | bytes 262176 | tf_op jit(solution)/shard_map/ppermute | solution.py:247
  39.0 0.0 collective-permute-start.14
  39.0 1.5 %collective-permute-done.14.refs_16_ = bf16[128,1024]{1,0:T(8,128)(2,1)S(1)} collective-permute-done((bf16[128,1024]{1,0:T(8,128)(2,1)S(1)}, bf16[128,1024]{1,0:T(8,128)(2,1)S(1)}, u32[]{:S(2)}, u32[]{:S(2)}) %collective-permute-start.14) | collective-permute-done | bytes 262176 | tf_op jit(solution)/shard_map/ppermute | solution.py:247
  40.6 6.1 %rounds.1 = (f32[64,1024]{1,0:T(8,128)}, bf16[128,256]{1,0:T(8,128)(2,1)S(1)}, bf16[128,256]{1,0:T(8,128)(2,1)S(1)}, bf16[128,256]{1,0:T(8,128)(2,1)S(1)}, bf16[128,256]{1,0:T(8,128)(2,1)S(1)}) custom-call(f32[264,1152]{1,0:T(8,128)S(1)} %some_rows.1.refs_0_, bf16[192,1024]{1,0:T(8,128)(2,1)} %copy-done, bf16[192,1024]{1,0:T(8,128)(2,1)} %copy-done.2, ...), custom_call_target="tpu_custom_call" | custom-call | flops 1 | bytes 1 | tf_op jit(solution)/shard_map/rounds/pallas_call | solution.py:336
  46.6 2.4 %collective-permute-start.15 = (bf16[128,256]{1,0:T(8,128)(2,1)S(1)}, bf16[128,256]{1,0:T(8,128)(2,1)S(1)}, u32[]{:S(2)}, u32[]{:S(2)}) collective-permute-start(bf16[128,256]{1,0:T(8,128)(2,1)S(1)} %get-tuple-element.24), channel_id=1, source_target_pairs={{0,12},{4,8},{8,4},{12,0},{1,13},{5,9},{9,5},{13,1},{2,14},{6,10},... | collective-permute-start | bytes 196616 | tf_op jit(solution)/shard_map/ppermute | solution.py:247
  49.0 2.1 %collective-permute-start.16 = (bf16[128,256]{1,0:T(8,128)(2,1)S(1)}, bf16[128,256]{1,0:T(8,128)(2,1)S(1)}, u32[]{:S(2)}, u32[]{:S(2)}) collective-permute-start(bf16[128,256]{1,0:T(8,128)(2,1)S(1)} %get-tuple-element.25), channel_id=1, source_target_pairs={{0,8},{4,12},{8,0},{12,4},{1,9},{5,13},{9,1},{13,5},{2,10},{6,14},... | collective-permute-start | bytes 196616 | tf_op jit(solution)/shard_map/ppermute | solution.py:247
  51.2 0.0 collective-permute-start.17
  51.2 0.0 copy-done.10
  51.2 0.3 places.1.places_ref
  51.5 1.3 %collective-permute-done.15.refs_0_ = bf16[128,256]{1,0:T(8,128)(2,1)S(1)} collective-permute-done((bf16[128,256]{1,0:T(8,128)(2,1)S(1)}, bf16[128,256]{1,0:T(8,128)(2,1)S(1)}, u32[]{:S(2)}, u32[]{:S(2)}) %collective-permute-start.15) | collective-permute-done | bytes 65568 | tf_op jit(solution)/shard_map/ppermute | solution.py:247
  52.8 4.0 %collective-permute-done.16.refs_1_ = bf16[128,256]{1,0:T(8,128)(2,1)S(1)} collective-permute-done((bf16[128,256]{1,0:T(8,128)(2,1)S(1)}, bf16[128,256]{1,0:T(8,128)(2,1)S(1)}, u32[]{:S(2)}, u32[]{:S(2)}) %collective-permute-start.16) | collective-permute-done | bytes 65568 | tf_op jit(solution)/shard_map/ppermute | solution.py:247
  56.8 0.0 collective-permute-done.17.refs_2_
  56.8 1.0 %unpack.1 = f32[256,256]{1,0:T(8,128)} custom-call(bf16[256,512]{1,0:T(8,128)(2,1)S(1)} %places.1.places_ref, bf16[128,256]{1,0:T(8,128)(2,1)S(1)} %collective-permute-done.15.refs_0_, bf16[128,256]{1,0:T(8,128)(2,1)S(1)} %collective-permute-done.16.refs_1_, bf16[128,256]{1,0:T(8,128)(2,1)S(1)} %collective-permute-done.17.refs_2_, ...), custom_call_target="tpu_custom_call" | custom-call | flops 1 | bytes 1 | tf_op jit(solution)/shard_map/unpack/pallas_call | solution.py:360
Async XLA Ops:
  2.2 34.7 %copy-start = (bf16[192,1024]{1,0:T(8,128)(2,1)}, bf16[192,1024]{1,0:T(8,128)(2,1)S(1)}, u32[]{:S(2)}) copy-start(bf16[192,1024]{1,0:T(8,128)(2,1)S(1)} %get-tuple-element.16.refs_0_.refs_1_) | copy-start | bytes 1179652
  2.2 14.9 %collective-permute-start.3 = (bf16[128,1024]{1,0:T(8,128)(2,1)S(1)}, bf16[128,1024]{1,0:T(8,128)(2,1)S(1)}, u32[]{:S(2)}, u32[]{:S(2)}) collective-permute-start(bf16[128,1024]{1,0:T(8,128)(2,1)S(1)} %get-tuple-element.17), channel_id=1, source_target_pairs={{0,4},{4,0},{8,12},{12,8},{1,5},{5,1},{9,13},{13,9},{2,6},{6,2},{1... | collective-permute-start | bytes 786440 | tf_op jit(solution)/shard_map/ppermute | solution.py:247
  5.3 14.3 %collective-permute-start.7 = (bf16[128,1024]{1,0:T(8,128)(2,1)S(1)}, bf16[128,1024]{1,0:T(8,128)(2,1)S(1)}, u32[]{:S(2)}, u32[]{:S(2)}) collective-permute-start(bf16[128,1024]{1,0:T(8,128)(2,1)S(1)} %get-tuple-element.18), channel_id=1, source_target_pairs={{0,8},{4,12},{8,0},{12,4},{1,9},{5,13},{9,1},{13,5},{2,10},{6,14},... | collective-permute-start | bytes 786440 | tf_op jit(solution)/shard_map/ppermute | solution.py:247
  7.9 15.7 %collective-permute-start = (bf16[192,1024]{1,0:T(8,128)(2,1)S(1)}, bf16[192,1024]{1,0:T(8,128)(2,1)S(1)}, u32[]{:S(2)}, u32[]{:S(2)}) collective-permute-start(bf16[192,1024]{1,0:T(8,128)(2,1)S(1)} %get-tuple-element.16.refs_0_.refs_1_), channel_id=1, source_target_pairs={{0,2},{1,3},{2,0},{3,1},{4,6},{5,7},{6,4},{7,5},{8,10},{9,11},{10,... | collective-permute-start | bytes 1179656 | tf_op jit(solution)/shard_map/ppermute | solution.py:247
  17.1 19.8 %copy-start.4 = (bf16[128,1024]{1,0:T(8,128)(2,1)}, bf16[128,1024]{1,0:T(8,128)(2,1)S(1)}, u32[]{:S(2)}) copy-start(bf16[128,1024]{1,0:T(8,128)(2,1)S(1)} %collective-permute-done.3.refs_4_.refs_5_) | copy-start | bytes 786436
  17.1 7.9 %collective-permute-start.5 = (bf16[128,1024]{1,0:T(8,128)(2,1)S(1)}, bf16[128,1024]{1,0:T(8,128)(2,1)S(1)}, u32[]{:S(2)}, u32[]{:S(2)}) collective-permute-start(bf16[128,1024]{1,0:T(8,128)(2,1)S(1)} %collective-permute-done.3.refs_4_.refs_5_), channel_id=1, source_target_pairs={{0,2},{1,3},{2,0},{3,1},{4,6},{5,7},{6,4},{7,5},{8,10},{9,11},{10,... | collective-permute-start | bytes 786440 | tf_op jit(solution)/shard_map/ppermute | solution.py:247
  18.8 6.3 %collective-permute-start.4 = (bf16[128,1024]{1,0:T(8,128)(2,1)S(1)}, bf16[128,1024]{1,0:T(8,128)(2,1)S(1)}, u32[]{:S(2)}, u32[]{:S(2)}) collective-permute-start(bf16[128,1024]{1,0:T(8,128)(2,1)S(1)} %collective-permute-done.3.refs_4_.refs_5_), channel_id=1, source_target_pairs={{0,1},{1,0},{2,3},{3,2},{4,5},{5,4},{6,7},{7,6},{8,9},{9,8},{10,11... | collective-permute-start | bytes 786440 | tf_op jit(solution)/shard_map/ppermute | solution.py:247
  19.6 17.3 %copy-start.5 = (bf16[128,1024]{1,0:T(8,128)(2,1)}, bf16[128,1024]{1,0:T(8,128)(2,1)S(1)}, u32[]{:S(2)}) copy-start(bf16[128,1024]{1,0:T(8,128)(2,1)S(1)} %collective-permute-done.7.refs_8_.refs_9_) | copy-start | bytes 786436
  19.6 9.8 %collective-permute-start.11 = (bf16[128,1024]{1,0:T(8,128)(2,1)S(1)}, bf16[128,1024]{1,0:T(8,128)(2,1)S(1)}, u32[]{:S(2)}, u32[]{:S(2)}) collective-permute-start(bf16[128,1024]{1,0:T(8,128)(2,1)S(1)} %get-tuple-element.20), channel_id=1, source_target_pairs={{0,12},{4,8},{8,4},{12,0},{1,13},{5,9},{9,5},{13,1},{2,14},{6,10},... | collective-permute-start | bytes 786440 | tf_op jit(solution)/shard_map/ppermute | solution.py:247
  22.1 8.1 %collective-permute-start.9 = (bf16[128,1024]{1,0:T(8,128)(2,1)S(1)}, bf16[128,1024]{1,0:T(8,128)(2,1)S(1)}, u32[]{:S(2)}, u32[]{:S(2)}) collective-permute-start(bf16[128,1024]{1,0:T(8,128)(2,1)S(1)} %collective-permute-done.7.refs_8_.refs_9_), channel_id=1, source_target_pairs={{0,2},{1,3},{2,0},{3,1},{4,6},{5,7},{6,4},{7,5},{8,10},{9,11},{10,... | collective-permute-start | bytes 786440 | tf_op jit(solution)/shard_map/ppermute | solution.py:247
  23.6 13.3 %copy-start.1 = (bf16[192,1024]{1,0:T(8,128)(2,1)}, bf16[192,1024]{1,0:T(8,128)(2,1)S(1)}, u32[]{:S(2)}) copy-start(bf16[192,1024]{1,0:T(8,128)(2,1)S(1)} %collective-permute-done.refs_2_.refs_3_) | copy-start | bytes 1179652
  23.6 6.6 %collective-permute-start.8 = (bf16[128,1024]{1,0:T(8,128)(2,1)S(1)}, bf16[128,1024]{1,0:T(8,128)(2,1)S(1)}, u32[]{:S(2)}, u32[]{:S(2)}) collective-permute-start(bf16[128,1024]{1,0:T(8,128)(2,1)S(1)} %collective-permute-done.7.refs_8_.refs_9_), channel_id=1, source_target_pairs={{0,1},{1,0},{2,3},{3,2},{4,5},{5,4},{6,7},{7,6},{8,9},{9,8},{10,11... | collective-permute-start | bytes 786440 | tf_op jit(solution)/shard_map/ppermute | solution.py:247
  25.0 11.9 %copy-start.6 = (bf16[128,1024]{1,0:T(8,128)(2,1)}, bf16[128,1024]{1,0:T(8,128)(2,1)S(1)}, u32[]{:S(2)}) copy-start(bf16[128,1024]{1,0:T(8,128)(2,1)S(1)} %collective-permute-done.5.refs_6_.refs_7_) | copy-start | bytes 786436
  25.0 5.7 %collective-permute-start.6 = (bf16[128,1024]{1,0:T(8,128)(2,1)S(1)}, bf16[128,1024]{1,0:T(8,128)(2,1)S(1)}, u32[]{:S(2)}, u32[]{:S(2)}) collective-permute-start(bf16[128,1024]{1,0:T(8,128)(2,1)S(1)} %collective-permute-done.5.refs_6_.refs_7_), channel_id=1, source_target_pairs={{0,1},{1,0},{2,3},{3,2},{4,5},{5,4},{6,7},{7,6},{8,9},{9,8},{10,11... | collective-permute-start | bytes 786440 | tf_op jit(solution)/shard_map/ppermute | solution.py:247
  25.0 11.9 %copy-start.7 = (bf16[128,1024]{1,0:T(8,128)(2,1)}, bf16[128,1024]{1,0:T(8,128)(2,1)S(1)}, u32[]{:S(2)}) copy-start(bf16[128,1024]{1,0:T(8,128)(2,1)S(1)} %collective-permute-done.4.refs_5_.refs_6_) | copy-start | bytes 786436
  25.1 7.1 %collective-permute-start.1 = (bf16[192,1024]{1,0:T(8,128)(2,1)S(1)}, bf16[192,1024]{1,0:T(8,128)(2,1)S(1)}, u32[]{:S(2)}, u32[]{:S(2)}) collective-permute-start(bf16[192,1024]{1,0:T(8,128)(2,1)S(1)} %get-tuple-element.16.refs_0_.refs_1_), channel_id=1, source_target_pairs={{0,1},{1,0},{2,3},{3,2},{4,5},{5,4},{6,7},{7,6},{8,9},{9,8},{10,11... | collective-permute-start | bytes 1179656 | tf_op jit(solution)/shard_map/ppermute | solution.py:247
  29.4 2.7 %collective-permute-start.2 = (bf16[192,1024]{1,0:T(8,128)(2,1)S(1)}, bf16[192,1024]{1,0:T(8,128)(2,1)S(1)}, u32[]{:S(2)}, u32[]{:S(2)}) collective-permute-start(bf16[192,1024]{1,0:T(8,128)(2,1)S(1)} %collective-permute-done.refs_2_.refs_3_), channel_id=1, source_target_pairs={{0,1},{1,0},{2,3},{3,2},{4,5},{5,4},{6,7},{7,6},{8,9},{9,8},{10,11... | collective-permute-start | bytes 1179656 | tf_op jit(solution)/shard_map/ppermute | solution.py:247
  30.2 1.9 %collective-permute-start.12 = (bf16[128,1024]{1,0:T(8,128)(2,1)S(1)}, bf16[128,1024]{1,0:T(8,128)(2,1)S(1)}, u32[]{:S(2)}, u32[]{:S(2)}) collective-permute-start(bf16[128,1024]{1,0:T(8,128)(2,1)S(1)} %collective-permute-done.11.refs_12_.refs_13_), channel_id=1, source_target_pairs={{0,1},{1,0},{2,3},{3,2},{4,5},{5,4},{6,7},{7,6},{8,9},{9,8},{10,11... | collective-permute-start | bytes 786440 | tf_op jit(solution)/shard_map/ppermute | solution.py:247
  30.2 6.7 %copy-start.8 = (bf16[128,1024]{1,0:T(8,128)(2,1)}, bf16[128,1024]{1,0:T(8,128)(2,1)S(1)}, u32[]{:S(2)}) copy-start(bf16[128,1024]{1,0:T(8,128)(2,1)S(1)} %collective-permute-done.8.refs_9_.refs_10_) | copy-start | bytes 786436
  30.2 1.9 %collective-permute-start.10 = (bf16[128,1024]{1,0:T(8,128)(2,1)S(1)}, bf16[128,1024]{1,0:T(8,128)(2,1)S(1)}, u32[]{:S(2)}, u32[]{:S(2)}) collective-permute-start(bf16[128,1024]{1,0:T(8,128)(2,1)S(1)} %collective-permute-done.9.refs_10_.refs_11_), channel_id=1, source_target_pairs={{0,1},{1,0},{2,3},{3,2},{4,5},{5,4},{6,7},{7,6},{8,9},{9,8},{10,11... | collective-permute-start | bytes 786440 | tf_op jit(solution)/shard_map/ppermute | solution.py:247
  30.7 6.2 %copy-start.9 = (bf16[128,1024]{1,0:T(8,128)(2,1)}, bf16[128,1024]{1,0:T(8,128)(2,1)S(1)}, u32[]{:S(2)}) copy-start(bf16[128,1024]{1,0:T(8,128)(2,1)S(1)} %collective-permute-done.6.refs_7_.refs_8_) | copy-start | bytes 786436
  30.7 8.3 %collective-permute-start.13 = (bf16[128,1024]{1,0:T(8,128)(2,1)S(1)}, bf16[128,1024]{1,0:T(8,128)(2,1)S(1)}, u32[]{:S(2)}, u32[]{:S(2)}) collective-permute-start(bf16[128,1024]{1,0:T(8,128)(2,1)S(1)} %collective-permute-done.11.refs_12_.refs_13_), channel_id=1, source_target_pairs={{0,2},{1,3},{2,0},{3,1},{4,6},{5,7},{6,4},{7,5},{8,10},{9,11},{10,... | collective-permute-start | bytes 786440 | tf_op jit(solution)/shard_map/ppermute | solution.py:247
  32.1 4.8 %copy-start.2 = (bf16[192,1024]{1,0:T(8,128)(2,1)}, bf16[192,1024]{1,0:T(8,128)(2,1)S(1)}, u32[]{:S(2)}) copy-start(bf16[192,1024]{1,0:T(8,128)(2,1)S(1)} %collective-permute-done.1.refs_1_.refs_2_) | copy-start | bytes 1179652
  32.1 4.8 %copy-start.3 = (bf16[192,1024]{1,0:T(8,128)(2,1)}, bf16[192,1024]{1,0:T(8,128)(2,1)S(1)}, u32[]{:S(2)}) copy-start(bf16[192,1024]{1,0:T(8,128)(2,1)S(1)} %collective-permute-done.2.refs_3_.refs_4_) | copy-start | bytes 1179652
  37.0 14.2 %copy-start.10 = (s32[256]{0:T(256)S(1)}, s32[256]{0:T(256)}, u32[]{:S(2)}) copy-start(s32[256]{0:T(256)} %param.4) | copy-start | bytes 3076
  39.0 1.5 %collective-permute-start.14 = (bf16[128,1024]{1,0:T(8,128)(2,1)S(1)}, bf16[128,1024]{1,0:T(8,128)(2,1)S(1)}, u32[]{:S(2)}, u32[]{:S(2)}) collective-permute-start(bf16[128,1024]{1,0:T(8,128)(2,1)S(1)} %collective-permute-done.13.refs_15_), channel_id=1, source_target_pairs={{0,1},{1,0},{2,3},{3,2},{4,5},{5,4},{6,7},{7,6},{8,9},{9,8},{10,11... | collective-permute-start | bytes 786440 | tf_op jit(solution)/shard_map/ppermute | solution.py:247
  46.6 6.2 %collective-permute-start.15 = (bf16[128,256]{1,0:T(8,128)(2,1)S(1)}, bf16[128,256]{1,0:T(8,128)(2,1)S(1)}, u32[]{:S(2)}, u32[]{:S(2)}) collective-permute-start(bf16[128,256]{1,0:T(8,128)(2,1)S(1)} %get-tuple-element.24), channel_id=1, source_target_pairs={{0,12},{4,8},{8,4},{12,0},{1,13},{5,9},{9,5},{13,1},{2,14},{6,10},... | collective-permute-start | bytes 196616 | tf_op jit(solution)/shard_map/ppermute | solution.py:247
  49.0 7.8 %collective-permute-start.16 = (bf16[128,256]{1,0:T(8,128)(2,1)S(1)}, bf16[128,256]{1,0:T(8,128)(2,1)S(1)}, u32[]{:S(2)}, u32[]{:S(2)}) collective-permute-start(bf16[128,256]{1,0:T(8,128)(2,1)S(1)} %get-tuple-element.25), channel_id=1, source_target_pairs={{0,8},{4,12},{8,0},{12,4},{1,9},{5,13},{9,1},{13,5},{2,10},{6,14},... | collective-permute-start | bytes 196616 | tf_op jit(solution)/shard_map/ppermute | solution.py:247
  51.2 5.7 %collective-permute-start.17 = (bf16[128,256]{1,0:T(8,128)(2,1)S(1)}, bf16[128,256]{1,0:T(8,128)(2,1)S(1)}, u32[]{:S(2)}, u32[]{:S(2)}) collective-permute-start(bf16[128,256]{1,0:T(8,128)(2,1)S(1)} %get-tuple-element.26), channel_id=1, source_target_pairs={{0,4},{4,0},{8,12},{12,8},{1,5},{5,1},{9,13},{13,9},{2,6},{6,2},{1... | collective-permute-start | bytes 196616 | tf_op jit(solution)/shard_map/ppermute | solution.py:247

commit v8 on v7

--- a/solution.py
+++ b/solution.py
@@ -96,11 +96,15 @@
     out[...] = jnp.where(lanes == column, 1.0, 0.0).astype(BF)
 
 
+def leaving(groups):
+    return [groups - 1, *range(1, groups - 1), 0]
+
+
 def unpack_kernel(places_ref, *refs):
     *logs, out = refs
     height = logs[0].shape[0]
     total = None
-    for g, block in enumerate(logs[::-1]):
+    for g, block in zip(leaving(len(logs)), logs):
         term = matmul(places_ref[:, g * height : (g + 1) * height], block[...], NN)
         total = term if total is None else total + term
     out[...] = total
@@ -345,7 +349,7 @@
         name="rounds",
     )(sofar, *[in_hbm(r) for r in earlier[: 3 * helpers - 2]], *earlier[3 * helpers - 2 :], *late)
 
-    back = [across(logs[g], g) for g in reversed(range(groups))]
+    back = [across(logs[g], g) for g in leaving(groups)]
     places = jax.ShapeDtypeStruct((count, groups * height), BF)
     out = jax.ShapeDtypeStruct((count, subs), F32)
     where = pl.pallas_call(

time: 58 us -> 58 us (level)
  transfers between devices with their start and end apart: 18 -> 18, of which waited for: 9 -> 10; matrix products, arithmetic and copies ran while one was open for 0% -> 0% of each run, Pallas kernels for 9% -> 9%
where the time goes in v8:
time: 58 us; the launch traced here: 57.8 us
  waiting for transfers between devices  23.6 us (41%)
  starting transfers between devices  19.7 us (34%)
  Pallas kernels  13.7 us (24%)
  between operations  0.8 us (1%)
    ppermute x18, waiting for transfers between devices, hop(): return lambda x: lax.ppermute(x, axis, pairs)  23.6 us
    ppermute x18, starting transfers between devices, hop(): return lambda x: lax.ppermute(x, axis, pairs)  19.7 us
    pallas_call x1, Pallas kernels, per_device(): pl.pallas_call(functools.partial(last_kernel, helpers, (len(earlier), len...  6.05 us
    pallas_call x1, Pallas kernels, per_device(): pl.pallas_call(functools.partial(some_kernel, helpers, height), out_shape...  4.72 us
    pallas_call x1, Pallas kernels, per_device(): pl.pallas_call(functools.partial(pack_kernel, depth, owners), out_shape=b...  1.56 us
  transfers between devices with their start and end apart: 18, of which 10 were waited for; matrix products, arithmetic and copies ran while one was open for 0% of the time, Pallas kernels for 9%

profile of v8, /device:TPU:0, one launch (start us, length us, event | category | flops | bytes accessed | tf_op | source)
XLA Modules:
  0.0 57.8 jit_solution(16769539283282552750)
XLA Ops:
  0.6 1.6 %pack.1 = (bf16[192,1024]{1,0:T(8,128)(2,1)S(1)}, bf16[128,1024]{1,0:T(8,128)(2,1)S(1)}, bf16[128,1024]{1,0:T(8,128)(2,1)S(1)}, bf16[128,1024]{1,0:T(8,128)(2,1)S(1)}) custom-call(s32[1,256]{1,0:T(1,128)} %bitcast.3, bf16[256,1024]{1,0:T(8,128)(2,1)} %points_hbm.1, bf16[64,1024]{1,0:T(8,128)(2,1)} %bitcast.5), custom_call_target="tpu_custom_call" | custom-call | flops 1 | bytes 1 | tf_op jit(solution)/shard_map/pack/pallas_call | solution.py:268
  2.2 0.0 copy-start
  2.2 3.1 %collective-permute-start.3 = (bf16[128,1024]{1,0:T(8,128)(2,1)S(1)}, bf16[128,1024]{1,0:T(8,128)(2,1)S(1)}, u32[]{:S(2)}, u32[]{:S(2)}) collective-permute-start(bf16[128,1024]{1,0:T(8,128)(2,1)S(1)} %get-tuple-element.17), channel_id=1, source_target_pairs={{0,4},{4,0},{8,12},{12,8},{1,5},{5,1},{9,13},{13,9},{2,6},{6,2},{1... | collective-permute-start | bytes 786440 | tf_op jit(solution)/shard_map/ppermute | solution.py:251
  5.3 2.6 %collective-permute-start.7 = (bf16[128,1024]{1,0:T(8,128)(2,1)S(1)}, bf16[128,1024]{1,0:T(8,128)(2,1)S(1)}, u32[]{:S(2)}, u32[]{:S(2)}) collective-permute-start(bf16[128,1024]{1,0:T(8,128)(2,1)S(1)} %get-tuple-element.18), channel_id=1, source_target_pairs={{0,8},{4,12},{8,0},{12,4},{1,9},{5,13},{9,1},{13,5},{2,10},{6,14},... | collective-permute-start | bytes 786440 | tf_op jit(solution)/shard_map/ppermute | solution.py:251
  7.9 1.5 %collective-permute-start = (bf16[192,1024]{1,0:T(8,128)(2,1)S(1)}, bf16[192,1024]{1,0:T(8,128)(2,1)S(1)}, u32[]{:S(2)}, u32[]{:S(2)}) collective-permute-start(bf16[192,1024]{1,0:T(8,128)(2,1)S(1)} %get-tuple-element.16.refs_0_.refs_1_), channel_id=1, source_target_pairs={{0,2},{1,3},{2,0},{3,1},{4,6},{5,7},{6,4},{7,5},{8,10},{9,11},{10,... | collective-permute-start | bytes 1179656 | tf_op jit(solution)/shard_map/ppermute | solution.py:251
  9.4 7.7 %collective-permute-done.3.refs_4_.refs_5_ = bf16[128,1024]{1,0:T(8,128)(2,1)S(1)} collective-permute-done((bf16[128,1024]{1,0:T(8,128)(2,1)S(1)}, bf16[128,1024]{1,0:T(8,128)(2,1)S(1)}, u32[]{:S(2)}, u32[]{:S(2)}) %collective-permute-start.3) | collective-permute-done | bytes 262176 | tf_op jit(solution)/shard_map/ppermute | solution.py:251
  17.1 0.0 copy-start.4
  17.1 1.7 %collective-permute-start.5 = (bf16[128,1024]{1,0:T(8,128)(2,1)S(1)}, bf16[128,1024]{1,0:T(8,128)(2,1)S(1)}, u32[]{:S(2)}, u32[]{:S(2)}) collective-permute-start(bf16[128,1024]{1,0:T(8,128)(2,1)S(1)} %collective-permute-done.3.refs_4_.refs_5_), channel_id=1, source_target_pairs={{0,2},{1,3},{2,0},{3,1},{4,6},{5,7},{6,4},{7,5},{8,10},{9,11},{10,... | collective-permute-start | bytes 786440 | tf_op jit(solution)/shard_map/ppermute | solution.py:251
  18.8 0.0 collective-permute-start.4
  18.8 0.9 %collective-permute-done.7.refs_8_.refs_9_ = bf16[128,1024]{1,0:T(8,128)(2,1)S(1)} collective-permute-done((bf16[128,1024]{1,0:T(8,128)(2,1)S(1)}, bf16[128,1024]{1,0:T(8,128)(2,1)S(1)}, u32[]{:S(2)}, u32[]{:S(2)}) %collective-permute-start.7) | collective-permute-done | bytes 262176 | tf_op jit(solution)/shard_map/ppermute | solution.py:251
  19.6 0.0 copy-start.5
  19.6 2.5 %collective-permute-start.11 = (bf16[128,1024]{1,0:T(8,128)(2,1)S(1)}, bf16[128,1024]{1,0:T(8,128)(2,1)S(1)}, u32[]{:S(2)}, u32[]{:S(2)}) collective-permute-start(bf16[128,1024]{1,0:T(8,128)(2,1)S(1)} %get-tuple-element.20), channel_id=1, source_target_pairs={{0,12},{4,8},{8,4},{12,0},{1,13},{5,9},{9,5},{13,1},{2,14},{6,10},... | collective-permute-start | bytes 786440 | tf_op jit(solution)/shard_map/ppermute | solution.py:251
  22.1 1.5 %collective-permute-start.9 = (bf16[128,1024]{1,0:T(8,128)(2,1)S(1)}, bf16[128,1024]{1,0:T(8,128)(2,1)S(1)}, u32[]{:S(2)}, u32[]{:S(2)}) collective-permute-start(bf16[128,1024]{1,0:T(8,128)(2,1)S(1)} %collective-permute-done.7.refs_8_.refs_9_), channel_id=1, source_target_pairs={{0,2},{1,3},{2,0},{3,1},{4,6},{5,7},{6,4},{7,5},{8,10},{9,11},{10,... | collective-permute-start | bytes 786440 | tf_op jit(solution)/shard_map/ppermute | solution.py:251
  23.6 0.0 collective-permute-done.refs_2_.refs_3_
  23.6 0.0 copy-start.1
  23.6 0.0 collective-permute-start.8
  23.6 1.4 %collective-permute-done.5.refs_6_.refs_7_ = bf16[128,1024]{1,0:T(8,128)(2,1)S(1)} collective-permute-done((bf16[128,1024]{1,0:T(8,128)(2,1)S(1)}, bf16[128,1024]{1,0:T(8,128)(2,1)S(1)}, u32[]{:S(2)}, u32[]{:S(2)}) %collective-permute-start.5) | collective-permute-done | bytes 262176 | tf_op jit(solution)/shard_map/ppermute | solution.py:251
  25.0 0.0 copy-start.6
  25.0 0.0 collective-permute-start.6
  25.0 0.0 collective-permute-done.4.refs_5_.refs_6_
  25.0 0.0 copy-start.7
  25.1 0.5 collective-permute-start.1
  25.6 3.8 %collective-permute-done.11.refs_12_.refs_13_ = bf16[128,1024]{1,0:T(8,128)(2,1)S(1)} collective-permute-done((bf16[128,1024]{1,0:T(8,128)(2,1)S(1)}, bf16[128,1024]{1,0:T(8,128)(2,1)S(1)}, u32[]{:S(2)}, u32[]{:S(2)}) %collective-permute-start.11) | collective-permute-done | bytes 262176 | tf_op jit(solution)/shard_map/ppermute | solution.py:251
  29.4 0.0 collective-permute-start.2
  29.4 0.8 %collective-permute-done.9.refs_10_.refs_11_ = bf16[128,1024]{1,0:T(8,128)(2,1)S(1)} collective-permute-done((bf16[128,1024]{1,0:T(8,128)(2,1)S(1)}, bf16[128,1024]{1,0:T(8,128)(2,1)S(1)}, u32[]{:S(2)}, u32[]{:S(2)}) %collective-permute-start.9) | collective-permute-done | bytes 262176 | tf_op jit(solution)/shard_map/ppermute | solution.py:251
  30.2 0.0 collective-permute-start.12
  30.2 0.0 collective-permute-done.8.refs_9_.refs_10_
  30.2 0.0 copy-start.8
  30.2 0.5 collective-permute-start.10
  30.7 0.0 collective-permute-done.6.refs_7_.refs_8_
  30.7 0.0 copy-start.9
  30.7 1.3 %collective-permute-start.13 = (bf16[128,1024]{1,0:T(8,128)(2,1)S(1)}, bf16[128,1024]{1,0:T(8,128)(2,1)S(1)}, u32[]{:S(2)}, u32[]{:S(2)}) collective-permute-start(bf16[128,1024]{1,0:T(8,128)(2,1)S(1)} %collective-permute-done.11.refs_12_.refs_13_), channel_id=1, source_target_pairs={{0,2},{1,3},{2,0},{3,1},{4,6},{5,7},{6,4},{7,5},{8,10},{9,11},{10,... | collective-permute-start | bytes 786440 | tf_op jit(solution)/shard_map/ppermute | solution.py:251
  32.1 0.0 collective-permute-done.12.refs_13_.refs_14_
  32.1 0.0 collective-permute-done.10.refs_11_.refs_12_
  32.1 0.0 collective-permute-done.1.refs_1_.refs_2_
  32.1 0.0 copy-start.2
  32.1 0.0 collective-permute-done.2.refs_3_.refs_4_
  32.1 0.0 copy-start.3
  32.1 4.7 %some_rows.1.refs_0_ = f32[264,1152]{1,0:T(8,128)S(1)} custom-call(bf16[192,1024]{1,0:T(8,128)(2,1)S(1)} %get-tuple-element.16.refs_0_.refs_1_, bf16[192,1024]{1,0:T(8,128)(2,1)S(1)} %collective-permute-done.1.refs_1_.refs_2_, bf16[192,1024]{1,0:T(8,128)(2,1)S(1)} %collective-permute-done.refs_2_.refs_3_, ...), custom_call_target="tpu_custom_call" | custom-call | flops 1 | bytes 1 | tf_op jit(solution)/shard_map/some_rows/pallas_call | solution.py:325
  36.9 0.0 copy-done
  36.9 0.0 copy-done.4
  36.9 0.0 copy-done.5
  36.9 0.0 copy-done.1
  36.9 0.0 copy-done.6
  36.9 0.0 copy-done.7
  36.9 0.0 copy-done.8
  36.9 0.0 copy-done.9
  36.9 0.0 copy-done.2
  37.0 0.0 copy-done.3
  37.0 0.0 copy-start.10
  37.0 2.0 %collective-permute-done.13.refs_15_ = bf16[128,1024]{1,0:T(8,128)(2,1)S(1)} collective-permute-done((bf16[128,1024]{1,0:T(8,128)(2,1)S(1)}, bf16[128,1024]{1,0:T(8,128)(2,1)S(1)}, u32[]{:S(2)}, u32[]{:S(2)}) %collective-permute-start.13) | collective-permute-done | bytes 262176 | tf_op jit(solution)/shard_map/ppermute | solution.py:251
  39.0 0.0 collective-permute-start.14
  39.0 1.5 %collective-permute-done.14.refs_16_ = bf16[128,1024]{1,0:T(8,128)(2,1)S(1)} collective-permute-done((bf16[128,1024]{1,0:T(8,128)(2,1)S(1)}, bf16[128,1024]{1,0:T(8,128)(2,1)S(1)}, u32[]{:S(2)}, u32[]{:S(2)}) %collective-permute-start.14) | collective-permute-done | bytes 262176 | tf_op jit(solution)/shard_map/ppermute | solution.py:251
  40.6 6.1 %rounds.1 = (f32[64,1024]{1,0:T(8,128)}, bf16[128,256]{1,0:T(8,128)(2,1)S(1)}, bf16[128,256]{1,0:T(8,128)(2,1)S(1)}, bf16[128,256]{1,0:T(8,128)(2,1)S(1)}, bf16[128,256]{1,0:T(8,128)(2,1)S(1)}) custom-call(f32[264,1152]{1,0:T(8,128)S(1)} %some_rows.1.refs_0_, bf16[192,1024]{1,0:T(8,128)(2,1)} %copy-done, bf16[192,1024]{1,0:T(8,128)(2,1)} %copy-done.2, ...), custom_call_target="tpu_custom_call" | custom-call | flops 1 | bytes 1 | tf_op jit(solution)/shard_map/rounds/pallas_call | solution.py:340
  46.6 2.4 %collective-permute-start.15 = (bf16[128,256]{1,0:T(8,128)(2,1)S(1)}, bf16[128,256]{1,0:T(8,128)(2,1)S(1)}, u32[]{:S(2)}, u32[]{:S(2)}) collective-permute-start(bf16[128,256]{1,0:T(8,128)(2,1)S(1)} %get-tuple-element.24), channel_id=1, source_target_pairs={{0,12},{4,8},{8,4},{12,0},{1,13},{5,9},{9,5},{13,1},{2,14},{6,10},... | collective-permute-start | bytes 196616 | tf_op jit(solution)/shard_map/ppermute | solution.py:251
  49.0 2.1 %collective-permute-start.16 = (bf16[128,256]{1,0:T(8,128)(2,1)S(1)}, bf16[128,256]{1,0:T(8,128)(2,1)S(1)}, u32[]{:S(2)}, u32[]{:S(2)}) collective-permute-start(bf16[128,256]{1,0:T(8,128)(2,1)S(1)} %get-tuple-element.25), channel_id=1, source_target_pairs={{0,4},{4,0},{8,12},{12,8},{1,5},{5,1},{9,13},{13,9},{2,6},{6,2},{1... | collective-permute-start | bytes 196616 | tf_op jit(solution)/shard_map/ppermute | solution.py:251
  51.2 0.0 collective-permute-start.17
  51.2 0.0 copy-done.10
  51.2 0.3 places.1.places_ref
  51.5 1.3 %collective-permute-done.15.refs_0_ = bf16[128,256]{1,0:T(8,128)(2,1)S(1)} collective-permute-done((bf16[128,256]{1,0:T(8,128)(2,1)S(1)}, bf16[128,256]{1,0:T(8,128)(2,1)S(1)}, u32[]{:S(2)}, u32[]{:S(2)}) %collective-permute-start.15) | collective-permute-done | bytes 65568 | tf_op jit(solution)/shard_map/ppermute | solution.py:251
  52.8 1.2 %collective-permute-done.16.refs_1_ = bf16[128,256]{1,0:T(8,128)(2,1)S(1)} collective-permute-done((bf16[128,256]{1,0:T(8,128)(2,1)S(1)}, bf16[128,256]{1,0:T(8,128)(2,1)S(1)}, u32[]{:S(2)}, u32[]{:S(2)}) %collective-permute-start.16) | collective-permute-done | bytes 65568 | tf_op jit(solution)/shard_map/ppermute | solution.py:251
  54.0 2.8 %collective-permute-done.17.refs_2_ = bf16[128,256]{1,0:T(8,128)(2,1)S(1)} collective-permute-done((bf16[128,256]{1,0:T(8,128)(2,1)S(1)}, bf16[128,256]{1,0:T(8,128)(2,1)S(1)}, u32[]{:S(2)}, u32[]{:S(2)}) %collective-permute-start.17) | collective-permute-done | bytes 65568 | tf_op jit(solution)/shard_map/ppermute | solution.py:251
  56.8 1.0 %unpack.1 = f32[256,256]{1,0:T(8,128)} custom-call(bf16[256,512]{1,0:T(8,128)(2,1)S(1)} %places.1.places_ref, bf16[128,256]{1,0:T(8,128)(2,1)S(1)} %collective-permute-done.15.refs_0_, bf16[128,256]{1,0:T(8,128)(2,1)S(1)} %collective-permute-done.16.refs_1_, bf16[128,256]{1,0:T(8,128)(2,1)S(1)} %collective-permute-done.17.refs_2_, ...), custom_call_target="tpu_custom_call" | custom-call | flops 1 | bytes 1 | tf_op jit(solution)/shard_map/unpack/pallas_call | solution.py:364
Async XLA Ops:
  2.2 34.7 %copy-start = (bf16[192,1024]{1,0:T(8,128)(2,1)}, bf16[192,1024]{1,0:T(8,128)(2,1)S(1)}, u32[]{:S(2)}) copy-start(bf16[192,1024]{1,0:T(8,128)(2,1)S(1)} %get-tuple-element.16.refs_0_.refs_1_) | copy-start | bytes 1179652
  2.2 14.9 %collective-permute-start.3 = (bf16[128,1024]{1,0:T(8,128)(2,1)S(1)}, bf16[128,1024]{1,0:T(8,128)(2,1)S(1)}, u32[]{:S(2)}, u32[]{:S(2)}) collective-permute-start(bf16[128,1024]{1,0:T(8,128)(2,1)S(1)} %get-tuple-element.17), channel_id=1, source_target_pairs={{0,4},{4,0},{8,12},{12,8},{1,5},{5,1},{9,13},{13,9},{2,6},{6,2},{1... | collective-permute-start | bytes 786440 | tf_op jit(solution)/shard_map/ppermute | solution.py:251
  5.3 14.3 %collective-permute-start.7 = (bf16[128,1024]{1,0:T(8,128)(2,1)S(1)}, bf16[128,1024]{1,0:T(8,128)(2,1)S(1)}, u32[]{:S(2)}, u32[]{:S(2)}) collective-permute-start(bf16[128,1024]{1,0:T(8,128)(2,1)S(1)} %get-tuple-element.18), channel_id=1, source_target_pairs={{0,8},{4,12},{8,0},{12,4},{1,9},{5,13},{9,1},{13,5},{2,10},{6,14},... | collective-permute-start | bytes 786440 | tf_op jit(solution)/shard_map/ppermute | solution.py:251
  7.9 15.7 %collective-permute-start = (bf16[192,1024]{1,0:T(8,128)(2,1)S(1)}, bf16[192,1024]{1,0:T(8,128)(2,1)S(1)}, u32[]{:S(2)}, u32[]{:S(2)}) collective-permute-start(bf16[192,1024]{1,0:T(8,128)(2,1)S(1)} %get-tuple-element.16.refs_0_.refs_1_), channel_id=1, source_target_pairs={{0,2},{1,3},{2,0},{3,1},{4,6},{5,7},{6,4},{7,5},{8,10},{9,11},{10,... | collective-permute-start | bytes 1179656 | tf_op jit(solution)/shard_map/ppermute | solution.py:251
  17.1 19.8 %copy-start.4 = (bf16[128,1024]{1,0:T(8,128)(2,1)}, bf16[128,1024]{1,0:T(8,128)(2,1)S(1)}, u32[]{:S(2)}) copy-start(bf16[128,1024]{1,0:T(8,128)(2,1)S(1)} %collective-permute-done.3.refs_4_.refs_5_) | copy-start | bytes 786436
  17.1 7.9 %collective-permute-start.5 = (bf16[128,1024]{1,0:T(8,128)(2,1)S(1)}, bf16[128,1024]{1,0:T(8,128)(2,1)S(1)}, u32[]{:S(2)}, u32[]{:S(2)}) collective-permute-start(bf16[128,1024]{1,0:T(8,128)(2,1)S(1)} %collective-permute-done.3.refs_4_.refs_5_), channel_id=1, source_target_pairs={{0,2},{1,3},{2,0},{3,1},{4,6},{5,7},{6,4},{7,5},{8,10},{9,11},{10,... | collective-permute-start | bytes 786440 | tf_op jit(solution)/shard_map/ppermute | solution.py:251
  18.8 6.3 %collective-permute-start.4 = (bf16[128,1024]{1,0:T(8,128)(2,1)S(1)}, bf16[128,1024]{1,0:T(8,128)(2,1)S(1)}, u32[]{:S(2)}, u32[]{:S(2)}) collective-permute-start(bf16[128,1024]{1,0:T(8,128)(2,1)S(1)} %collective-permute-done.3.refs_4_.refs_5_), channel_id=1, source_target_pairs={{0,1},{1,0},{2,3},{3,2},{4,5},{5,4},{6,7},{7,6},{8,9},{9,8},{10,11... | collective-permute-start | bytes 786440 | tf_op jit(solution)/shard_map/ppermute | solution.py:251
  19.6 17.3 %copy-start.5 = (bf16[128,1024]{1,0:T(8,128)(2,1)}, bf16[128,1024]{1,0:T(8,128)(2,1)S(1)}, u32[]{:S(2)}) copy-start(bf16[128,1024]{1,0:T(8,128)(2,1)S(1)} %collective-permute-done.7.refs_8_.refs_9_) | copy-start | bytes 786436
  19.6 9.8 %collective-permute-start.11 = (bf16[128,1024]{1,0:T(8,128)(2,1)S(1)}, bf16[128,1024]{1,0:T(8,128)(2,1)S(1)}, u32[]{:S(2)}, u32[]{:S(2)}) collective-permute-start(bf16[128,1024]{1,0:T(8,128)(2,1)S(1)} %get-tuple-element.20), channel_id=1, source_target_pairs={{0,12},{4,8},{8,4},{12,0},{1,13},{5,9},{9,5},{13,1},{2,14},{6,10},... | collective-permute-start | bytes 786440 | tf_op jit(solution)/shard_map/ppermute | solution.py:251
  22.1 8.1 %collective-permute-start.9 = (bf16[128,1024]{1,0:T(8,128)(2,1)S(1)}, bf16[128,1024]{1,0:T(8,128)(2,1)S(1)}, u32[]{:S(2)}, u32[]{:S(2)}) collective-permute-start(bf16[128,1024]{1,0:T(8,128)(2,1)S(1)} %collective-permute-done.7.refs_8_.refs_9_), channel_id=1, source_target_pairs={{0,2},{1,3},{2,0},{3,1},{4,6},{5,7},{6,4},{7,5},{8,10},{9,11},{10,... | collective-permute-start | bytes 786440 | tf_op jit(solution)/shard_map/ppermute | solution.py:251
  23.6 13.3 %copy-start.1 = (bf16[192,1024]{1,0:T(8,128)(2,1)}, bf16[192,1024]{1,0:T(8,128)(2,1)S(1)}, u32[]{:S(2)}) copy-start(bf16[192,1024]{1,0:T(8,128)(2,1)S(1)} %collective-permute-done.refs_2_.refs_3_) | copy-start | bytes 1179652
  23.6 6.6 %collective-permute-start.8 = (bf16[128,1024]{1,0:T(8,128)(2,1)S(1)}, bf16[128,1024]{1,0:T(8,128)(2,1)S(1)}, u32[]{:S(2)}, u32[]{:S(2)}) collective-permute-start(bf16[128,1024]{1,0:T(8,128)(2,1)S(1)} %collective-permute-done.7.refs_8_.refs_9_), channel_id=1, source_target_pairs={{0,1},{1,0},{2,3},{3,2},{4,5},{5,4},{6,7},{7,6},{8,9},{9,8},{10,11... | collective-permute-start | bytes 786440 | tf_op jit(solution)/shard_map/ppermute | solution.py:251
  25.0 11.9 %copy-start.6 = (bf16[128,1024]{1,0:T(8,128)(2,1)}, bf16[128,1024]{1,0:T(8,128)(2,1)S(1)}, u32[]{:S(2)}) copy-start(bf16[128,1024]{1,0:T(8,128)(2,1)S(1)} %collective-permute-done.5.refs_6_.refs_7_) | copy-start | bytes 786436
  25.0 5.7 %collective-permute-start.6 = (bf16[128,1024]{1,0:T(8,128)(2,1)S(1)}, bf16[128,1024]{1,0:T(8,128)(2,1)S(1)}, u32[]{:S(2)}, u32[]{:S(2)}) collective-permute-start(bf16[128,1024]{1,0:T(8,128)(2,1)S(1)} %collective-permute-done.5.refs_6_.refs_7_), channel_id=1, source_target_pairs={{0,1},{1,0},{2,3},{3,2},{4,5},{5,4},{6,7},{7,6},{8,9},{9,8},{10,11... | collective-permute-start | bytes 786440 | tf_op jit(solution)/shard_map/ppermute | solution.py:251
  25.0 11.9 %copy-start.7 = (bf16[128,1024]{1,0:T(8,128)(2,1)}, bf16[128,1024]{1,0:T(8,128)(2,1)S(1)}, u32[]{:S(2)}) copy-start(bf16[128,1024]{1,0:T(8,128)(2,1)S(1)} %collective-permute-done.4.refs_5_.refs_6_) | copy-start | bytes 786436
  25.1 7.1 %collective-permute-start.1 = (bf16[192,1024]{1,0:T(8,128)(2,1)S(1)}, bf16[192,1024]{1,0:T(8,128)(2,1)S(1)}, u32[]{:S(2)}, u32[]{:S(2)}) collective-permute-start(bf16[192,1024]{1,0:T(8,128)(2,1)S(1)} %get-tuple-element.16.refs_0_.refs_1_), channel_id=1, source_target_pairs={{0,1},{1,0},{2,3},{3,2},{4,5},{5,4},{6,7},{7,6},{8,9},{9,8},{10,11... | collective-permute-start | bytes 1179656 | tf_op jit(solution)/shard_map/ppermute | solution.py:251
  29.4 2.7 %collective-permute-start.2 = (bf16[192,1024]{1,0:T(8,128)(2,1)S(1)}, bf16[192,1024]{1,0:T(8,128)(2,1)S(1)}, u32[]{:S(2)}, u32[]{:S(2)}) collective-permute-start(bf16[192,1024]{1,0:T(8,128)(2,1)S(1)} %collective-permute-done.refs_2_.refs_3_), channel_id=1, source_target_pairs={{0,1},{1,0},{2,3},{3,2},{4,5},{5,4},{6,7},{7,6},{8,9},{9,8},{10,11... | collective-permute-start | bytes 1179656 | tf_op jit(solution)/shard_map/ppermute | solution.py:251
  30.2 1.9 %collective-permute-start.12 = (bf16[128,1024]{1,0:T(8,128)(2,1)S(1)}, bf16[128,1024]{1,0:T(8,128)(2,1)S(1)}, u32[]{:S(2)}, u32[]{:S(2)}) collective-permute-start(bf16[128,1024]{1,0:T(8,128)(2,1)S(1)} %collective-permute-done.11.refs_12_.refs_13_), channel_id=1, source_target_pairs={{0,1},{1,0},{2,3},{3,2},{4,5},{5,4},{6,7},{7,6},{8,9},{9,8},{10,11... | collective-permute-start | bytes 786440 | tf_op jit(solution)/shard_map/ppermute | solution.py:251
  30.2 6.7 %copy-start.8 = (bf16[128,1024]{1,0:T(8,128)(2,1)}, bf16[128,1024]{1,0:T(8,128)(2,1)S(1)}, u32[]{:S(2)}) copy-start(bf16[128,1024]{1,0:T(8,128)(2,1)S(1)} %collective-permute-done.8.refs_9_.refs_10_) | copy-start | bytes 786436
  30.2 1.9 %collective-permute-start.10 = (bf16[128,1024]{1,0:T(8,128)(2,1)S(1)}, bf16[128,1024]{1,0:T(8,128)(2,1)S(1)}, u32[]{:S(2)}, u32[]{:S(2)}) collective-permute-start(bf16[128,1024]{1,0:T(8,128)(2,1)S(1)} %collective-permute-done.9.refs_10_.refs_11_), channel_id=1, source_target_pairs={{0,1},{1,0},{2,3},{3,2},{4,5},{5,4},{6,7},{7,6},{8,9},{9,8},{10,11... | collective-permute-start | bytes 786440 | tf_op jit(solution)/shard_map/ppermute | solution.py:251
  30.7 6.2 %copy-start.9 = (bf16[128,1024]{1,0:T(8,128)(2,1)}, bf16[128,1024]{1,0:T(8,128)(2,1)S(1)}, u32[]{:S(2)}) copy-start(bf16[128,1024]{1,0:T(8,128)(2,1)S(1)} %collective-permute-done.6.refs_7_.refs_8_) | copy-start | bytes 786436
  30.7 8.3 %collective-permute-start.13 = (bf16[128,1024]{1,0:T(8,128)(2,1)S(1)}, bf16[128,1024]{1,0:T(8,128)(2,1)S(1)}, u32[]{:S(2)}, u32[]{:S(2)}) collective-permute-start(bf16[128,1024]{1,0:T(8,128)(2,1)S(1)} %collective-permute-done.11.refs_12_.refs_13_), channel_id=1, source_target_pairs={{0,2},{1,3},{2,0},{3,1},{4,6},{5,7},{6,4},{7,5},{8,10},{9,11},{10,... | collective-permute-start | bytes 786440 | tf_op jit(solution)/shard_map/ppermute | solution.py:251
  32.1 4.8 %copy-start.2 = (bf16[192,1024]{1,0:T(8,128)(2,1)}, bf16[192,1024]{1,0:T(8,128)(2,1)S(1)}, u32[]{:S(2)}) copy-start(bf16[192,1024]{1,0:T(8,128)(2,1)S(1)} %collective-permute-done.1.refs_1_.refs_2_) | copy-start | bytes 1179652
  32.1 4.8 %copy-start.3 = (bf16[192,1024]{1,0:T(8,128)(2,1)}, bf16[192,1024]{1,0:T(8,128)(2,1)S(1)}, u32[]{:S(2)}) copy-start(bf16[192,1024]{1,0:T(8,128)(2,1)S(1)} %collective-permute-done.2.refs_3_.refs_4_) | copy-start | bytes 1179652
  37.0 14.2 %copy-start.10 = (s32[256]{0:T(256)S(1)}, s32[256]{0:T(256)}, u32[]{:S(2)}) copy-start(s32[256]{0:T(256)} %param.4) | copy-start | bytes 3076
  39.0 1.5 %collective-permute-start.14 = (bf16[128,1024]{1,0:T(8,128)(2,1)S(1)}, bf16[128,1024]{1,0:T(8,128)(2,1)S(1)}, u32[]{:S(2)}, u32[]{:S(2)}) collective-permute-start(bf16[128,1024]{1,0:T(8,128)(2,1)S(1)} %collective-permute-done.13.refs_15_), channel_id=1, source_target_pairs={{0,1},{1,0},{2,3},{3,2},{4,5},{5,4},{6,7},{7,6},{8,9},{9,8},{10,11... | collective-permute-start | bytes 786440 | tf_op jit(solution)/shard_map/ppermute | solution.py:251
  46.6 6.2 %collective-permute-start.15 = (bf16[128,256]{1,0:T(8,128)(2,1)S(1)}, bf16[128,256]{1,0:T(8,128)(2,1)S(1)}, u32[]{:S(2)}, u32[]{:S(2)}) collective-permute-start(bf16[128,256]{1,0:T(8,128)(2,1)S(1)} %get-tuple-element.24), channel_id=1, source_target_pairs={{0,12},{4,8},{8,4},{12,0},{1,13},{5,9},{9,5},{13,1},{2,14},{6,10},... | collective-permute-start | bytes 196616 | tf_op jit(solution)/shard_map/ppermute | solution.py:251
  49.0 5.0 %collective-permute-start.16 = (bf16[128,256]{1,0:T(8,128)(2,1)S(1)}, bf16[128,256]{1,0:T(8,128)(2,1)S(1)}, u32[]{:S(2)}, u32[]{:S(2)}) collective-permute-start(bf16[128,256]{1,0:T(8,128)(2,1)S(1)} %get-tuple-element.25), channel_id=1, source_target_pairs={{0,4},{4,0},{8,12},{12,8},{1,5},{5,1},{9,13},{13,9},{2,6},{6,2},{1... | collective-permute-start | bytes 196616 | tf_op jit(solution)/shard_map/ppermute | solution.py:251
  51.2 5.7 %collective-permute-start.17 = (bf16[128,256]{1,0:T(8,128)(2,1)S(1)}, bf16[128,256]{1,0:T(8,128)(2,1)S(1)}, u32[]{:S(2)}, u32[]{:S(2)}) collective-permute-start(bf16[128,256]{1,0:T(8,128)(2,1)S(1)} %get-tuple-element.26), channel_id=1, source_target_pairs={{0,8},{4,12},{8,0},{12,4},{1,9},{5,13},{9,1},{13,5},{2,10},{6,14},... | collective-permute-start | bytes 196616 | tf_op jit(solution)/shard_map/ppermute | solution.py:251
